TPU v7x, 512 devices: a whole 4x4x16 slice. The times are simulated.
512 devices in a mesh: member: 16 (over y, x_lo, core), node: 32 (over z, x_hi).
Axes of the slice: x: 4 (x_hi: 2, x_lo: 2; x = x_hi * 2 + x_lo), y: 4, z: 16, core: 2. Of those that a mesh axis runs over, the one named last changes fastest.
Arguments:
- latent: bfloat16 [8192, 1024], P('node', 'member'), may hold values from -6 to 6
- member_perturbations: bfloat16 [16, 8192, 1024], P('member', 'node'), may hold values from -12 to 12
- layer_norm_gain: bfloat16 [1024], replicated, may hold values from 0.099609375 to 1.8984375
- query_key_value_weight: bfloat16 [1024, 1536], P('node'), may hold values from -0.1875 to 0.1875
- output_weight_matrix: bfloat16 [512, 1024], P('node'), may hold values from -0.25 to 0.25
- decoder_weight_matrix: bfloat16 [98, 1024], replicated, may hold values from -0.1875 to 0.1875
- observed_truth: float32 [98, 8192], P(None, 'node'), may hold values from -9 to 9
- region_mask: int32 [8192], P('node'), may hold values from 0 to 1, as said below
- node_window_halfspan: int32 [8192], P('node'), may hold values from 64 to 256, as said below
Outputs:
- loss: float32 [], replicated
- latent_grad: float32 [8192, 1024], P('node', 'member')
- noise_grad: float32 [16, 8192, 1024], P('member', 'node')
Inputs may be any that keep to these rules, and one draw needn't show every extreme that they name: `region_mask`: 1 on one contiguous run of 2048 nodes whose start is drawn, 0 on all other nodes. `node_window_halfspan`: equal to 256 on every node of the region.
All inputs are finite; a program needn't handle non-finite values.
Results may differ from a plain program's by a relative error of at most 0.019.
Values may be sent and summed in bfloat16 or wider, within the bound.
No kernel may reach another device: no remote copies, remote signals or barrier semaphores. Data moves between devices by JAX's collectives and lax.ppermute only.
A program may use at most 64 MiB of HBM per device.

v0:
```python
import jax
import jax.numpy as jnp
from jax import lax
from jax.sharding import PartitionSpec as P

HEADS = 8
HALF = 256


norm_epsilon = 1e-05
head_epsilon = 1e-06
smooth_width = 0.1
region_share = 0.25


def with_halo(block, sides, width):
    for axis, dim in sides:
        count = lax.axis_size(axis)
        forward = [(i, i + 1) for i in range(count - 1)]
        backward = [(target, source) for source, target in forward]
        low = lax.ppermute(
            lax.slice_in_dim(block, block.shape[dim] - width, None, axis=dim), axis, forward
        )
        high = lax.ppermute(lax.slice_in_dim(block, 0, width, axis=dim), axis, backward)
        block = jnp.concatenate([low, block, high], axis=dim)
    return block


def shifted(value, axis, steps):
    count = lax.axis_size(axis)
    leading, last = (max(0, -steps), min(count, count - steps))
    return lax.ppermute(value, axis, [(source, source + steps) for source in range(leading, last)])


def contract_trailing_axis(left, right):
    return lax.dot_general(
        left, right, (((1,), (1,)), ((), ())), preferred_element_type=jnp.float32
    )


def contract_first(left, right):
    return lax.dot_general(
        left, right, (((0,), (0,)), ((), ())), preferred_element_type=jnp.float32
    )


def layer_norm(hidden_state):
    average = jnp.mean(hidden_state, axis=1, keepdims=True)
    centred = hidden_state - average
    inverse = lax.rsqrt(jnp.mean(centred * centred, axis=1, keepdims=True) + norm_epsilon)
    return (centred * inverse, inverse)


def layer_norm_back(standard, inverse, loss_derivative):
    first_term = jnp.mean(loss_derivative, axis=1, keepdims=True)
    second_term = standard * jnp.mean(loss_derivative * standard, axis=1, keepdims=True)
    return inverse * (loss_derivative - first_term - second_term)


def head_norm(block_rows, head_count):
    row_count = block_rows.shape[0]
    per_head = block_rows.reshape(row_count, head_count, -1)
    inverse = lax.rsqrt(jnp.mean(per_head * per_head, axis=2, keepdims=True) + head_epsilon)
    return ((per_head * inverse).reshape(row_count, -1), inverse)


def head_norm_back(unit_rows, inverse, upstream, head_count):
    row_count = unit_rows.shape[0]
    unit_heads = unit_rows.reshape(row_count, head_count, -1)
    up_heads = upstream.reshape(row_count, head_count, -1)
    along = jnp.mean(up_heads * unit_heads, axis=2, keepdims=True)
    return (inverse * (up_heads - unit_heads * along)).reshape(row_count, -1)


def window_mask(row_start, node_window_halfspan, node_total, half_window):
    row_count = node_window_halfspan.shape[0]
    query_pos = row_start + jnp.arange(row_count, dtype=jnp.int32)[:, None]
    key_pos = (
        row_start - half_window + jnp.arange(row_count + 2 * half_window, dtype=jnp.int32)[None, :]
    )
    offset = key_pos - query_pos
    inside = (offset >= -node_window_halfspan[:, None]) & (offset < node_window_halfspan[:, None])
    return inside & (key_pos >= 0) & (key_pos < node_total)


def head_weights(q_head, k_head, allowed, factor):
    exponent = jnp.where(allowed, jnp.exp(contract_trailing_axis(q_head, k_head) * factor), 0.0)
    return exponent / jnp.sum(exponent, axis=1, keepdims=True)


def attend(q_norm, kv_ext, allowed, head_count):
    inner_width = q_norm.shape[1]
    head_size = inner_width // head_count
    factor = head_size ** (-0.5)

    def one_head(head_index, mixed):
        head_start = head_index * head_size
        q_head = lax.dynamic_slice_in_dim(q_norm, head_start, head_size, 1)
        k_head = lax.dynamic_slice_in_dim(kv_ext, head_start, head_size, 1)
        v_head = lax.dynamic_slice_in_dim(kv_ext, inner_width + head_start, head_size, 1)
        probabilities = head_weights(q_head, k_head, allowed, factor).astype(jnp.bfloat16)
        result = jnp.dot(probabilities, v_head, preferred_element_type=jnp.float32).astype(
            jnp.bfloat16
        )
        return lax.dynamic_update_slice_in_dim(mixed, result, head_start, 1)

    return lax.fori_loop(0, head_count, one_head, jnp.zeros(q_norm.shape, jnp.bfloat16))


def attend_back(q_norm, kv_ext, allowed, mixed_grad, head_count):
    inner_width = q_norm.shape[1]
    head_size = inner_width // head_count
    factor = head_size ** (-0.5)
    row_count = q_norm.shape[0]

    def one_head(head_index, state):
        q_grad, kv_grad, row_sums, row_dots = state
        head_start = head_index * head_size
        q_head = lax.dynamic_slice_in_dim(q_norm, head_start, head_size, 1)
        k_head = lax.dynamic_slice_in_dim(kv_ext, head_start, head_size, 1)
        v_head = lax.dynamic_slice_in_dim(kv_ext, inner_width + head_start, head_size, 1)
        out_grad = lax.dynamic_slice_in_dim(mixed_grad, head_start, head_size, 1)
        exponent = jnp.where(allowed, jnp.exp(contract_trailing_axis(q_head, k_head) * factor), 0.0)
        total = jnp.sum(exponent, axis=1, keepdims=True)
        weights = exponent / total
        probabilities = weights.astype(jnp.bfloat16)
        weight_grad = contract_trailing_axis(out_grad, v_head)
        row_dot = jnp.sum(weights * weight_grad, axis=1, keepdims=True)
        score_grad = (weights * (weight_grad - row_dot) * factor).astype(jnp.bfloat16)
        q_part = jnp.dot(score_grad, k_head, preferred_element_type=jnp.float32)
        k_part = contract_first(score_grad, q_head)
        v_part = contract_first(probabilities, out_grad)
        q_grad = lax.dynamic_update_slice_in_dim(q_grad, q_part, head_start, 1)
        kv_grad = lax.dynamic_update_slice_in_dim(kv_grad, k_part, head_start, 1)
        kv_grad = lax.dynamic_update_slice_in_dim(kv_grad, v_part, inner_width + head_start, 1)
        row_sums = lax.dynamic_update_slice_in_dim(row_sums, total, head_index, 1)
        row_dots = lax.dynamic_update_slice_in_dim(row_dots, row_dot, head_index, 1)
        return (q_grad, kv_grad, row_sums, row_dots)

    start_state = (
        jnp.zeros(q_norm.shape, jnp.float32),
        jnp.zeros(kv_ext.shape, jnp.float32),
        jnp.zeros((row_count, head_count), jnp.float32),
        jnp.zeros((row_count, head_count), jnp.float32),
    )
    return lax.fori_loop(0, head_count, one_head, start_state)


def softened_magnitude(difference):
    return jnp.sqrt(difference * difference + smooth_width * smooth_width)


def softened_derivative(difference):
    return difference / softened_magnitude(difference)


def shards(
    latent,
    member_perturbations,
    layer_norm_gain,
    query_key_value_weight,
    output_weight_matrix,
    decoder_weight_matrix,
    observed_truth,
    region_mask,
    node_window_halfspan,
):
    row_count = member_perturbations.shape[1]
    inner_width = query_key_value_weight.shape[1] // 3
    var_count = decoder_weight_matrix.shape[0]
    member_count = lax.axis_size("member")
    node_total = row_count * lax.axis_size("node")
    row_start = lax.axis_index("node") * row_count
    shared = lax.all_gather(latent, "member", axis=1, tiled=True)
    hidden_state = shared.astype(jnp.float32) + member_perturbations[0].astype(jnp.float32)
    standard, inverse = layer_norm(hidden_state)
    normed = (standard * layer_norm_gain.astype(jnp.float32)).astype(jnp.bfloat16)
    full_qkv, full_out = (
        lax.all_gather(query_key_value_weight, "node", axis=0, tiled=True),
        lax.all_gather(output_weight_matrix, "node", axis=0, tiled=True),
    )
    projected = jnp.dot(normed, full_qkv, preferred_element_type=jnp.float32)
    q_unit, q_inverse = head_norm(projected[:, :inner_width], HEADS)
    k_unit, k_inverse = head_norm(projected[:, inner_width : 2 * inner_width], HEADS)
    q_norm = q_unit.astype(jnp.bfloat16)
    key_value = jnp.concatenate(
        [k_unit.astype(jnp.bfloat16), projected[:, 2 * inner_width :].astype(jnp.bfloat16)], axis=1
    )
    kv_ext = with_halo(key_value, (("node", 0),), HALF)
    allowed = window_mask(row_start, node_window_halfspan, node_total, HALF)
    mixed = attend(q_norm, kv_ext, allowed, HEADS)
    branch = jnp.dot(mixed, full_out, preferred_element_type=jnp.float32)
    updated_state = (hidden_state + branch).astype(jnp.bfloat16)
    realization_outlook = contract_trailing_axis(decoder_weight_matrix, updated_state)
    cell_surface_factor = 1.0 - (1.0 - region_share) * region_mask.astype(jnp.float32)
    all_members_joined = lax.all_gather(realization_outlook[None], "member", axis=0, tiled=True)
    mutual_separations = realization_outlook[None] - all_members_joined
    misfit_vs_truth = realization_outlook - observed_truth
    loss_derivative = softened_derivative(misfit_vs_truth) - jnp.sum(
        softened_derivative(mutual_separations), axis=0
    ) / (member_count - 1)
    dispersion_amount = (jnp.sum(softened_magnitude(mutual_separations), axis=0) - smooth_width) / (
        2 * (member_count - 1)
    )
    incomplete_crps_sum = jnp.sum(
        cell_surface_factor * (softened_magnitude(misfit_vs_truth) - dispersion_amount)
    )
    pred_grad = (cell_surface_factor * loss_derivative).astype(jnp.bfloat16)
    upd_grad = contract_first(pred_grad, decoder_weight_matrix)
    upd_round = upd_grad.astype(jnp.bfloat16)
    mixed_grad = contract_trailing_axis(upd_round, full_out).astype(jnp.bfloat16)
    q_grad, kv_grad, row_sums, row_dots = attend_back(q_norm, kv_ext, allowed, mixed_grad, HEADS)
    own_grad = kv_grad[HALF : HALF + row_count]
    lower_rim = kv_grad[:HALF]
    upper_rim = kv_grad[HALF + row_count :]
    from_upper = shifted(lower_rim, "node", -1)
    from_lower = shifted(upper_rim, "node", 1)
    own_grad = own_grad.at[:HALF].add(from_lower)
    own_grad = own_grad.at[row_count - HALF :].add(from_upper)
    q_raw = head_norm_back(q_unit, q_inverse, q_grad, HEADS)
    k_raw = head_norm_back(k_unit, k_inverse, own_grad[:, :inner_width], HEADS)
    qkv_grad = jnp.concatenate([q_raw, k_raw, own_grad[:, inner_width:]], axis=1).astype(
        jnp.bfloat16
    )
    normed_grad = contract_trailing_axis(qkv_grad, full_qkv)
    hidden_grad = upd_grad + layer_norm_back(
        standard, inverse, normed_grad * layer_norm_gain.astype(jnp.float32)
    )
    noise_grad = hidden_grad[None]
    latent_grad = lax.psum_scatter(hidden_grad, "member", scatter_dimension=1, tiled=True)
    score = lax.psum(incomplete_crps_sum, ("member", "node"))
    loss = score / (member_count * node_total * var_count)
    return (loss, latent_grad, noise_grad)


def solution(mesh):
    placed = (
        P("node", "member"),
        P("member", "node", None),
        P(),
        P("node", None),
        P("node", None),
        P(),
        P(None, "node"),
        P("node"),
        P("node"),
    )
    return jax.shard_map(
        shards,
        mesh=mesh,
        in_specs=placed,
        out_specs=(P(), P("node", "member"), P("member", "node", None)),
        check_vma=False,
    )
```

profile of v0, /device:TPU:1, one launch (start us, length us, event | category | flops | bytes accessed | tf_op | source)
XLA Modules:
  0.0 615.1 jit_solution(1013792244680990992)
XLA Ops:
  8.7 25.9 %all_gather.12 = bf16[256,1024]{0,1:T(8,128)(2,1)S(1)} all-gather(bf16[256,64]{0,1:T(8,128)(2,1)} %param.21), channel_id=1, replica_groups=mesh['member'=16,'node'=32] {'member'}, dimensions={1}, use_global_device_ids=true | all-gather | bytes 557056 | tf_op jit(solution)/shard_map/all_gather | solution.py:174
  35.4 129.0 %all-gather.6.cloned.1.call-done = bf16[1024,1536]{1,0:T(8,128)(2,1)} async-done(((bf16[32,1536]{1,0:T(8,128)(2,1)}), bf16[1024,1536]{1,0:T(8,128)(2,1)}) %all-gather.6.cloned.1.call-update) | async-done | bytes 3145744 | tf_op jit(solution)/shard_map/all_gather | solution.py:179
  164.4 3.0 fusion.46
  169.3 1.4 copy.35
  171.7 1.2 copy.36
  173.8 1.2 copy.38
  176.3 1.3 collective-permute-start.1
  177.6 5.5 collective-permute-start
  183.3 4.4 collective-permute-done.1
  188.5 9.0 %collective-permute-done = bf16[256,1024]{1,0:T(8,128)(2,1)S(1)} collective-permute-done((bf16[256,1024]{1,0:T(8,128)(2,1)S(1)}, bf16[256,1024]{1,0:T(8,128)(2,1)S(1)}, u32[]{:S(2)}, u32[]{:S(2)}) %collective-permute-start) | collective-permute-done | bytes 524320 | tf_op jit(solution)/shard_map/ppermute | solution.py:21
  197.5 1.3 pad_maximum_fusion
  198.9 15.8 %while.38 = (s32[]{:T(128)}, bf16[256,512]{0,1:T(8,128)(2,1)S(1)}, bf16[256,512]{1,0:T(8,128)(2,1)}, bf16[768,1024]{1,0:T(8,128)(2,1)S(1)}, s32[256]{0:T(256)S(1...) while((s32[]{:T(128)}, bf16[256,512]{0,1:T(8,128)(2,1)S(1)}, ...), condition=%wide.region_6.7_spmd.clone, body=%wide.region_4.6_spmd.clone.sunk | while | flops 52510472 | bytes 2075918 | solution.py:107
  198.9 1.5 fusion.91
  200.9 1.5 fusion.91
  202.9 1.5 fusion.91
  204.8 1.5 fusion.91
  206.8 1.5 fusion.91
  208.8 1.5 fusion.91
  210.8 1.5 fusion.91
  212.7 1.5 fusion.91
  214.7 107.9 %all-gather.8.cloned.1.call-done = bf16[512,1024]{1,0:T(8,128)(2,1)} async-done(((bf16[16,1024]{1,0:T(8,128)(2,1)}), bf16[512,1024]{1,0:T(8,128)(2,1)}) %all-gather.8.cloned.1.call-update) | async-done | bytes 1048592 | tf_op jit(solution)/shard_map/all_gather | solution.py:180
  322.7 2.6 fusion.38
  325.4 45.0 %all-gather.10.cloned.1.call-done = f32[16,98,256]{2,1,0:T(8,128)} async-done(((f32[1,98,256]{2,1,0:T(8,128)}), f32[16,98,256]{2,1,0:T(8,128)}) %all-gather.10.cloned.1.call-update) | async-done | bytes 1605648 | tf_op jit(solution)/shard_map/all_gather | solution.py:196
  370.4 3.0 fusion.36
  373.8 1.2 convolution_convert_fusion.1
  376.1 53.3 %while.39 = (s32[]{:T(128)}, f32[256,512]{0,1:T(8,128)}, f32[768,1024]{0,1:T(8,128)S(1)}, bf16[256,512]{1,0:T(8,128)(2,1)}, bf16[768,1024]{1,0:T(8,128)(2,1)}, /...) while((s32[]{:T(128)}, f32[256,512]{0,1:T(8,128)}, ...), condition=%wide.region_14.15_spmd.clone, body=%wide.region_11.14_spmd.clone.sunk | while | flops 129564168 | bytes 8271698 | solution.py:146
  376.1 1.6 fusion.99
  377.7 1.4 multiply_reduce_fusion.9
  379.3 2.0 convolution_dynamic-update-slice_fusion.6
  382.8 1.6 fusion.99
  384.4 1.4 multiply_reduce_fusion.9
  386.0 2.0 convolution_dynamic-update-slice_fusion.6
  389.4 1.6 fusion.99
  391.1 1.4 multiply_reduce_fusion.9
  392.6 2.0 convolution_dynamic-update-slice_fusion.6
  394.6 1.1 convolution_dynamic-update-slice_fusion.7
  396.1 1.6 fusion.99
  397.7 1.4 multiply_reduce_fusion.9
  399.3 2.0 convolution_dynamic-update-slice_fusion.6
  402.8 1.6 fusion.99
  404.4 1.4 multiply_reduce_fusion.9
  406.0 2.0 convolution_dynamic-update-slice_fusion.6
  409.4 1.6 fusion.99
  411.1 1.4 multiply_reduce_fusion.9
  412.6 2.0 convolution_dynamic-update-slice_fusion.6
  416.1 1.6 fusion.99
  417.7 1.4 multiply_reduce_fusion.9
  419.3 2.0 convolution_dynamic-update-slice_fusion.6
  422.8 1.6 fusion.99
  424.4 1.4 multiply_reduce_fusion.9
  426.0 2.0 convolution_dynamic-update-slice_fusion.6
  429.4 2.4 copy.42
  431.8 2.8 fusion.69
  434.6 4.4 collective-permute-start.2
  439.0 1.5 collective-permute-start.3
  442.7 41.3 %collective-permute-done.2 = f32[256,1024]{1,0:T(8,128)S(1)} collective-permute-done((f32[256,1024]{1,0:T(8,128)}, f32[256,1024]{1,0:T(8,128)S(1)}, u32[]{:S(2)}, u32[]{:S(2)}) %collective-permute-start.2) | collective-permute-done | bytes 1048608 | tf_op jit(solution)/shard_map/ppermute | solution.py:32
  484.0 1.8 fusion.39
  487.4 2.2 copy.45
  489.6 1.3 multiply_reduce_fusion.3
  491.8 2.0 copy.46
  493.9 2.2 multiply_convert_fusion.4
  496.8 1.2 fusion.66
  498.5 1.3 copy.49
  500.5 106.3 %psum.7 = f32[]{:T(128)} all-reduce(f32[]{:T(128)} %multiply_reduce_fusion.7), channel_id=1, replica_groups=mesh['member'=16,'node'=32] {'member','node'}, use_global_device_ids=true, to_apply=%region_9.10 | all-reduce | flops 1 | bytes 8 | tf_op jit(solution)/shard_map/psum | solution.py:231
  (158 shorter events, 32.0 us)
Async XLA Ops:
  7.2 315.5 %copy-start = (bf16[98,1024]{1,0:T(8,128)(2,1)S(1)}, bf16[98,1024]{1,0:T(8,128)(2,1)}, u32[]{:S(2)}) copy-start(bf16[98,1024]{1,0:T(8,128)(2,1)} %param.26) | copy-start | bytes 602116
  7.2 27.6 %copy-start.10 = (bf16[1,256,1024]{2,1,0:T(8,128)(2,1)S(1)}, bf16[1,256,1024]{2,1,0:T(8,128)(2,1)}, u32[]{:S(2)}) copy-start(bf16[1,256,1024]{2,1,0:T(8,128)(2,1)} %param.22) | copy-start | bytes 1572868
  7.2 157.2 %all-gather.6.cloned.1.call-start = ((), (), s32[]{:S(2)}) async-start(), calls=%async_computation.1 | async-start | bytes 3244032 | tf_op jit(solution)/shard_map/all_gather | solution.py:179
  7.9 314.7 %all-gather.8.cloned.1.call-start = ((), (), s32[]{:S(2)}) async-start(), calls=%async_computation.2 | async-start | bytes 1081344 | tf_op jit(solution)/shard_map/all_gather | solution.py:180
  34.8 287.8 %copy-start.3 = (bf16[256,1024]{1,0:T(8,128)(2,1)}, bf16[256,1024]{1,0:T(8,128)(2,1)S(1)}, u32[]{:S(2)}) copy-start(bf16[256,1024]{1,0:T(8,128)(2,1)S(1)} %copy.34) | copy-start | bytes 1572868
  167.4 7.7 %copy-start.5 = (f32[256,1536]{1,0:T(8,128)}, f32[256,1536]{1,0:T(8,128)S(1)}, u32[]{:S(2)}) copy-start(f32[256,1536]{1,0:T(8,128)S(1)} %fusion.46) | copy-start | bytes 4718596
  169.2 2.4 copy-start.13
  170.7 3.1 copy-start.14
  172.9 3.1 copy-start.7
  175.1 1.2 copy-start.9
  175.1 1.1 copy-start.20
  175.1 8.1 %copy-start.30 = (s32[256]{0:T(256)S(1)}, s32[256]{0:T(256)}, u32[]{:S(2)}) copy-start(s32[256]{0:T(256)} %param.29) | copy-start | bytes 3076
  176.0 1.6 copy-start.19
  176.3 11.4 %collective-permute-start.1 = (bf16[256,1024]{1,0:T(8,128)(2,1)S(1)}, bf16[256,1024]{1,0:T(8,128)(2,1)S(1)}, u32[]{:S(2)}, u32[]{:S(2)}) collective-permute-start(bf16[256,1024]{1,0:T(8,128)(2,1)S(1)} %pad_maximum_fusion.1), channel_id=1, source_target_pairs={{1,0},{2,1},{3,2},{4,3},{5,4},{6,5},{7,6},{8,7},{9,8},{10,9},{11,1... | collective-permute-start | bytes 1572872 | tf_op jit(solution)/shard_map/ppermute | solution.py:24
  177.6 19.9 %collective-permute-start = (bf16[256,1024]{1,0:T(8,128)(2,1)S(1)}, bf16[256,1024]{1,0:T(8,128)(2,1)S(1)}, u32[]{:S(2)}, u32[]{:S(2)}) collective-permute-start(bf16[256,1024]{1,0:T(8,128)(2,1)S(1)} %pad_maximum_fusion.1), channel_id=1, source_target_pairs={{0,1},{1,2},{2,3},{3,4},{4,5},{5,6},{6,7},{7,8},{8,9},{9,10},{10,1... | collective-permute-start | bytes 1572872 | tf_op jit(solution)/shard_map/ppermute | solution.py:21
  183.2 187.2 %all-gather.10.cloned.1.call-start = ((), (), s32[]{:S(2)}) async-start(), calls=%async_computation.3 | async-start | bytes 1810432 | tf_op jit(solution)/shard_map/all_gather | solution.py:196
  187.7 0.8 copy-start.23
  198.8 123.8 %copy-start.11 = (bf16[1,256,1024]{2,1,0:T(8,128)(2,1)S(1)}, bf16[1,256,1024]{2,1,0:T(8,128)(2,1)}, u32[]{:S(2)}) copy-start(bf16[1,256,1024]{2,1,0:T(8,128)(2,1)} %param.22) | copy-start | bytes 1572868
  214.7 158.7 %copy-start.18 = (bf16[768,1024]{1,0:T(8,128)(2,1)}, bf16[768,1024]{1,0:T(8,128)(2,1)S(1)}, u32[]{:S(2)}) copy-start(bf16[768,1024]{1,0:T(8,128)(2,1)S(1)} %get-tuple-element.743) | copy-start | bytes 4718596
  214.7 110.7 %copy-start.29 = (s32[256]{0:T(256)S(1)}, s32[256]{0:T(256)}, u32[]{:S(2)}) copy-start(s32[256]{0:T(256)} %param.28) | copy-start | bytes 3076
  325.3 48.1 %copy-start.21 = (f32[256,98]{0,1:T(8,128)S(1)}, f32[256,98]{0,1:T(8,128)}, u32[]{:S(2)}) copy-start(f32[256,98]{0,1:T(8,128)} %fusion.38) | copy-start | bytes 301060
  325.3 48.1 %copy-start.24 = (f32[98,256]{1,0:T(8,128)S(1)}, f32[98,256]{1,0:T(8,128)}, u32[]{:S(2)}) copy-start(f32[98,256]{1,0:T(8,128)} %param.27) | copy-start | bytes 301060
  325.3 282.1 %reduce-scatter.4.cloned.1.call-start = ((), (), s32[]{:S(2)}) async-start(), calls=%async_computation.4 | async-start | bytes 1114112
  370.4 3.4 copy-start.22
  373.8 2.3 copy-start.1
  376.1 1.6 copy-start.27
  382.8 1.6 copy-start.27
  389.4 1.6 copy-start.27
  396.1 1.6 copy-start.27
  402.7 1.6 copy-start.27
  409.4 1.6 copy-start.27
  416.1 1.6 copy-start.27
  422.8 1.6 copy-start.27
  431.8 8.7 %copy-start.16 = (f32[256,512]{0,1:T(8,128)S(1)}, f32[256,512]{0,1:T(8,128)}, u32[]{:S(2)}) copy-start(f32[256,512]{0,1:T(8,128)} %get-tuple-element.353) | copy-start | bytes 1572868
  431.8 9.7 %copy-start.15 = (f32[256,512]{0,1:T(8,128)S(1)}, f32[256,512]{0,1:T(8,128)}, u32[]{:S(2)}) copy-start(f32[256,512]{0,1:T(8,128)} %copy-done.14) | copy-start | bytes 1572868
  434.6 49.4 %collective-permute-start.2 = (f32[256,1024]{1,0:T(8,128)}, f32[256,1024]{1,0:T(8,128)S(1)}, u32[]{:S(2)}, u32[]{:S(2)}) collective-permute-start(f32[256,1024]{1,0:T(8,128)} %get-tuple-element.478), channel_id=1, source_target_pairs={{0,1},{1,2},{2,3},{3,4},{4,5},{5,6},{6,7},{7,8},{8,9},{9,10},{10,1... | collective-permute-start | bytes 3145736 | tf_op jit(solution)/shard_map/ppermute | solution.py:32
  439.0 45.0 %collective-permute-start.3 = (f32[256,1024]{1,0:T(8,128)S(1)}, f32[256,1024]{1,0:T(8,128)}, u32[]{:S(2)}, u32[]{:S(2)}) collective-permute-start(f32[256,1024]{1,0:T(8,128)S(1)} %get-tuple-element.479), channel_id=1, source_target_pairs={{1,0},{2,1},{3,2},{4,3},{5,4},{6,5},{7,6},{8,7},{9,8},{10,9},{11,1... | collective-permute-start | bytes 3145736 | tf_op jit(solution)/shard_map/ppermute | solution.py:32
  487.4 6.5 %copy-start.6 = (f32[256,1536]{1,0:T(8,128)S(1)}, f32[256,1536]{1,0:T(8,128)}, u32[]{:S(2)}) copy-start(f32[256,1536]{1,0:T(8,128)} %copy-done.5) | copy-start | bytes 4718596
  487.4 6.5 %copy-start.8 = (f32[256,512]{1,0:T(8,128)S(1)}, f32[256,512]{1,0:T(8,128)}, u32[]{:S(2)}) copy-start(f32[256,512]{1,0:T(8,128)} %copy-done.7) | copy-start | bytes 1572868
  493.9 2.2 copy-start.4
  493.9 2.2 copy-start.12
  493.9 2.2 copy-start.28
  493.9 2.9 copy-start.31
  496.8 1.2 copy-start.2
  498.5 2.1 copy-start.17
  498.5 1.4 copy-start.25
  498.5 1.4 copy-start.26
Sparse Core Ops, SparseCore 0:
  11.1 153.2 all-gather.5
  183.3 139.3 all-gather.7
  325.4 44.8 all-gather.9
  500.0 69.0 reduce-scatter.3
where the time goes:
time: 617 us; the launch traced here: 615 us
  waiting for transfers between devices  337 us (55%)
  blocking collectives  132 us (21%)
  matrix products  75.3 us (12%)
  local copies, waits for them, and re-layouts  26 us (4%)
  between operations  16.1 us (3%)
  other arithmetic  14.7 us (2%)
  starting transfers between devices  12.8 us (2%)
    all_gather x1, waiting for transfers between devices, shards(): lax.all_gather(query_key_value_weight, 'node', axis=0, tiled=True)  129 us
    all_gather x1, waiting for transfers between devices, shards(): lax.all_gather(output_weight_matrix, 'node', axis=0, tiled=True)  108 us
    psum x1, blocking collectives, shards(): score = lax.psum(incomplete_crps_sum, ('member', 'node'))  106 us
    all_gather x1, waiting for transfers between devices, shards(): lax.all_gather(realization_outlook[None], 'member', axis=0, tiled=True)  45 us
    ppermute x2, waiting for transfers between devices, shifted(): lax.ppermute(value, axis, [(source, source + steps) for source in range(l...  41.3 us
    dot_general x27, matrix products, contract_trailing_axis(): lax.dot_general(left, right, (((1,), (1,)), ((), ())), preferred_element_...  40.6 us
    all_gather x1, blocking collectives, shards(): shared = lax.all_gather(latent, 'member', axis=1, tiled=True)  25.9 us
    dot_general x8, matrix products, one_head(): q_part = jnp.dot(score_grad, k_head, preferred_element_type=jnp.float32)  16 us
  transfers between devices with their start and end apart: 8, of which 6 were waited for; matrix products, arithmetic and copies ran while one was open for 3% of the time, Pallas kernels for 0%

commit v1 on v0

v1 whole, which is shorter than its diff:
```python
import functools
import math

import jax
import jax.numpy as jnp
from jax import lax
from jax.experimental import pallas as pl
from jax.experimental.pallas import tpu as pltpu
from jax.sharding import Mesh, PartitionSpec as P

HEADS = 8
HEAD = 64
INNER = 512
ROWS = 256
HALF = 256
EXT = ROWS + 2 * HALF
WIDTH = 1024
VARS = 98
LANES = 128
MEMBERS = 16
SLOT = ROWS // MEMBERS
TILE = 128
WINDOW = TILE + 2 * HALF
PACKED = 2048

norm_epsilon = 1e-05
head_epsilon = 1e-06
smooth_width = 0.1
region_share = 0.25
exponent_scale = math.log2(math.e) / 8.0

MEMBER = ("y", "xl", "c")
NODE = ("z", "xh")
EVERY = MEMBER + NODE

bf16 = jnp.bfloat16
f32 = jnp.float32


def mm(left, right):
    return lax.dot_general(left, right, (((1,), (0,)), ((), ())), preferred_element_type=f32)


def mm_t(left, right):
    return lax.dot_general(left, right, (((1,), (1,)), ((), ())), preferred_element_type=f32)


def split(value):
    high = value.astype(bf16)
    return high, (value - high.astype(f32)).astype(bf16)


def segment_matrix(scale):
    rows = lax.broadcasted_iota(jnp.int32, (INNER, INNER), 0) // HEAD
    columns = lax.broadcasted_iota(jnp.int32, (INNER, INNER), 1) // HEAD
    return jnp.where(rows == columns, scale, 0.0).astype(bf16)


def head_sums(value, segments):
    high, low = split(value)
    return mm(high, segments) + mm(low, segments)


def lane_index(rows, lanes):
    return lax.broadcasted_iota(jnp.int32, (rows, lanes), 1)


def norm_kernel(lat_ref, low_ref, own_ref, high_ref, gain_ref, normed_ref, latent_ref):
    gain = gain_ref[...].astype(f32)
    for block, pert_ref in enumerate((low_ref, own_ref, high_ref)):
        for part in range(2):
            rows = slice(part * TILE, (part + 1) * TILE)
            lanes = slice(block * ROWS + part * TILE, block * ROWS + (part + 1) * TILE)
            lat = lat_ref[:, lanes].astype(f32).T
            if block == 1:
                latent_ref[rows, :] = lat.astype(bf16)
            hidden = lat + pert_ref[rows, :].astype(f32)
            centred = hidden - jnp.mean(hidden, axis=1, keepdims=True)
            inverse = lax.rsqrt(jnp.mean(centred * centred, axis=1, keepdims=True) + norm_epsilon)
            normed_ref[lanes, :] = (centred * inverse * gain).astype(bf16)


def out_weights(w_ref, side):
    rows = slice(side * 16, side * 16 + 16)
    return w_ref[:, rows, 3 * INNER :].reshape(INNER // 2, INNER)


def qkv_weights(w_ref, part):
    return w_ref[:, :, part * INNER : (part + 1) * INNER].reshape(INNER, INNER)


def forward_kernel(
    place_ref, normed_ref, wa_ref, wb_ref, latent_ref, pert_ref, reach_ref, decoder_ref,
    q_ref, k_ref, v_ref, unit_ref, factor_ref, mixed_ref, total_ref, forecast_ref,
    bias_ref, mixed_low_ref,
):
    core = place_ref[0]
    row_start = place_ref[1]
    segments = segment_matrix(1.0 / HEAD)
    near = pl.ds(pl.multiple_of(core * INNER, INNER), INNER)
    far = pl.ds(pl.multiple_of((1 - core) * INNER, INNER), INNER)
    for block in range(3):
        rows = slice(block * ROWS, (block + 1) * ROWS)
        left, right = normed_ref[rows, near], normed_ref[rows, far]
        for part, out_ref in enumerate((q_ref, k_ref, v_ref)):
            projected = mm(left, qkv_weights(wa_ref, part)) + mm(right, qkv_weights(wb_ref, part))
            if part < 2:
                factor = lax.rsqrt(head_sums(projected * projected, segments) + head_epsilon)
                unit = projected * factor
                if block == 1:
                    unit_ref[:, part * INNER : (part + 1) * INNER] = unit
                    factor_ref[:, part * INNER : (part + 1) * INNER] = factor
                projected = unit
            out_ref[rows, :] = projected.astype(bf16)

    for tile in range(2):
        offset = (
            lane_index(TILE, WINDOW)
            - HALF
            - lax.broadcasted_iota(jnp.int32, (TILE, WINDOW), 0)
        )
        position = row_start - HALF + tile * TILE + lane_index(TILE, WINDOW)
        reach = reach_ref[tile * TILE : (tile + 1) * TILE, :]
        inside = (offset >= -reach) & (offset < reach) & (position >= 0) & (position < place_ref[2])
        bias_ref[tile] = jnp.where(inside, 0.0, -1e30)

    first = lane_index(1, LANES) < HEAD

    def one_pair(pair, carry):
        lanes = pl.ds(pl.multiple_of(pair * LANES, LANES), LANES)
        for tile in range(2):
            rows = slice(tile * TILE, (tile + 1) * TILE)
            window = slice(tile * TILE, tile * TILE + WINDOW)
            queries = q_ref[ROWS + tile * TILE : ROWS + (tile + 1) * TILE, lanes]
            keys = k_ref[window, lanes]
            values = v_ref[window, lanes]
            bias = bias_ref[tile]
            outs = []
            for mine in (first, ~first):
                score = mm_t(jnp.where(mine, queries, jnp.zeros_like(queries)), keys)
                weight = jnp.exp2(score * exponent_scale + bias).astype(bf16)
                outs.append(mm(weight, jnp.where(mine, values, jnp.ones_like(values))))
            total = pltpu.roll(jnp.where(first, outs[1], outs[0]), HEAD, 1)
            mixed = jnp.where(first, outs[0], outs[1]) / total
            mixed_ref[rows, lanes] = mixed
            mixed_low_ref[rows, lanes] = mixed.astype(bf16)
            total_ref[rows, lanes] = total
        return carry

    lax.fori_loop(0, HEADS // 2, one_pair, 0)

    near_out = pl.ds(pl.multiple_of(core * (INNER // 2), INNER // 2), INNER // 2)
    far_out = pl.ds(pl.multiple_of((1 - core) * (INNER // 2), INNER // 2), INNER // 2)
    left, right = mixed_low_ref[:, near_out], mixed_low_ref[:, far_out]
    forecast = jnp.zeros((ROWS, LANES), f32)
    for side in range(2):
        columns = slice(side * INNER, (side + 1) * INNER)
        branch = mm(left, out_weights(wa_ref, side)) + mm(right, out_weights(wb_ref, side))
        hidden = latent_ref[:, columns].astype(f32) + pert_ref[:, columns].astype(f32)
        updated = (hidden + branch).astype(bf16)
        forecast = forecast + mm_t(updated, decoder_ref[:, columns])
    forecast_ref[...] = forecast


def score_kernel(forecast_ref, truth_ref, area_ref, out_ref):
    lanes = lane_index(SLOT, LANES)
    area = jnp.where(lanes < VARS, area_ref[...], 0.0)
    truth = truth_ref[...]
    square = smooth_width * smooth_width
    loss = jnp.zeros((SLOT, LANES), f32)
    for member in range(MEMBERS):
        own = forecast_ref[member]
        pull = jnp.zeros((SLOT, LANES), f32)
        spread = jnp.zeros((SLOT, LANES), f32)
        for other in range(MEMBERS):
            if other == member:
                continue
            gap = own - forecast_ref[other]
            power = gap * gap + square
            inverse = lax.rsqrt(power)
            pull = pull + gap * inverse
            spread = spread + power * inverse
        gap = own - truth
        power = gap * gap + square
        inverse = lax.rsqrt(power)
        loss = loss + area * (power * inverse - spread * (0.5 / (MEMBERS - 1)))
        out_ref[member] = (area * (gap * inverse - pull * (1.0 / (MEMBERS - 1)))).astype(bf16)
    total = jnp.sum(jnp.sum(loss, axis=1, keepdims=True), axis=0, keepdims=True)
    total = jnp.broadcast_to(total, (SLOT, LANES))
    high, rest = split(total)
    middle = rest
    low = (total - high.astype(f32) - middle.astype(f32)).astype(bf16)
    for member in range(MEMBERS):
        kept = out_ref[member]
        kept = jnp.where(lanes == VARS, high, kept)
        kept = jnp.where(lanes == VARS + 1, middle, kept)
        out_ref[member] = jnp.where(lanes == VARS + 2, low, kept)


def mixed_gradient(upd_low, core, wa_ref, wb_ref, target_ref, rows):
    near_out = pl.ds(pl.multiple_of(core * (INNER // 2), INNER // 2), INNER // 2)
    far_out = pl.ds(pl.multiple_of((1 - core) * (INNER // 2), INNER // 2), INNER // 2)
    for w_ref, lanes in ((wa_ref, near_out), (wb_ref, far_out)):
        target_ref[rows, lanes] = mm_t(upd_low[:, :INNER], out_weights(w_ref, 0)) + mm_t(
            upd_low[:, INNER:], out_weights(w_ref, 1)
        )


def gradient_operands(scaled, row_dot, g0_ref, g1_ref, rows):
    first = lane_index(1, LANES) < HEAD
    spot = lane_index(ROWS, LANES) % HEAD
    for pair in range(HEADS // 2):
        lanes = slice(pair * LANES, (pair + 1) * LANES)
        high, low = split(-pltpu.roll(row_dot[:, lanes], HEAD, 1))
        zero = jnp.zeros_like(high)
        extra = jnp.where(spot == 0, high, jnp.where(spot == 1, low, zero))
        own = scaled[:, lanes]
        g0_ref[rows, lanes] = jnp.where(first, own, extra)
        g1_ref[rows, lanes] = jnp.where(first, extra, own)


def pick(base, rows, lanes):
    row = lax.broadcasted_iota(jnp.int32, (rows, lanes), 0)
    lane = lane_index(rows, lanes)
    return row, lane


def upstream_kernel(
    place_ref, pg_ref, decoder_ref, wa_ref, wb_ref, mixed_ref, total_ref,
    upd_ref, scaled_ref, g0_ref, g1_ref, message_ref, loss_ref, grad_ref,
):
    core = place_ref[0]
    pg = pg_ref[...]
    upd = mm(pg, decoder_ref[...])
    upd_ref[...] = upd
    everything = slice(0, ROWS)
    mixed_gradient(upd.astype(bf16), core, wa_ref, wb_ref, grad_ref, everything)
    grad = grad_ref[...].astype(bf16).astype(f32)
    total = total_ref[...]
    inverse = 1.0 / total
    row_dot = head_sums(grad * mixed_ref[...], segment_matrix(1.0)) * inverse
    scaled = (grad * inverse).astype(bf16)
    scaled_ref[...] = scaled
    gradient_operands(scaled, row_dot, g0_ref, g1_ref, everything)

    row, lane = pick(None, INNER, LANES)
    head_row = (row % HEAD == 0)
    chosen = lambda start: jnp.where(head_row & (lane == start + row // HEAD), 1.0, 0.0).astype(bf16)
    high, low = split(total)
    stats = mm(high, chosen(VARS)) + mm(low, chosen(VARS + 8)) + mm(row_dot.astype(bf16), chosen(VARS + 16))
    lanes = lane_index(ROWS, LANES)
    message_ref[...] = jnp.where(lanes < VARS, pg.astype(f32), stats).astype(bf16)
    kept = jnp.where((lanes >= VARS) & (lanes < VARS + 3), pg.astype(f32), 0.0)
    total_loss = jnp.sum(jnp.sum(kept, axis=1, keepdims=True), axis=0, keepdims=True) * (1.0 / SLOT)
    loss_ref[...] = jnp.broadcast_to(total_loss, (8, LANES))


def query_kernel(
    place_ref, q_ref, k_ref, v_ref, g0_ref, g1_ref, reach_ref, qgrad_ref, bias_ref,
):
    row_start = place_ref[1]
    for tile in range(2):
        offset = (
            lane_index(TILE, WINDOW)
            - HALF
            - lax.broadcasted_iota(jnp.int32, (TILE, WINDOW), 0)
        )
        position = row_start - HALF + tile * TILE + lane_index(TILE, WINDOW)
        reach = reach_ref[tile * TILE : (tile + 1) * TILE, :]
        inside = (offset >= -reach) & (offset < reach) & (position >= 0) & (position < place_ref[2])
        bias_ref[tile] = jnp.where(inside, 0.0, -1e30)
    first = lane_index(1, LANES) < HEAD

    def one_pair(pair, carry):
        lanes = pl.ds(pl.multiple_of(pair * LANES, LANES), LANES)
        for tile in range(2):
            rows = slice(tile * TILE, (tile + 1) * TILE)
            window = slice(tile * TILE, tile * TILE + WINDOW)
            queries = q_ref[ROWS + tile * TILE : ROWS + (tile + 1) * TILE, lanes]
            keys = k_ref[window, lanes]
            values = v_ref[window, lanes]
            bias = bias_ref[tile]
            grads = []
            for mine, g_ref in ((first, g0_ref), (~first, g1_ref)):
                score = mm_t(jnp.where(mine, queries, jnp.zeros_like(queries)), keys)
                weight = jnp.exp2(score * exponent_scale + bias)
                pull = mm_t(g_ref[rows, lanes], jnp.where(mine, values, jnp.ones_like(values)))
                grads.append(mm((weight * pull).astype(bf16), keys))
            qgrad_ref[rows, lanes] = jnp.where(first, grads[0], grads[1]) * 0.125
        return carry

    lax.fori_loop(0, HEADS // 2, one_pair, 0)


def backward_kernel(
    place_ref, low_ref, high_ref, decoder_ref, wa_ref, wb_ref, q_ref, k_ref, v_ref,
    scaled_ref, g0_ref, g1_ref, reach_ref, qgrad_ref, unit_ref, factor_ref,
    latent_ref, pert_ref, gain_ref, upd_ref, loss_a_ref, loss_b_ref,
    noise_ref, send_ref,
    all_scaled, all_g0, all_g1, bias_ref, grad_ref, kv_ref, normed_grad_ref,
):
    core = place_ref[0]
    row, lane = pick(None, LANES, INNER)
    spread = lambda start: row == start + lane // HEAD
    expand_total = jnp.where(spread(VARS) | spread(VARS + 8), 1.0, 0.0).astype(bf16)
    expand_dot = jnp.where(spread(VARS + 16), 1.0, 0.0).astype(bf16)
    middle = slice(ROWS, 2 * ROWS)
    all_scaled[middle, :] = scaled_ref[...]
    all_g0[middle, :] = g0_ref[...]
    all_g1[middle, :] = g1_ref[...]
    for block, message_ref in ((0, low_ref), (2, high_ref)):
        rows = slice(block * ROWS, (block + 1) * ROWS)
        message = message_ref[...]
        mixed_gradient(mm(message, decoder_ref[...]).astype(bf16), core, wa_ref, wb_ref, grad_ref, slice(0, ROWS))
        grad = grad_ref[...].astype(bf16).astype(f32)
        total = mm(message, expand_total)
        scaled = (grad / jnp.where(total > 0.0, total, 1.0)).astype(bf16)
        all_scaled[rows, :] = scaled
        gradient_operands(scaled, mm(message, expand_dot), all_g0, all_g1, rows)

    for tile in range(2):
        offset = (
            HALF
            + lax.broadcasted_iota(jnp.int32, (TILE, WINDOW), 0)
            - lane_index(TILE, WINDOW)
        )
        reach = reach_ref[0:1, tile * TILE : tile * TILE + WINDOW]
        bias_ref[tile] = jnp.where((offset >= -reach) & (offset < reach), 0.0, -1e30)
    first = lane_index(1, LANES) < HEAD

    def one_pair(pair, carry):
        start = pl.multiple_of(pair * LANES, LANES)
        lanes = pl.ds(start, LANES)
        value_lanes = pl.ds(pl.multiple_of(INNER + start, LANES), LANES)
        for tile in range(2):
            rows = slice(tile * TILE, (tile + 1) * TILE)
            window = slice(tile * TILE, tile * TILE + WINDOW)
            keys = k_ref[ROWS + tile * TILE : ROWS + (tile + 1) * TILE, lanes]
            values = v_ref[ROWS + tile * TILE : ROWS + (tile + 1) * TILE, lanes]
            queries = q_ref[window, lanes]
            scaled = all_scaled[window, lanes]
            bias = bias_ref[tile]
            key_grads = []
            value_grads = []
            for mine, g_ref in ((first, all_g0), (~first, all_g1)):
                score = mm_t(jnp.where(mine, keys, jnp.zeros_like(keys)), queries)
                weight = jnp.exp2(score * exponent_scale + bias)
                pull = mm_t(jnp.where(mine, values, jnp.ones_like(values)), g_ref[window, lanes])
                value_grads.append(mm(weight.astype(bf16), scaled))
                key_grads.append(mm((weight * pull).astype(bf16), queries))
            kv_ref[rows, lanes] = jnp.where(first, key_grads[0], key_grads[1]) * 0.125
            kv_ref[rows, value_lanes] = jnp.where(first, value_grads[0], value_grads[1])
        return carry

    lax.fori_loop(0, HEADS // 2, one_pair, 0)

    segments = segment_matrix(1.0 / HEAD)
    parts = []
    for part, grad in ((0, qgrad_ref[...]), (1, kv_ref[:, :INNER])):
        columns = slice(part * INNER, (part + 1) * INNER)
        unit = unit_ref[:, columns]
        along = head_sums(grad * unit, segments)
        parts.append((factor_ref[:, columns] * (grad - unit * along)).astype(bf16))
    parts.append(kv_ref[:, INNER:].astype(bf16))
    near = pl.ds(pl.multiple_of(core * INNER, INNER), INNER)
    far = pl.ds(pl.multiple_of((1 - core) * INNER, INNER), INNER)
    for w_ref, lanes in ((wa_ref, near), (wb_ref, far)):
        normed_grad_ref[:, lanes] = (
            mm_t(parts[0], qkv_weights(w_ref, 0))
            + mm_t(parts[1], qkv_weights(w_ref, 1))
            + mm_t(parts[2], qkv_weights(w_ref, 2))
        )
    gain = gain_ref[...].astype(f32)
    for part in range(2):
        rows = slice(part * TILE, (part + 1) * TILE)
        hidden = latent_ref[rows, :].astype(f32) + pert_ref[rows, :].astype(f32)
        centred = hidden - jnp.mean(hidden, axis=1, keepdims=True)
        inverse = lax.rsqrt(jnp.mean(centred * centred, axis=1, keepdims=True) + norm_epsilon)
        standard = centred * inverse
        grad = normed_grad_ref[rows, :] * gain
        first_term = jnp.mean(grad, axis=1, keepdims=True)
        second_term = standard * jnp.mean(grad * standard, axis=1, keepdims=True)
        result = upd_ref[rows, :] + inverse * (grad - first_term - second_term)
        noise_ref[rows, :] = result
        turned = result.T.astype(bf16)
        for member in range(MEMBERS):
            send_ref[member, :HEAD, rows] = turned[member * HEAD : (member + 1) * HEAD, :]
    loss = jnp.broadcast_to(loss_a_ref[0:1, 0:1] + loss_b_ref[0:1, 0:1], (16, ROWS))
    high, mid = split(loss)
    low = (loss - high.astype(f32) - mid.astype(f32)).astype(bf16)
    lanes = lane_index(16, ROWS)
    tail = jnp.where(lanes == 0, high, jnp.where(lanes == 1, mid, jnp.where(lanes == 2, low, jnp.zeros_like(low))))
    for member in range(MEMBERS):
        send_ref[member, HEAD:, :] = tail


def finish_kernel(received_ref, latent_grad_ref, loss_ref):
    total = received_ref[0].astype(f32)
    for member in range(1, MEMBERS):
        total = total + received_ref[member].astype(f32)
    latent_grad_ref[...] = total[:HEAD]
    loss_ref[...] = jnp.broadcast_to(jnp.sum(total[HEAD : HEAD + 1, :], axis=1, keepdims=True), (8, LANES))


def call(body, outs, scratch, cost, *operands):
    specs = [
        pl.BlockSpec(memory_space=pltpu.SMEM if o.dtype == jnp.int32 and o.ndim == 1 else pltpu.VMEM)
        for o in operands
    ]
    result = pl.pallas_call(
        body,
        out_shape=tuple(jax.ShapeDtypeStruct(shape, kind) for shape, kind in outs),
        in_specs=specs,
        out_specs=tuple(pl.BlockSpec(memory_space=pltpu.VMEM) for _ in outs),
        scratch_shapes=[pltpu.VMEM(shape, kind) for shape, kind in scratch],
        compiler_params=pltpu.CompilerParams(vmem_limit_bytes=40 * 1024 * 1024),
        cost_estimate=pl.CostEstimate(flops=cost, bytes_accessed=4_000_000, transcendentals=0),
    )(*operands)
    return result


def both_ways(block):
    count = lax.axis_size(NODE)
    low = lax.ppermute(block, NODE, [(i, i + 1) for i in range(count - 1)])
    high = lax.ppermute(block, NODE, [(i + 1, i) for i in range(count - 1)])
    return low, high


def flat(y, xl, c, z, xh):
    return (((y * 2 + xl) * 2 + c) * 16 + z) * 2 + xh


def rank(y, xl, c):
    return c * 8 + y * 2 + xl


def members():
    return [(y, xl, c) for y in range(4) for xl in range(2) for c in range(2)]


def weight_route():
    by_rank = {rank(*member): member for member in members()}
    pairs = []
    for member in members():
        for z in range(16):
            for xh in range(2):
                source = flat(*by_rank[z], rank(*member), xh)
                pairs.append((source, flat(*member, z, xh)))
    return pairs


def loss_route(step):
    pairs = []
    for index, member in enumerate(members()):
        for node in range(32):
            target = (node + 2 * index + step) % 32
            pairs.append((flat(*member, node // 2, node % 2), flat(*member, target // 2, target % 2)))
    return pairs


def shards(
    latent,
    member_perturbations,
    layer_norm_gain,
    query_key_value_weight,
    output_weight_matrix,
    decoder_weight_matrix,
    observed_truth,
    region_mask,
    node_window_halfspan,
):
    pert = member_perturbations[0]
    node_total = ROWS * lax.axis_size(NODE)
    core = lax.axis_index("c")
    member = lax.axis_index(MEMBER)
    place = jnp.stack([core, lax.axis_index(NODE) * ROWS, jnp.int32(node_total)]).astype(jnp.int32)

    packed = jnp.concatenate(
        [
            query_key_value_weight,
            jnp.concatenate([output_weight_matrix[:, :INNER], output_weight_matrix[:, INNER:]], axis=0),
        ],
        axis=1,
    )
    with jax.named_scope("weights_over_node"):
        mine = lax.ppermute(packed, EVERY, weight_route())
    with jax.named_scope("latent_halo"):
        shared = jnp.concatenate(
            [latent.T, jnp.pad(node_window_halfspan.astype(bf16)[None], ((0, 15), (0, 0)))], axis=0
        )
        shared_low, shared_high = both_ways(shared)
        extended = jnp.concatenate([shared_low, shared, shared_high], axis=1)
        reach_row = extended[HEAD : HEAD + 8].astype(jnp.int32)
    with jax.named_scope("perturbation_halo"):
        pert_low, pert_high = both_ways(pert)
    with jax.named_scope("latent_over_member"):
        latent_turned = lax.all_gather(extended[:HEAD], MEMBER, axis=0, tiled=True)
    with jax.named_scope("weights_over_member"):
        wa = lax.all_to_all(
            jnp.broadcast_to(mine[None], (16,) + mine.shape), ("y", "xl", "xh"), 0, 0, tiled=True
        )
    with jax.named_scope("weights_over_core"):
        wb = lax.ppermute(wa, "c", [(0, 1), (1, 0)])

    reach_column = node_window_halfspan[:, None]
    decoder = jnp.pad(decoder_weight_matrix, ((0, LANES - VARS), (0, 0)))
    truth = lax.dynamic_slice_in_dim(observed_truth, member * SLOT, SLOT, 1)
    truth = jnp.pad(truth.T, ((0, 0), (0, LANES - VARS)))
    mask = lax.dynamic_slice_in_dim(region_mask, member * SLOT, SLOT, 0)
    area = (1.0 - (1.0 - region_share) * mask.astype(f32))[:, None]
    gain = layer_norm_gain[None]

    with jax.named_scope("layer_norm"):
        normed, latent_own = call(
            norm_kernel,
            [((EXT, WIDTH), bf16), ((ROWS, WIDTH), bf16)],
            [],
            1_000_000_000,
            latent_turned, pert_low, pert, pert_high, gain,
        )
    with jax.named_scope("forward"):
        q, k, v, unit, factor, mixed, total, forecast = call(
            forward_kernel,
            [((EXT, INNER), bf16)] * 3
            + [((ROWS, WIDTH), f32)] * 2
            + [((ROWS, INNER), f32)] * 2
            + [((ROWS, LANES), f32)],
            [((2, TILE, WINDOW), f32), ((ROWS, INNER), bf16)],
            4_000_000_000,
            place, normed, wa, wb, latent_own, pert, reach_column, decoder,
        )
    with jax.named_scope("forecasts_over_member"):
        forecasts = lax.all_to_all(
            forecast.reshape(MEMBERS, SLOT, LANES), MEMBER, 0, 0, tiled=True
        )
    with jax.named_scope("score"):
        (pred_grads,) = call(
            score_kernel, [((MEMBERS, SLOT, LANES), bf16)], [], 10_000_000, forecasts, truth, area
        )
    with jax.named_scope("gradients_over_member"):
        pred_grad = lax.all_to_all(pred_grads, MEMBER, 0, 0, tiled=True).reshape(ROWS, LANES)
    with jax.named_scope("upstream"):
        upd, scaled, g0, g1, message, loss_part = call(
            upstream_kernel,
            [((ROWS, WIDTH), f32)] + [((ROWS, INNER), bf16)] * 3 + [((ROWS, LANES), bf16), ((8, LANES), f32)],
            [((ROWS, INNER), f32)],
            500_000_000,
            place, pred_grad, decoder, wa, wb, mixed, total,
        )
    with jax.named_scope("gradient_halo"):
        message_low, message_high = both_ways(message)
    with jax.named_scope("loss_over_node"):
        loss_a = lax.ppermute(loss_part, EVERY, loss_route(0))
        loss_b = lax.ppermute(loss_part, EVERY, loss_route(1))
    with jax.named_scope("query_gradients"):
        (qgrad,) = call(
            query_kernel,
            [((ROWS, INNER), f32)],
            [((2, TILE, WINDOW), f32)],
            4_000_000_000,
            place, q, k, v, g0, g1, reach_column,
        )
    with jax.named_scope("backward"):
        noise, send = call(
            backward_kernel,
            [((ROWS, WIDTH), f32), ((MEMBERS, HEAD + 16, ROWS), bf16)],
            [((EXT, INNER), bf16)] * 3
            + [((2, TILE, WINDOW), f32), ((ROWS, INNER), f32), ((ROWS, WIDTH), f32), ((ROWS, WIDTH), f32)],
            4_000_000_000,
            place, message_low, message_high, decoder, wa, wb, q, k, v, scaled, g0, g1, reach_row,
            qgrad, unit, factor, latent_own, pert, gain, upd, loss_a, loss_b,
        )
    with jax.named_scope("latent_gradient_over_member"):
        received = lax.all_to_all(send, MEMBER, 0, 0, tiled=True)
    with jax.named_scope("finish"):
        latent_grad, loss = call(
            finish_kernel, [((HEAD, ROWS), f32), ((8, LANES), f32)], [], 10_000_000, received
        )
    loss = loss[0, 0] / (MEMBERS * node_total * VARS)
    return (loss, latent_grad.T, noise[None])


def solution(mesh):
    fine = Mesh(mesh.devices.reshape(4, 2, 2, 16, 2), EVERY)
    placed = (
        P(NODE, MEMBER),
        P(MEMBER, NODE, None),
        P(),
        P(NODE, None),
        P(NODE, None),
        P(),
        P(None, NODE),
        P(NODE),
        P(NODE),
    )
    return jax.shard_map(
        shards,
        mesh=fine,
        in_specs=placed,
        out_specs=(P(), P(NODE, MEMBER), P(MEMBER, NODE, None)),
        check_vma=False,
    )
```

time: 617 us -> 235 us (0.38)
  waiting for transfers between devices: 337 us -> 66.4 us
  blocking collectives: 132 us -> 27.5 us
  matrix products: 75.3 us -> 0 us
  starting transfers between devices: 12.8 us -> 70.2 us
  Pallas kernels: 0 us -> 36.2 us
  other arithmetic: 14.7 us -> 1.8 us
  local copies, waits for them, and re-layouts: 26 us -> 15.5 us
    all_gather x3 -> x1, waiting for transfers between devices: 282 us -> 10.1 us  [shards(): latent_turned = lax.all_gather(extended[:HEAD], MEMBER, axis=0, tiled=True)]
    psum x1 -> x0, blocking collectives: 106 us -> none  [shards(): score = lax.psum(incomplete_crps_sum, ('member', 'node'))]
    dot_general x61 -> x0, matrix products: 75.3 us -> none  [the longest x27 40.6 us: contract_trailing_axis(): lax.dot_general(left, right, (((1,), (1,)), ((), ())), preferred_element_...]
    ppermute x4 -> x10, starting transfers between devices: 12.7 us -> 49.9 us  [the longest x3 17.5 us: both_ways(): low = lax.ppermute(block, NODE, [(i, i + 1) for i in range(count - 1)])]
    pallas_call x0 -> x7, Pallas kernels: none -> 36.2 us  [call(): pl.pallas_call(body, out_shape=tuple((jax.ShapeDtypeStruct(shape, kind) f...]
    all_to_all x0 -> x1, blocking collectives: none -> 27.5 us  [shards(): received = lax.all_to_all(send, MEMBER, 0, 0, tiled=True)]
    all_gather x1 -> x0, blocking collectives: 25.9 us -> none  [shards(): shared = lax.all_gather(latent, 'member', axis=1, tiled=True)]
    all_to_all x0 -> x3, starting transfers between devices: none -> 20.3 us  [the longest x1 11.5 us: shards(): lax.all_to_all(jnp.broadcast_to(mine[None], (16,) + mine.shape), ('y', 'x...]
  transfers between devices with their start and end apart: 8 -> 14, of which waited for: 6 -> 7; matrix products, arithmetic and copies ran while one was open for 3% -> 2% of each run, Pallas kernels for 0% -> 3%
where the time goes in v1:
time: 235 us; the launch traced here: 234 us
  starting transfers between devices  70.2 us (30%)
  waiting for transfers between devices  66.4 us (28%)
  Pallas kernels  36.2 us (15%)
  blocking collectives  27.5 us (12%)
  between operations  16.2 us (7%)
  local copies, waits for them, and re-layouts  15.5 us (7%)
    pallas_call x7, Pallas kernels, call(): pl.pallas_call(body, out_shape=tuple((jax.ShapeDtypeStruct(shape, kind) f...  36.2 us
    all_to_all x1, blocking collectives, shards(): received = lax.all_to_all(send, MEMBER, 0, 0, tiled=True)  27.5 us
    ppermute x3, waiting for transfers between devices, both_ways(): high = lax.ppermute(block, NODE, [(i + 1, i) for i in range(count - 1)])  26.6 us
    ppermute x3, starting transfers between devices, both_ways(): low = lax.ppermute(block, NODE, [(i, i + 1) for i in range(count - 1)])  17.5 us
    ppermute x3, waiting for transfers between devices, both_ways(): low = lax.ppermute(block, NODE, [(i, i + 1) for i in range(count - 1)])  16.9 us
    ppermute x1, starting transfers between devices, shards(): mine = lax.ppermute(packed, EVERY, weight_route())  16.8 us
    all_to_all x1, starting transfers between devices, shards(): lax.all_to_all(jnp.broadcast_to(mine[None], (16,) + mine.shape), ('y', 'x...  11.5 us
    all_gather x1, waiting for transfers between devices, shards(): latent_turned = lax.all_gather(extended[:HEAD], MEMBER, axis=0, tiled=True)  10.1 us
  transfers between devices with their start and end apart: 14, of which 7 were waited for; matrix products, arithmetic and copies ran while one was open for 2% of the time, Pallas kernels for 3%

profile of v1, /device:TPU:1, one launch (start us, length us, event | category | flops | bytes accessed | tf_op | source)
XLA Modules:
  0.0 233.7 jit_solution(10265528600650215165)
XLA Ops:
  7.2 0.0 copy-start
  7.2 0.8 fusion
  8.0 0.9 maximum_maximum_fusion
  8.9 16.8 %collective-permute-start.4 = (bf16[32,2048]{1,0:T(8,128)(2,1)S(1)}, bf16[32,2048]{1,0:T(8,128)(2,1)S(1)}, u32[]{:S(2)}, u32[]{:S(2)}) collective-permute-start(bf16[32,2048]{1,0:T(8,128)(2,1)S(1)} %maximum_maximum_fusion), channel_id=1, source_target_pairs={{0,0},{1,1},{64,2},{65,3},{128,4},{129,5},{192,6},{193,7},{256,8},... | collective-permute-start | bytes 393224 | tf_op jit(solution)/shard_map/weights_over_node/ppermute | solution.py:486
  25.7 3.0 %collective-permute-done.4 = bf16[32,2048]{1,0:T(8,128)(2,1)S(1)} collective-permute-done((bf16[32,2048]{1,0:T(8,128)(2,1)S(1)}, bf16[32,2048]{1,0:T(8,128)(2,1)S(1)}, u32[]{:S(2)}, u32[]{:S(2)}) %collective-permute-start.4) | collective-permute-done | bytes 131104 | tf_op jit(solution)/shard_map/weights_over_node/ppermute | solution.py:486
  28.7 1.6 broadcast_in_dim.23
  30.3 11.5 %all-to-all-start = ((bf16[16,32,2048]{2,1,0:T(8,128)(2,1)}), bf16[16,32,2048]{2,1,0:T(8,128)(2,1)S(1)}, u32[]{:S(2)}, u32[]{:S(2)}) async-start(bf16[16,32,2048]{2,1,0:T(8,128)(2,1)} %broadcast_in_dim.23), calls=%async_computation | async-start | bytes 4194304 | tf_op jit(solution)/shard_map/weights_over_member/all_to_all | solution.py:499
  41.8 0.0 all-gather.2.cloned.1.call-start
  42.0 1.3 collective-permute-start.1
  43.3 5.5 %collective-permute-start = (bf16[80,256]{1,0:T(8,128)(2,1)S(1)}, bf16[80,256]{1,0:T(8,128)(2,1)S(1)}, u32[]{:S(2)}, u32[]{:S(2)}) collective-permute-start(bf16[80,256]{1,0:T(8,128)(2,1)S(1)} %pad_maximum_fusion.1), channel_id=1, source_target_pairs={{0,1},{1,2},{2,3},{3,4},{4,5},{5,6},{6,7},{7,8},{8,9},{9,10},{10,1... | collective-permute-start | bytes 122888 | tf_op jit(solution)/shard_map/latent_halo/ppermute | solution.py:424
  48.8 19.6 %collective-permute-done.1 = bf16[80,256]{1,0:T(8,128)(2,1)S(1)} collective-permute-done((bf16[80,256]{1,0:T(8,128)(2,1)S(1)}, bf16[80,256]{1,0:T(8,128)(2,1)S(1)}, u32[]{:S(2)}, u32[]{:S(2)}) %collective-permute-start.1) | collective-permute-done | bytes 40992 | tf_op jit(solution)/shard_map/latent_halo/ppermute | solution.py:425
  68.4 0.0 collective-permute-done
  68.4 0.7 slice.20
  69.0 0.0 all-gather.2.cloned.1.call-update
  69.1 0.0 all-to-all-done.wa_ref
  69.1 1.9 collective-permute-start.5
  71.0 1.3 collective-permute-start.3
  72.3 6.3 %collective-permute-start.2 = (bf16[256,1024]{1,0:T(8,128)(2,1)S(1)}, bf16[256,1024]{1,0:T(8,128)(2,1)}, u32[]{:S(2)}, u32[]{:S(2)}) collective-permute-start(bf16[256,1024]{1,0:T(8,128)(2,1)S(1)} %bitcast.15), channel_id=1, source_target_pairs={{0,1},{1,2},{2,3},{3,4},{4,5},{5,6},{6,7},{7,8},{8,9},{9,10},{10,1... | collective-permute-start | bytes 1572872 | tf_op jit(solution)/shard_map/perturbation_halo/ppermute | solution.py:424
  78.6 0.8 copy.14.reach_ref
  79.4 1.0 pad.13.decoder_ref
  80.4 0.1 pad_add_fusion.place_ref
  80.5 6.9 %collective-permute-done.3.high_ref = bf16[256,1024]{1,0:T(8,128)(2,1)S(1)} collective-permute-done((bf16[256,1024]{1,0:T(8,128)(2,1)S(1)}, bf16[256,1024]{1,0:T(8,128)(2,1)S(1)}, u32[]{:S(2)}, u32[]{:S(2)}) %collective-permute-start.3) | collective-permute-done | bytes 524320 | tf_op jit(solution)/shard_map/perturbation_halo/ppermute | solution.py:425
  87.4 16.9 %collective-permute-done.2.low_ref = bf16[256,1024]{1,0:T(8,128)(2,1)} collective-permute-done((bf16[256,1024]{1,0:T(8,128)(2,1)S(1)}, bf16[256,1024]{1,0:T(8,128)(2,1)}, u32[]{:S(2)}, u32[]{:S(2)}) %collective-permute-start.2) | collective-permute-done | bytes 524320 | tf_op jit(solution)/shard_map/perturbation_halo/ppermute | solution.py:424
  104.3 10.1 %all-gather.2.cloned.1.call-done.lat_ref = bf16[1024,768]{1,0:T(8,128)(2,1)} async-done(((bf16[64,768]{1,0:T(8,128)(2,1)}), bf16[1024,768]{1,0:T(8,128)(2,1)}) %all-gather.2.cloned.1.call-update) | async-done | bytes 1572880 | tf_op jit(solution)/shard_map/latent_over_member/all_gather | solution.py:497
  114.4 1.4 copy-done.5
  115.8 2.6 %layer_norm.1 = (bf16[768,1024]{1,0:T(8,128)(2,1)S(1)}, bf16[256,1024]{1,0:T(8,128)(2,1)S(1)}) custom-call(bf16[1024,768]{1,0:T(8,128)(2,1)S(1)} %copy-done.5, bf16[256,1024]{1,0:T(8,128)(2,1)} %collective-permute-done.2.low_ref, bf16[256,1024]{1,0:T(8,128)(2,1)S(1)} %bitcast.16, bf16[256,1024]{1,0:T(8,128)(2,1)S(1)} %collective-permute-done.3.high_ref, ...), custom_call_target="tpu_custom_call" | custom-call | flops 1000000000 | bytes 4000000 | tf_op jit(solution)/shard_map/layer_norm/pallas_call | solution.py:410
  118.4 0.0 collective-permute-done.5.wb_ref
  118.4 0.0 copy-start.7
  118.4 1.2 copy-done.7
  119.6 11.7 %forward.1 = (bf16[768,512]{1,0:T(8,128)(2,1)S(1)}, bf16[768,512]{1,0:T(8,128)(2,1)S(1)}, bf16[768,512]{1,0:T(8,128)(2,1)S(1)}, f32[256,1024]{1,0:T(8,128)S(1)},...) custom-call(s32[3]{0:T(128)S(1)} %pad_add_fusion.place_ref, ...), custom_call_target="tpu_custom_call" | custom-call | flops 4000000000 | bytes 4000000 | tf_op jit(solution)/shard_map/forward/pallas_call | solution.py:410
  131.3 0.6 copy-done.4
  132.0 1.0 copy-done.11
  132.9 1.0 copy-done.13
  133.9 0.9 copy-done.15
  134.8 0.9 copy-done.17
  135.7 0.9 copy-done.19
  136.6 4.3 %all-to-all-start.1 = ((f32[16,16,128]{2,1,0:T(8,128)}), f32[16,16,128]{2,1,0:T(8,128)}, u32[]{:S(2)}, u32[]{:S(2)}) async-start(f32[16,16,128]{2,1,0:T(8,128)} %bitcast.13), calls=%async_computation.1 | async-start | bytes 262144 | tf_op jit(solution)/shard_map/forecasts_over_member/all_to_all | solution.py:533
  140.8 0.1 subtract_bitcast_fusion
  140.9 0.1 copy.16.area_ref
  141.0 0.7 constant_dynamic-slice_fusion
  141.7 0.9 copy.18
  142.6 4.5 %all-to-all-done.1.forecast_ref = f32[16,16,128]{2,1,0:T(8,128)} async-done(((f32[16,16,128]{2,1,0:T(8,128)}), f32[16,16,128]{2,1,0:T(8,128)}, u32[]{:S(2)}, u32[]{:S(2)}) %all-to-all-start.1) | async-done | bytes 131104 | tf_op jit(solution)/shard_map/forecasts_over_member/all_to_all | solution.py:533
  147.1 1.6 score.1
  148.6 0.0 copy-start.1
  148.7 0.6 copy-done.1
  149.3 4.5 %all-to-all-start.2 = ((bf16[16,16,128]{2,1,0:T(8,128)(2,1)}), bf16[16,16,128]{2,1,0:T(8,128)(2,1)}, u32[]{:S(2)}, u32[]{:S(2)}) async-start(bf16[16,16,128]{2,1,0:T(8,128)(2,1)} %copy-done.1), calls=%async_computation.2 | async-start | bytes 131072 | tf_op jit(solution)/shard_map/gradients_over_member/all_to_all | solution.py:541
  153.8 0.7 maximum_convert_fusion.reach_ref
  154.5 5.3 %all-to-all-done.2 = bf16[16,16,128]{2,1,0:T(8,128)(2,1)} async-done(((bf16[16,16,128]{2,1,0:T(8,128)(2,1)}), bf16[16,16,128]{2,1,0:T(8,128)(2,1)}, u32[]{:S(2)}, u32[]{:S(2)}) %all-to-all-start.2) | async-done | bytes 65568 | tf_op jit(solution)/shard_map/gradients_over_member/all_to_all | solution.py:541
  159.8 3.3 %upstream.1 = (f32[256,1024]{1,0:T(8,128)S(1)}, bf16[256,512]{1,0:T(8,128)(2,1)S(1)}, bf16[256,512]{1,0:T(8,128)(2,1)S(1)}, bf16[256,512]{1,0:T(8,128)(2,1)S(1)}...) custom-call(s32[3]{0:T(128)S(1)} %pad_add_fusion.place_ref, bf16[256,128]{1,0:T(8,128)(2,1)} %bitcast.8.pg_ref, ...), custom_call_target="tpu_custom_call" | custom-call | flops 500000000 | bytes 4000000 | tf_op jit(solution)/shard_map/upstream/pallas_call | solution.py:410
  163.1 6.4 %collective-permute-start.9 = (f32[8,128]{1,0:T(8,128)S(1)}, f32[8,128]{1,0:T(8,128)S(1)}, u32[]{:S(2)}, u32[]{:S(2)}) collective-permute-start(f32[8,128]{1,0:T(8,128)S(1)} %get-tuple-element.38), channel_id=1, source_target_pairs={{0,1},{1,2},{2,3},{3,4},{4,5},{5,6},{6,7},{7,8},{8,9},{9,10},{10,1... | collective-permute-start | bytes 12296 | tf_op jit(solution)/shard_map/loss_over_node/ppermute | solution.py:554
  169.5 3.4 %collective-permute-start.8 = (f32[8,128]{1,0:T(8,128)S(1)}, f32[8,128]{1,0:T(8,128)S(1)}, u32[]{:S(2)}, u32[]{:S(2)}) collective-permute-start(f32[8,128]{1,0:T(8,128)S(1)} %get-tuple-element.38), channel_id=1, source_target_pairs={{0,0},{1,1},{2,2},{3,3},{4,4},{5,5},{6,6},{7,7},{8,8},{9,9},{10,10... | collective-permute-start | bytes 12296 | tf_op jit(solution)/shard_map/loss_over_node/ppermute | solution.py:553
  172.9 1.3 collective-permute-start.7
  174.2 5.7 %collective-permute-start.6 = (bf16[256,128]{1,0:T(8,128)(2,1)S(1)}, bf16[256,128]{1,0:T(8,128)(2,1)S(1)}, u32[]{:S(2)}, u32[]{:S(2)}) collective-permute-start(bf16[256,128]{1,0:T(8,128)(2,1)S(1)} %get-tuple-element.28), channel_id=1, source_target_pairs={{0,1},{1,2},{2,3},{3,4},{4,5},{5,6},{6,7},{7,8},{8,9},{9,10},{10,1... | collective-permute-start | bytes 196616 | tf_op jit(solution)/shard_map/gradient_halo/ppermute | solution.py:424
  179.9 0.0 copy-start.8
  179.9 0.0 copy-start.12
  180.0 5.2 %query_gradients.1.qgrad_ref = f32[256,512]{1,0:T(8,128)S(1)} custom-call(s32[3]{0:T(128)S(1)} %pad_add_fusion.place_ref, bf16[768,512]{1,0:T(8,128)(2,1)S(1)} %copy-done.16, bf16[768,512]{1,0:T(8,128)(2,1)S(1)} %copy-done.18, bf16[768,512]{1,0:T(8,128)(2,1)S(1)} %copy-done.20, bf16[256,512]{1,0:T(8,128)(2,1)S(1)} %get-tuple-element.33.g0_ref, ...), custom_call_target="tpu_custom_call" | custom-call | flops 4000000000 | bytes 4000000 | tf_op jit(solution)/shard_map/query_gradients/pallas_call | solution.py:410
  185.2 0.0 collective-permute-done.9.loss_b_ref
  185.2 0.0 collective-permute-done.8.loss_a_ref
  185.2 0.0 collective-permute-done.7.high_ref
  185.2 0.0 collective-permute-done.6.low_ref
  185.3 11.2 %backward.1 = (f32[256,1024]{1,0:T(8,128)}, bf16[16,80,256]{2,1,0:T(8,128)(2,1)S(1)}) custom-call(s32[3]{0:T(128)S(1)} %pad_add_fusion.place_ref, bf16[256,128]{1,0:T(8,128)(2,1)S(1)} %collective-permute-done.6.low_ref, bf16[256,128]{1,0:T(8,128)(2,1)S(1)} %collective-permute-done.7.high_ref, bf16[128,1024]{1,0:T(8,128)(2,1)S(1)} %pad.13.decoder_ref, ...), custom_call_target="tpu_custom_call" | custom-call | flops 4000000000 | bytes 4000000 | tf_op jit(solution)/shard_map/backward/pallas_call | solution.py:410
  196.4 27.5 %all_to_all.20.received_ref = bf16[16,80,256]{2,1,0:T(8,128)(2,1)S(1)} all-to-all(bf16[16,80,256]{2,1,0:T(8,128)(2,1)S(1)} %get-tuple-element.39), channel_id=1, replica_groups=mesh['y'=4,'xl'=2,'c'=2,'z'=16,'xh'=2] {'y','xl','c'}, dimensions={0} | all-to-all | bytes 1310720 | tf_op jit(solution)/shard_map/latent_gradient_over_member/all_to_all | solution.py:574
  223.9 0.7 finish.1
  224.6 0.5 slice.19
  (47 shorter events, 0.1 us)
Async XLA Ops:
  7.2 133.8 %copy-start = (f32[98,256]{1,0:T(8,128)S(1)}, f32[98,256]{1,0:T(8,128)}, u32[]{:S(2)}) copy-start(f32[98,256]{1,0:T(8,128)} %param.15) | copy-start | bytes 301060
  8.9 19.9 %collective-permute-start.4 = (bf16[32,2048]{1,0:T(8,128)(2,1)S(1)}, bf16[32,2048]{1,0:T(8,128)(2,1)S(1)}, u32[]{:S(2)}, u32[]{:S(2)}) collective-permute-start(bf16[32,2048]{1,0:T(8,128)(2,1)S(1)} %maximum_maximum_fusion), channel_id=1, source_target_pairs={{0,0},{1,1},{64,2},{65,3},{128,4},{129,5},{192,6},{193,7},{256,8},... | collective-permute-start | bytes 393224 | tf_op jit(solution)/shard_map/weights_over_node/ppermute | solution.py:486
  30.3 11.5 %copy-start.25 = (s32[256]{0:T(256)S(1)}, s32[256]{0:T(256)}, u32[]{:S(2)}) copy-start(s32[256]{0:T(256)} %param.17) | copy-start | bytes 3076
  30.3 11.6 %copy-start.21 = (bf16[256,64]{0,1:T(8,128)(2,1)S(1)}, bf16[256,64]{0,1:T(8,128)(2,1)}, u32[]{:S(2)}) copy-start(bf16[256,64]{0,1:T(8,128)(2,1)} %param.9) | copy-start | bytes 98308
  30.3 40.7 %copy-start.6 = (bf16[1,256,1024]{2,1,0:T(8,128)(2,1)S(1)}, bf16[1,256,1024]{2,1,0:T(8,128)(2,1)}, u32[]{:S(2)}) copy-start(bf16[1,256,1024]{2,1,0:T(8,128)(2,1)} %param.10) | copy-start | bytes 1572868
  30.3 48.3 %copy-start.24 = (bf16[1024]{0:T(1024)(128)(2,1)S(1)}, bf16[1024]{0:T(1024)(128)(2,1)}, u32[]{:S(2)}) copy-start(bf16[1024]{0:T(1024)(128)(2,1)} %param.11) | copy-start | bytes 6148
  30.3 38.7 %all-to-all-start = ((bf16[16,32,2048]{2,1,0:T(8,128)(2,1)}), bf16[16,32,2048]{2,1,0:T(8,128)(2,1)S(1)}, u32[]{:S(2)}, u32[]{:S(2)}) async-start(bf16[16,32,2048]{2,1,0:T(8,128)(2,1)} %broadcast_in_dim.23), calls=%async_computation | async-start | bytes 4194304 | tf_op jit(solution)/shard_map/weights_over_member/all_to_all | solution.py:499
  41.8 72.5 %all-gather.2.cloned.1.call-start = ((), (), s32[]{:S(2)}) async-start(), calls=%async_computation.4 | async-start | bytes 1671168 | tf_op jit(solution)/shard_map/latent_over_member/all_gather | solution.py:497
  42.0 26.4 %collective-permute-start.1 = (bf16[80,256]{1,0:T(8,128)(2,1)S(1)}, bf16[80,256]{1,0:T(8,128)(2,1)S(1)}, u32[]{:S(2)}, u32[]{:S(2)}) collective-permute-start(bf16[80,256]{1,0:T(8,128)(2,1)S(1)} %pad_maximum_fusion.1), channel_id=1, source_target_pairs={{1,0},{2,1},{3,2},{4,3},{5,4},{6,5},{7,6},{8,7},{9,8},{10,9},{11,1... | collective-permute-start | bytes 122888 | tf_op jit(solution)/shard_map/latent_halo/ppermute | solution.py:425
  43.3 25.1 %collective-permute-start = (bf16[80,256]{1,0:T(8,128)(2,1)S(1)}, bf16[80,256]{1,0:T(8,128)(2,1)S(1)}, u32[]{:S(2)}, u32[]{:S(2)}) collective-permute-start(bf16[80,256]{1,0:T(8,128)(2,1)S(1)} %pad_maximum_fusion.1), channel_id=1, source_target_pairs={{0,1},{1,2},{2,3},{3,4},{4,5},{5,6},{6,7},{7,8},{8,9},{9,10},{10,1... | collective-permute-start | bytes 122888 | tf_op jit(solution)/shard_map/latent_halo/ppermute | solution.py:424
  68.4 10.3 %copy-start.22 = (bf16[80,256]{1,0:T(8,128)(2,1)}, bf16[80,256]{1,0:T(8,128)(2,1)S(1)}, u32[]{:S(2)}) copy-start(bf16[80,256]{1,0:T(8,128)(2,1)S(1)} %collective-permute-done.1) | copy-start | bytes 122884
  68.4 10.3 %copy-start.23 = (bf16[80,256]{1,0:T(8,128)(2,1)}, bf16[80,256]{1,0:T(8,128)(2,1)S(1)}, u32[]{:S(2)}) copy-start(bf16[80,256]{1,0:T(8,128)(2,1)S(1)} %collective-permute-done) | copy-start | bytes 122884
  69.1 49.3 %collective-permute-start.5 = (bf16[16,32,2048]{2,1,0:T(8,128)(2,1)S(1)}, bf16[16,32,2048]{2,1,0:T(8,128)(2,1)}, u32[]{:S(2)}, u32[]{:S(2)}) collective-permute-start(bf16[16,32,2048]{2,1,0:T(8,128)(2,1)S(1)} %all-to-all-done.wa_ref), channel_id=1, source_target_pairs={{0,32},{32,0},{1,33},{33,1},{2,34},{34,2},{3,35},{35,3},{4,36},{36... | collective-permute-start | bytes 6291464 | tf_op jit(solution)/shard_map/weights_over_core/ppermute | solution.py:503
  71.0 16.4 %collective-permute-start.3 = (bf16[256,1024]{1,0:T(8,128)(2,1)S(1)}, bf16[256,1024]{1,0:T(8,128)(2,1)S(1)}, u32[]{:S(2)}, u32[]{:S(2)}) collective-permute-start(bf16[256,1024]{1,0:T(8,128)(2,1)S(1)} %bitcast.14), channel_id=1, source_target_pairs={{1,0},{2,1},{3,2},{4,3},{5,4},{6,5},{7,6},{8,7},{9,8},{10,9},{11,1... | collective-permute-start | bytes 1572872 | tf_op jit(solution)/shard_map/perturbation_halo/ppermute | solution.py:425
  72.3 32.0 %collective-permute-start.2 = (bf16[256,1024]{1,0:T(8,128)(2,1)S(1)}, bf16[256,1024]{1,0:T(8,128)(2,1)}, u32[]{:S(2)}, u32[]{:S(2)}) collective-permute-start(bf16[256,1024]{1,0:T(8,128)(2,1)S(1)} %bitcast.15), channel_id=1, source_target_pairs={{0,1},{1,2},{2,3},{3,4},{4,5},{5,6},{6,7},{7,8},{8,9},{9,10},{10,1... | collective-permute-start | bytes 1572872 | tf_op jit(solution)/shard_map/perturbation_halo/ppermute | solution.py:424
  114.4 1.4 copy-start.5
  115.8 2.6 %copy-start.2 = (s32[256,1]{1,0:T(8,128)S(1)}, s32[256,1]{1,0:T(8,128)}, u32[]{:S(2)}) copy-start(s32[256,1]{1,0:T(8,128)} %copy.14.reach_ref) | copy-start | bytes 3076
  118.4 13.0 %copy-start.9 = (bf16[256,1024]{1,0:T(8,128)(2,1)}, bf16[256,1024]{1,0:T(8,128)(2,1)S(1)}, u32[]{:S(2)}) copy-start(bf16[256,1024]{1,0:T(8,128)(2,1)S(1)} %get-tuple-element.24.latent_ref) | copy-start | bytes 1572868
  118.4 1.2 copy-start.7
  119.6 21.2 %copy-start.26 = (s32[256]{0:T(256)S(1)}, s32[256]{0:T(256)}, u32[]{:S(2)}) copy-start(s32[256]{0:T(256)} %param.16) | copy-start | bytes 3076
  131.3 0.6 copy-start.4
  132.0 1.0 copy-start.11
  132.9 1.0 copy-start.13
  133.9 0.9 copy-start.15
  134.8 0.9 copy-start.17
  135.7 0.9 copy-start.19
  136.6 10.5 %all-to-all-start.1 = ((f32[16,16,128]{2,1,0:T(8,128)}), f32[16,16,128]{2,1,0:T(8,128)}, u32[]{:S(2)}, u32[]{:S(2)}) async-start(f32[16,16,128]{2,1,0:T(8,128)} %bitcast.13), calls=%async_computation.1 | async-start | bytes 262144 | tf_op jit(solution)/shard_map/forecasts_over_member/all_to_all | solution.py:533
  148.6 0.6 copy-start.1
  149.3 10.5 %all-to-all-start.2 = ((bf16[16,16,128]{2,1,0:T(8,128)(2,1)}), bf16[16,16,128]{2,1,0:T(8,128)(2,1)}, u32[]{:S(2)}, u32[]{:S(2)}) async-start(bf16[16,16,128]{2,1,0:T(8,128)(2,1)} %copy-done.1), calls=%async_computation.2 | async-start | bytes 131072 | tf_op jit(solution)/shard_map/gradients_over_member/all_to_all | solution.py:541
  159.8 20.1 %copy-start.3 = (s32[256,1]{1,0:T(8,128)S(1)}, s32[256,1]{1,0:T(8,128)}, u32[]{:S(2)}) copy-start(s32[256,1]{1,0:T(8,128)} %copy.14.reach_ref) | copy-start | bytes 3076
  159.8 20.1 %copy-start.16 = (bf16[768,512]{1,0:T(8,128)(2,1)S(1)}, bf16[768,512]{1,0:T(8,128)(2,1)}, u32[]{:S(2)}) copy-start(bf16[768,512]{1,0:T(8,128)(2,1)} %copy-done.15) | copy-start | bytes 2359300
  159.8 20.1 %copy-start.18 = (bf16[768,512]{1,0:T(8,128)(2,1)S(1)}, bf16[768,512]{1,0:T(8,128)(2,1)}, u32[]{:S(2)}) copy-start(bf16[768,512]{1,0:T(8,128)(2,1)} %copy-done.17) | copy-start | bytes 2359300
  159.8 20.1 %copy-start.20 = (bf16[768,512]{1,0:T(8,128)(2,1)S(1)}, bf16[768,512]{1,0:T(8,128)(2,1)}, u32[]{:S(2)}) copy-start(bf16[768,512]{1,0:T(8,128)(2,1)} %copy-done.19) | copy-start | bytes 2359300
  163.1 22.1 %collective-permute-start.9 = (f32[8,128]{1,0:T(8,128)S(1)}, f32[8,128]{1,0:T(8,128)S(1)}, u32[]{:S(2)}, u32[]{:S(2)}) collective-permute-start(f32[8,128]{1,0:T(8,128)S(1)} %get-tuple-element.38), channel_id=1, source_target_pairs={{0,1},{1,2},{2,3},{3,4},{4,5},{5,6},{6,7},{7,8},{8,9},{9,10},{10,1... | collective-permute-start | bytes 12296 | tf_op jit(solution)/shard_map/loss_over_node/ppermute | solution.py:554
  169.5 15.7 %collective-permute-start.8 = (f32[8,128]{1,0:T(8,128)S(1)}, f32[8,128]{1,0:T(8,128)S(1)}, u32[]{:S(2)}, u32[]{:S(2)}) collective-permute-start(f32[8,128]{1,0:T(8,128)S(1)} %get-tuple-element.38), channel_id=1, source_target_pairs={{0,0},{1,1},{2,2},{3,3},{4,4},{5,5},{6,6},{7,7},{8,8},{9,9},{10,10... | collective-permute-start | bytes 12296 | tf_op jit(solution)/shard_map/loss_over_node/ppermute | solution.py:553
  172.9 12.3 %collective-permute-start.7 = (bf16[256,128]{1,0:T(8,128)(2,1)S(1)}, bf16[256,128]{1,0:T(8,128)(2,1)S(1)}, u32[]{:S(2)}, u32[]{:S(2)}) collective-permute-start(bf16[256,128]{1,0:T(8,128)(2,1)S(1)} %get-tuple-element.28), channel_id=1, source_target_pairs={{1,0},{2,1},{3,2},{4,3},{5,4},{6,5},{7,6},{8,7},{9,8},{10,9},{11,1... | collective-permute-start | bytes 196616 | tf_op jit(solution)/shard_map/gradient_halo/ppermute | solution.py:425
  174.2 11.0 %collective-permute-start.6 = (bf16[256,128]{1,0:T(8,128)(2,1)S(1)}, bf16[256,128]{1,0:T(8,128)(2,1)S(1)}, u32[]{:S(2)}, u32[]{:S(2)}) collective-permute-start(bf16[256,128]{1,0:T(8,128)(2,1)S(1)} %get-tuple-element.28), channel_id=1, source_target_pairs={{0,1},{1,2},{2,3},{3,4},{4,5},{5,6},{6,7},{7,8},{8,9},{9,10},{10,1... | collective-permute-start | bytes 196616 | tf_op jit(solution)/shard_map/gradient_halo/ppermute | solution.py:424
  179.9 5.3 %copy-start.8 = (bf16[1,256,1024]{2,1,0:T(8,128)(2,1)S(1)}, bf16[1,256,1024]{2,1,0:T(8,128)(2,1)}, u32[]{:S(2)}) copy-start(bf16[1,256,1024]{2,1,0:T(8,128)(2,1)} %param.10) | copy-start | bytes 1572868
  179.9 5.3 %copy-start.10 = (bf16[256,1024]{1,0:T(8,128)(2,1)S(1)}, bf16[256,1024]{1,0:T(8,128)(2,1)}, u32[]{:S(2)}) copy-start(bf16[256,1024]{1,0:T(8,128)(2,1)} %copy-done.9) | copy-start | bytes 1572868
  179.9 5.3 %copy-start.12 = (f32[256,1024]{1,0:T(8,128)S(1)}, f32[256,1024]{1,0:T(8,128)}, u32[]{:S(2)}) copy-start(f32[256,1024]{1,0:T(8,128)} %copy-done.11) | copy-start | bytes 3145732
  180.0 5.3 %copy-start.14 = (f32[256,1024]{1,0:T(8,128)S(1)}, f32[256,1024]{1,0:T(8,128)}, u32[]{:S(2)}) copy-start(f32[256,1024]{1,0:T(8,128)} %copy-done.13) | copy-start | bytes 3145732
Sparse Core Ops, SparseCore 0:
  69.2 45.1 all-gather.1

commit v2 on v1

--- a/solution.py
+++ b/solution.py
@@ -21,6 +21,9 @@
 SLOT = ROWS // MEMBERS
 TILE = 128
 WINDOW = TILE + 2 * HALF
+LOSS_LANE = 122
+REACH_LANE = 125
+BLOCK = 256
 PACKED = 2048
 
 norm_epsilon = 1e-05
@@ -51,33 +54,34 @@
 
 
 def segment_matrix(scale):
-    rows = lax.broadcasted_iota(jnp.int32, (INNER, INNER), 0) // HEAD
-    columns = lax.broadcasted_iota(jnp.int32, (INNER, INNER), 1) // HEAD
+    rows = lax.broadcasted_iota(jnp.int32, (BLOCK, BLOCK), 0) // HEAD
+    columns = lax.broadcasted_iota(jnp.int32, (BLOCK, BLOCK), 1) // HEAD
     return jnp.where(rows == columns, scale, 0.0).astype(bf16)
 
 
 def head_sums(value, segments):
     high, low = split(value)
-    return mm(high, segments) + mm(low, segments)
+    parts = []
+    for start in range(0, INNER, BLOCK):
+        lanes = slice(start, start + BLOCK)
+        parts.append(mm(high[:, lanes], segments) + mm(low[:, lanes], segments))
+    return jnp.concatenate(parts, axis=1)
 
 
 def lane_index(rows, lanes):
     return lax.broadcasted_iota(jnp.int32, (rows, lanes), 1)
 
 
-def norm_kernel(lat_ref, low_ref, own_ref, high_ref, gain_ref, normed_ref, latent_ref):
+def norm_kernel(lat_ref, pert_ref, gain_ref, normed_ref, latent_ref):
     gain = gain_ref[...].astype(f32)
-    for block, pert_ref in enumerate((low_ref, own_ref, high_ref)):
-        for part in range(2):
-            rows = slice(part * TILE, (part + 1) * TILE)
-            lanes = slice(block * ROWS + part * TILE, block * ROWS + (part + 1) * TILE)
-            lat = lat_ref[:, lanes].astype(f32).T
-            if block == 1:
-                latent_ref[rows, :] = lat.astype(bf16)
-            hidden = lat + pert_ref[rows, :].astype(f32)
-            centred = hidden - jnp.mean(hidden, axis=1, keepdims=True)
-            inverse = lax.rsqrt(jnp.mean(centred * centred, axis=1, keepdims=True) + norm_epsilon)
-            normed_ref[lanes, :] = (centred * inverse * gain).astype(bf16)
+    for part in range(2):
+        rows = slice(part * TILE, (part + 1) * TILE)
+        lat = lat_ref[:, rows].astype(f32).T
+        latent_ref[rows, :] = lat.astype(bf16)
+        hidden = lat + pert_ref[rows, :].astype(f32)
+        centred = hidden - jnp.mean(hidden, axis=1, keepdims=True)
+        inverse = lax.rsqrt(jnp.mean(centred * centred, axis=1, keepdims=True) + norm_epsilon)
+        normed_ref[rows, :] = (centred * inverse * gain).astype(bf16)
 
 
 def out_weights(w_ref, side):
@@ -89,19 +93,30 @@
     return w_ref[:, :, part * INNER : (part + 1) * INNER].reshape(INNER, INNER)
 
 
+def core_halves(place_ref, size):
+    core = place_ref[2]
+    return (
+        pl.ds(pl.multiple_of(core * size, size), size),
+        pl.ds(pl.multiple_of((1 - core) * size, size), size),
+    )
+
+
+def column_of(row_ref):
+    row = jnp.broadcast_to(row_ref[...].astype(f32), (LANES, ROWS))
+    return row.T.astype(jnp.int32)
+
+
 def forward_kernel(
-    place_ref, normed_ref, wa_ref, wb_ref, latent_ref, pert_ref, reach_ref, decoder_ref,
+    place_ref, low_ref, own_ref, high_ref, wa_ref, wb_ref, latent_ref, pert_ref, reach_ref, decoder_ref,
     q_ref, k_ref, v_ref, unit_ref, factor_ref, mixed_ref, total_ref, forecast_ref,
     bias_ref, mixed_low_ref,
 ):
-    core = place_ref[0]
-    row_start = place_ref[1]
+    row_start = place_ref[0]
     segments = segment_matrix(1.0 / HEAD)
-    near = pl.ds(pl.multiple_of(core * INNER, INNER), INNER)
-    far = pl.ds(pl.multiple_of((1 - core) * INNER, INNER), INNER)
-    for block in range(3):
+    near, far = core_halves(place_ref, INNER)
+    for block, normed_ref in enumerate((low_ref, own_ref, high_ref)):
         rows = slice(block * ROWS, (block + 1) * ROWS)
-        left, right = normed_ref[rows, near], normed_ref[rows, far]
+        left, right = normed_ref[:, near], normed_ref[:, far]
         for part, out_ref in enumerate((q_ref, k_ref, v_ref)):
             projected = mm(left, qkv_weights(wa_ref, part)) + mm(right, qkv_weights(wb_ref, part))
             if part < 2:
@@ -113,6 +128,7 @@
                 projected = unit
             out_ref[rows, :] = projected.astype(bf16)
 
+    column = column_of(reach_ref)
     for tile in range(2):
         offset = (
             lane_index(TILE, WINDOW)
@@ -120,14 +136,14 @@
             - lax.broadcasted_iota(jnp.int32, (TILE, WINDOW), 0)
         )
         position = row_start - HALF + tile * TILE + lane_index(TILE, WINDOW)
-        reach = reach_ref[tile * TILE : (tile + 1) * TILE, :]
-        inside = (offset >= -reach) & (offset < reach) & (position >= 0) & (position < place_ref[2])
+        reach = column[tile * TILE : (tile + 1) * TILE, 0:1]
+        inside = (offset >= -reach) & (offset < reach) & (position >= 0) & (position < place_ref[1])
         bias_ref[tile] = jnp.where(inside, 0.0, -1e30)
 
     first = lane_index(1, LANES) < HEAD
 
-    def one_pair(pair, carry):
-        lanes = pl.ds(pl.multiple_of(pair * LANES, LANES), LANES)
+    for pair in range(HEADS // 2):
+        lanes = slice(pair * LANES, (pair + 1) * LANES)
         for tile in range(2):
             rows = slice(tile * TILE, (tile + 1) * TILE)
             window = slice(tile * TILE, tile * TILE + WINDOW)
@@ -145,13 +161,9 @@
             mixed_ref[rows, lanes] = mixed
             mixed_low_ref[rows, lanes] = mixed.astype(bf16)
             total_ref[rows, lanes] = total
-        return carry
-
-    lax.fori_loop(0, HEADS // 2, one_pair, 0)
-
-    near_out = pl.ds(pl.multiple_of(core * (INNER // 2), INNER // 2), INNER // 2)
-    far_out = pl.ds(pl.multiple_of((1 - core) * (INNER // 2), INNER // 2), INNER // 2)
-    left, right = mixed_low_ref[:, near_out], mixed_low_ref[:, far_out]
+
+    near, far = core_halves(place_ref, INNER // 2)
+    left, right = mixed_low_ref[:, near], mixed_low_ref[:, far]
     forecast = jnp.zeros((ROWS, LANES), f32)
     for side in range(2):
         columns = slice(side * INNER, (side + 1) * INNER)
@@ -197,13 +209,12 @@
         out_ref[member] = jnp.where(lanes == VARS + 2, low, kept)
 
 
-def mixed_gradient(upd_low, core, wa_ref, wb_ref, target_ref, rows):
-    near_out = pl.ds(pl.multiple_of(core * (INNER // 2), INNER // 2), INNER // 2)
-    far_out = pl.ds(pl.multiple_of((1 - core) * (INNER // 2), INNER // 2), INNER // 2)
-    for w_ref, lanes in ((wa_ref, near_out), (wb_ref, far_out)):
-        target_ref[rows, lanes] = mm_t(upd_low[:, :INNER], out_weights(w_ref, 0)) + mm_t(
+def mixed_gradient(upd_low, place_ref, wa_ref, wb_ref, target_ref):
+    for w_ref, lanes in zip((wa_ref, wb_ref), core_halves(place_ref, INNER // 2)):
+        target_ref[:, lanes] = mm_t(upd_low[:, :INNER], out_weights(w_ref, 0)) + mm_t(
             upd_low[:, INNER:], out_weights(w_ref, 1)
         )
+    return target_ref[...].astype(bf16).astype(f32)
 
 
 def gradient_operands(scaled, row_dot, g0_ref, g1_ref, rows):
@@ -219,23 +230,21 @@
         g1_ref[rows, lanes] = jnp.where(first, extra, own)
 
 
-def pick(base, rows, lanes):
+def pick(rows, lanes):
     row = lax.broadcasted_iota(jnp.int32, (rows, lanes), 0)
     lane = lane_index(rows, lanes)
     return row, lane
 
 
 def upstream_kernel(
-    place_ref, pg_ref, decoder_ref, wa_ref, wb_ref, mixed_ref, total_ref,
+    place_ref, pg_ref, decoder_ref, wa_ref, wb_ref, mixed_ref, total_ref, reach_ref,
     upd_ref, scaled_ref, g0_ref, g1_ref, message_ref, loss_ref, grad_ref,
 ):
-    core = place_ref[0]
     pg = pg_ref[...]
     upd = mm(pg, decoder_ref[...])
     upd_ref[...] = upd
     everything = slice(0, ROWS)
-    mixed_gradient(upd.astype(bf16), core, wa_ref, wb_ref, grad_ref, everything)
-    grad = grad_ref[...].astype(bf16).astype(f32)
+    grad = mixed_gradient(upd.astype(bf16), place_ref, wa_ref, wb_ref, grad_ref)
     total = total_ref[...]
     inverse = 1.0 / total
     row_dot = head_sums(grad * mixed_ref[...], segment_matrix(1.0)) * inverse
@@ -243,22 +252,37 @@
     scaled_ref[...] = scaled
     gradient_operands(scaled, row_dot, g0_ref, g1_ref, everything)
 
-    row, lane = pick(None, INNER, LANES)
+    row, lane = pick(INNER, LANES)
     head_row = (row % HEAD == 0)
     chosen = lambda start: jnp.where(head_row & (lane == start + row // HEAD), 1.0, 0.0).astype(bf16)
     high, low = split(total)
     stats = mm(high, chosen(VARS)) + mm(low, chosen(VARS + 8)) + mm(row_dot.astype(bf16), chosen(VARS + 16))
     lanes = lane_index(ROWS, LANES)
-    message_ref[...] = jnp.where(lanes < VARS, pg.astype(f32), stats).astype(bf16)
+    message = jnp.where(lanes < VARS, pg.astype(f32), stats)
+    message = jnp.where(lanes == REACH_LANE, column_of(reach_ref).astype(f32), message)
     kept = jnp.where((lanes >= VARS) & (lanes < VARS + 3), pg.astype(f32), 0.0)
-    total_loss = jnp.sum(jnp.sum(kept, axis=1, keepdims=True), axis=0, keepdims=True) * (1.0 / SLOT)
-    loss_ref[...] = jnp.broadcast_to(total_loss, (8, LANES))
+    loss = jnp.sum(jnp.sum(kept, axis=1, keepdims=True), axis=0, keepdims=True) * (1.0 / SLOT)
+    loss_ref[...] = jnp.broadcast_to(loss, (8, LANES))
+    high, middle = split(loss)
+    low = (loss - high.astype(f32) - middle.astype(f32)).astype(bf16)
+    for lane, part in enumerate((high, middle, low)):
+        message = jnp.where(lanes == LOSS_LANE + lane, part.astype(f32), message)
+    message_ref[...] = message.astype(bf16)
+
+
+def pair_kernel(place_ref, own_ref, low_ref, high_ref, out_ref):
+    lanes = lane_index(1, LANES)
+    even = place_ref[3] == 0
+    nearby = jnp.where(even, high_ref[0:16, :].astype(f32), low_ref[0:16, :].astype(f32))[0:1, :]
+    nearby = jnp.where((lanes >= LOSS_LANE) & (lanes < LOSS_LANE + 3), nearby, 0.0)
+    out_ref[...] = own_ref[...] + jnp.sum(nearby, axis=1, keepdims=True)
 
 
 def query_kernel(
     place_ref, q_ref, k_ref, v_ref, g0_ref, g1_ref, reach_ref, qgrad_ref, bias_ref,
 ):
-    row_start = place_ref[1]
+    row_start = place_ref[0]
+    column = column_of(reach_ref)
     for tile in range(2):
         offset = (
             lane_index(TILE, WINDOW)
@@ -266,13 +290,13 @@
             - lax.broadcasted_iota(jnp.int32, (TILE, WINDOW), 0)
         )
         position = row_start - HALF + tile * TILE + lane_index(TILE, WINDOW)
-        reach = reach_ref[tile * TILE : (tile + 1) * TILE, :]
-        inside = (offset >= -reach) & (offset < reach) & (position >= 0) & (position < place_ref[2])
+        reach = column[tile * TILE : (tile + 1) * TILE, 0:1]
+        inside = (offset >= -reach) & (offset < reach) & (position >= 0) & (position < place_ref[1])
         bias_ref[tile] = jnp.where(inside, 0.0, -1e30)
     first = lane_index(1, LANES) < HEAD
 
-    def one_pair(pair, carry):
-        lanes = pl.ds(pl.multiple_of(pair * LANES, LANES), LANES)
+    for pair in range(HEADS // 2):
+        lanes = slice(pair * LANES, (pair + 1) * LANES)
         for tile in range(2):
             rows = slice(tile * TILE, (tile + 1) * TILE)
             window = slice(tile * TILE, tile * TILE + WINDOW)
@@ -287,20 +311,15 @@
                 pull = mm_t(g_ref[rows, lanes], jnp.where(mine, values, jnp.ones_like(values)))
                 grads.append(mm((weight * pull).astype(bf16), keys))
             qgrad_ref[rows, lanes] = jnp.where(first, grads[0], grads[1]) * 0.125
-        return carry
-
-    lax.fori_loop(0, HEADS // 2, one_pair, 0)
 
 
 def backward_kernel(
     place_ref, low_ref, high_ref, decoder_ref, wa_ref, wb_ref, q_ref, k_ref, v_ref,
     scaled_ref, g0_ref, g1_ref, reach_ref, qgrad_ref, unit_ref, factor_ref,
-    latent_ref, pert_ref, gain_ref, upd_ref, loss_a_ref, loss_b_ref,
-    noise_ref, send_ref,
-    all_scaled, all_g0, all_g1, bias_ref, grad_ref, kv_ref, normed_grad_ref,
+    qkv_grad_ref,
+    all_scaled, all_g0, all_g1, all_reach, bias_ref, grad_ref, kv_ref,
 ):
-    core = place_ref[0]
-    row, lane = pick(None, LANES, INNER)
+    row, lane = pick(LANES, INNER)
     spread = lambda start: row == start + lane // HEAD
     expand_total = jnp.where(spread(VARS) | spread(VARS + 8), 1.0, 0.0).astype(bf16)
     expand_dot = jnp.where(spread(VARS + 16), 1.0, 0.0).astype(bf16)
@@ -308,11 +327,15 @@
     all_scaled[middle, :] = scaled_ref[...]
     all_g0[middle, :] = g0_ref[...]
     all_g1[middle, :] = g1_ref[...]
+    all_reach[:, middle] = jnp.broadcast_to(reach_ref[...], (8, ROWS))
     for block, message_ref in ((0, low_ref), (2, high_ref)):
         rows = slice(block * ROWS, (block + 1) * ROWS)
         message = message_ref[...]
-        mixed_gradient(mm(message, decoder_ref[...]).astype(bf16), core, wa_ref, wb_ref, grad_ref, slice(0, ROWS))
-        grad = grad_ref[...].astype(bf16).astype(f32)
+        turned = message.astype(f32).T
+        all_reach[:, rows] = jnp.broadcast_to(turned[REACH_LANE : REACH_LANE + 1, :], (8, ROWS)).astype(jnp.int32)
+        grad = mixed_gradient(
+            mm(message, decoder_ref[...]).astype(bf16), place_ref, wa_ref, wb_ref, grad_ref
+        )
         total = mm(message, expand_total)
         scaled = (grad / jnp.where(total > 0.0, total, 1.0)).astype(bf16)
         all_scaled[rows, :] = scaled
@@ -324,14 +347,13 @@
             + lax.broadcasted_iota(jnp.int32, (TILE, WINDOW), 0)
             - lane_index(TILE, WINDOW)
         )
-        reach = reach_ref[0:1, tile * TILE : tile * TILE + WINDOW]
+        reach = all_reach[0:1, tile * TILE : tile * TILE + WINDOW]
         bias_ref[tile] = jnp.where((offset >= -reach) & (offset < reach), 0.0, -1e30)
     first = lane_index(1, LANES) < HEAD
 
-    def one_pair(pair, carry):
-        start = pl.multiple_of(pair * LANES, LANES)
-        lanes = pl.ds(start, LANES)
-        value_lanes = pl.ds(pl.multiple_of(INNER + start, LANES), LANES)
+    for pair in range(HEADS // 2):
+        lanes = slice(pair * LANES, (pair + 1) * LANES)
+        value_lanes = slice(INNER + pair * LANES, INNER + (pair + 1) * LANES)
         for tile in range(2):
             rows = slice(tile * TILE, (tile + 1) * TILE)
             window = slice(tile * TILE, tile * TILE + WINDOW)
@@ -350,21 +372,22 @@
                 key_grads.append(mm((weight * pull).astype(bf16), queries))
             kv_ref[rows, lanes] = jnp.where(first, key_grads[0], key_grads[1]) * 0.125
             kv_ref[rows, value_lanes] = jnp.where(first, value_grads[0], value_grads[1])
-        return carry
-
-    lax.fori_loop(0, HEADS // 2, one_pair, 0)
 
     segments = segment_matrix(1.0 / HEAD)
-    parts = []
     for part, grad in ((0, qgrad_ref[...]), (1, kv_ref[:, :INNER])):
         columns = slice(part * INNER, (part + 1) * INNER)
         unit = unit_ref[:, columns]
         along = head_sums(grad * unit, segments)
-        parts.append((factor_ref[:, columns] * (grad - unit * along)).astype(bf16))
-    parts.append(kv_ref[:, INNER:].astype(bf16))
-    near = pl.ds(pl.multiple_of(core * INNER, INNER), INNER)
-    far = pl.ds(pl.multiple_of((1 - core) * INNER, INNER), INNER)
-    for w_ref, lanes in ((wa_ref, near), (wb_ref, far)):
+        qkv_grad_ref[:, columns] = (factor_ref[:, columns] * (grad - unit * along)).astype(bf16)
+    qkv_grad_ref[:, 2 * INNER :] = kv_ref[:, INNER:].astype(bf16)
+
+
+def hidden_kernel(
+    place_ref, qkv_grad_ref, wa_ref, wb_ref, latent_ref, pert_ref, gain_ref, upd_ref, loss_ref,
+    noise_ref, send_ref, normed_grad_ref,
+):
+    parts = [qkv_grad_ref[:, part * INNER : (part + 1) * INNER] for part in range(3)]
+    for w_ref, lanes in zip((wa_ref, wb_ref), core_halves(place_ref, INNER)):
         normed_grad_ref[:, lanes] = (
             mm_t(parts[0], qkv_weights(w_ref, 0))
             + mm_t(parts[1], qkv_weights(w_ref, 1))
@@ -385,13 +408,15 @@
         turned = result.T.astype(bf16)
         for member in range(MEMBERS):
             send_ref[member, :HEAD, rows] = turned[member * HEAD : (member + 1) * HEAD, :]
-    loss = jnp.broadcast_to(loss_a_ref[0:1, 0:1] + loss_b_ref[0:1, 0:1], (16, ROWS))
-    high, mid = split(loss)
-    low = (loss - high.astype(f32) - mid.astype(f32)).astype(bf16)
+    loss = jnp.broadcast_to(loss_ref[0:1, 0:1], (16, ROWS))
+    high, middle = split(loss)
+    low = (loss - high.astype(f32) - middle.astype(f32)).astype(bf16)
     lanes = lane_index(16, ROWS)
-    tail = jnp.where(lanes == 0, high, jnp.where(lanes == 1, mid, jnp.where(lanes == 2, low, jnp.zeros_like(low))))
+    tail = jnp.zeros((16, ROWS), f32)
+    for lane, part in enumerate((high, middle, low)):
+        tail = jnp.where(lanes == lane, part.astype(f32), tail)
     for member in range(MEMBERS):
-        send_ref[member, HEAD:, :] = tail
+        send_ref[member, HEAD:, :] = tail.astype(bf16)
 
 
 def finish_kernel(received_ref, latent_grad_ref, loss_ref):
@@ -402,18 +427,20 @@
     loss_ref[...] = jnp.broadcast_to(jnp.sum(total[HEAD : HEAD + 1, :], axis=1, keepdims=True), (8, LANES))
 
 
-def call(body, outs, scratch, cost, *operands):
-    specs = [
-        pl.BlockSpec(memory_space=pltpu.SMEM if o.dtype == jnp.int32 and o.ndim == 1 else pltpu.VMEM)
-        for o in operands
+def call(body, outs, scratch, megabytes, cost, *operands, far=()):
+    spaces = [
+        pltpu.SMEM if o.dtype == jnp.int32 and o.ndim == 1 else pltpu.HBM if i in far else pltpu.VMEM
+        for i, o in enumerate(operands)
     ]
+    specs = [pl.BlockSpec(memory_space=space) for space in spaces]
+    semaphores = [pltpu.SemaphoreType.DMA((len(far),))] if far else []
     result = pl.pallas_call(
         body,
         out_shape=tuple(jax.ShapeDtypeStruct(shape, kind) for shape, kind in outs),
         in_specs=specs,
         out_specs=tuple(pl.BlockSpec(memory_space=pltpu.VMEM) for _ in outs),
-        scratch_shapes=[pltpu.VMEM(shape, kind) for shape, kind in scratch],
-        compiler_params=pltpu.CompilerParams(vmem_limit_bytes=40 * 1024 * 1024),
+        scratch_shapes=[pltpu.VMEM(shape, kind) for shape, kind in scratch] + semaphores,
+        compiler_params=pltpu.CompilerParams(vmem_limit_bytes=megabytes * 1024 * 1024),
         cost_estimate=pl.CostEstimate(flops=cost, bytes_accessed=4_000_000, transcendentals=0),
     )(*operands)
     return result
@@ -449,12 +476,12 @@
     return pairs
 
 
-def loss_route(step):
+def loss_route():
     pairs = []
-    for index, member in enumerate(members()):
-        for node in range(32):
-            target = (node + 2 * index + step) % 32
-            pairs.append((flat(*member, node // 2, node % 2), flat(*member, target // 2, target % 2)))
+    for shift, member in enumerate(members()):
+        for z in range(16):
+            for xh in range(2):
+                pairs.append((flat(*member, z, xh), flat(*member, (z + shift) % 16, xh)))
     return pairs
 
 
@@ -471,9 +498,8 @@
 ):
     pert = member_perturbations[0]
     node_total = ROWS * lax.axis_size(NODE)
-    core = lax.axis_index("c")
     member = lax.axis_index(MEMBER)
-    place = jnp.stack([core, lax.axis_index(NODE) * ROWS, jnp.int32(node_total)]).astype(jnp.int32)
+    place = jnp.stack([lax.axis_index(NODE) * ROWS, jnp.int32(node_total), lax.axis_index("c"), lax.axis_index("xh")]).astype(jnp.int32)
 
     packed = jnp.concatenate(
         [
@@ -484,40 +510,40 @@
     )
     with jax.named_scope("weights_over_node"):
         mine = lax.ppermute(packed, EVERY, weight_route())
-    with jax.named_scope("latent_halo"):
-        shared = jnp.concatenate(
-            [latent.T, jnp.pad(node_window_halfspan.astype(bf16)[None], ((0, 15), (0, 0)))], axis=0
-        )
-        shared_low, shared_high = both_ways(shared)
-        extended = jnp.concatenate([shared_low, shared, shared_high], axis=1)
-        reach_row = extended[HEAD : HEAD + 8].astype(jnp.int32)
-    with jax.named_scope("perturbation_halo"):
-        pert_low, pert_high = both_ways(pert)
-    with jax.named_scope("latent_over_member"):
-        latent_turned = lax.all_gather(extended[:HEAD], MEMBER, axis=0, tiled=True)
-    with jax.named_scope("weights_over_member"):
-        wa = lax.all_to_all(
-            jnp.broadcast_to(mine[None], (16,) + mine.shape), ("y", "xl", "xh"), 0, 0, tiled=True
-        )
-    with jax.named_scope("weights_over_core"):
-        wb = lax.ppermute(wa, "c", [(0, 1), (1, 0)])
-
-    reach_column = node_window_halfspan[:, None]
     decoder = jnp.pad(decoder_weight_matrix, ((0, LANES - VARS), (0, 0)))
     truth = lax.dynamic_slice_in_dim(observed_truth, member * SLOT, SLOT, 1)
     truth = jnp.pad(truth.T, ((0, 0), (0, LANES - VARS)))
     mask = lax.dynamic_slice_in_dim(region_mask, member * SLOT, SLOT, 0)
     area = (1.0 - (1.0 - region_share) * mask.astype(f32))[:, None]
-    gain = layer_norm_gain[None]
-
+    area = jnp.broadcast_to(area, (SLOT, LANES))
+    latent_copies = jnp.broadcast_to(latent.T[None], (MEMBERS, HEAD, ROWS))
+    place, reach_row, decoder, truth, area, gain, latent_copies = lax.optimization_barrier(
+        (place, node_window_halfspan[None], decoder, truth, area,
+         layer_norm_gain[None], latent_copies)
+    )
+    with jax.named_scope("latent_over_member"):
+        latent_turned = lax.all_to_all(latent_copies, MEMBER, 0, 0, tiled=True).reshape(WIDTH, ROWS)
     with jax.named_scope("layer_norm"):
         normed, latent_own = call(
             norm_kernel,
-            [((EXT, WIDTH), bf16), ((ROWS, WIDTH), bf16)],
+            [((ROWS, WIDTH), bf16), ((ROWS, WIDTH), bf16)],
             [],
+            8,
             1_000_000_000,
-            latent_turned, pert_low, pert, pert_high, gain,
-        )
+            latent_turned, pert, gain,
+        )
+    mine, normed = lax.optimization_barrier((mine, normed))
+    with jax.named_scope("normed_halo"):
+        normed_low, normed_high = both_ways(normed)
+    with jax.named_scope("weights_over_x"):
+        row = lax.all_to_all(jnp.broadcast_to(mine[None], (4,) + mine.shape), ("xl", "xh"), 0, 0, tiled=True)
+        row = row.reshape(128, PACKED)
+    with jax.named_scope("weights_over_y"):
+        wa = lax.all_to_all(jnp.broadcast_to(row[None], (4,) + row.shape), "y", 0, 0, tiled=True)
+        wa = wa.reshape(16, 32, PACKED)
+    wa, normed_low, normed_high = lax.optimization_barrier((wa, normed_low, normed_high))
+    with jax.named_scope("weights_over_core"):
+        wb = lax.ppermute(wa, "c", [(0, 1), (1, 0)])
     with jax.named_scope("forward"):
         q, k, v, unit, factor, mixed, total, forecast = call(
             forward_kernel,
@@ -526,8 +552,9 @@
             + [((ROWS, INNER), f32)] * 2
             + [((ROWS, LANES), f32)],
             [((2, TILE, WINDOW), f32), ((ROWS, INNER), bf16)],
+            40,
             4_000_000_000,
-            place, normed, wa, wb, latent_own, pert, reach_column, decoder,
+            place, normed_low, normed, normed_high, wa, wb, latent_own, pert, reach_row, decoder,
         )
     with jax.named_scope("forecasts_over_member"):
         forecasts = lax.all_to_all(
@@ -535,7 +562,7 @@
         )
     with jax.named_scope("score"):
         (pred_grads,) = call(
-            score_kernel, [((MEMBERS, SLOT, LANES), bf16)], [], 10_000_000, forecasts, truth, area
+            score_kernel, [((MEMBERS, SLOT, LANES), bf16)], [], 8, 10_000_000, forecasts, truth, area
         )
     with jax.named_scope("gradients_over_member"):
         pred_grad = lax.all_to_all(pred_grads, MEMBER, 0, 0, tiled=True).reshape(ROWS, LANES)
@@ -544,37 +571,52 @@
             upstream_kernel,
             [((ROWS, WIDTH), f32)] + [((ROWS, INNER), bf16)] * 3 + [((ROWS, LANES), bf16), ((8, LANES), f32)],
             [((ROWS, INNER), f32)],
+            16,
             500_000_000,
-            place, pred_grad, decoder, wa, wb, mixed, total,
+            place, pred_grad, decoder, wa, wb, mixed, total, reach_row,
         )
     with jax.named_scope("gradient_halo"):
         message_low, message_high = both_ways(message)
-    with jax.named_scope("loss_over_node"):
-        loss_a = lax.ppermute(loss_part, EVERY, loss_route(0))
-        loss_b = lax.ppermute(loss_part, EVERY, loss_route(1))
     with jax.named_scope("query_gradients"):
         (qgrad,) = call(
             query_kernel,
             [((ROWS, INNER), f32)],
             [((2, TILE, WINDOW), f32)],
+            12,
             4_000_000_000,
-            place, q, k, v, g0, g1, reach_column,
-        )
+            place, q, k, v, g0, g1, reach_row,
+        )
+    with jax.named_scope("loss_over_node"):
+        (loss_part,) = call(
+            pair_kernel, [((8, LANES), f32)], [], 4, 10_000, place, loss_part, message_low, message_high
+        )
+        loss_part = lax.ppermute(loss_part, EVERY, loss_route())
     with jax.named_scope("backward"):
-        noise, send = call(
+        (qkv_grad,) = call(
             backward_kernel,
-            [((ROWS, WIDTH), f32), ((MEMBERS, HEAD + 16, ROWS), bf16)],
+            [((ROWS, 3 * INNER), bf16)],
             [((EXT, INNER), bf16)] * 3
-            + [((2, TILE, WINDOW), f32), ((ROWS, INNER), f32), ((ROWS, WIDTH), f32), ((ROWS, WIDTH), f32)],
+            + [((8, EXT), jnp.int32)]
+            + [((2, TILE, WINDOW), f32), ((ROWS, INNER), f32), ((ROWS, WIDTH), f32)],
+            24,
             4_000_000_000,
             place, message_low, message_high, decoder, wa, wb, q, k, v, scaled, g0, g1, reach_row,
-            qgrad, unit, factor, latent_own, pert, gain, upd, loss_a, loss_b,
+            qgrad, unit, factor,
+        )
+    with jax.named_scope("hidden_gradient"):
+        noise, send = call(
+            hidden_kernel,
+            [((ROWS, WIDTH), f32), ((MEMBERS, HEAD + 16, ROWS), bf16)],
+            [((ROWS, WIDTH), f32)],
+            16,
+            1_000_000_000,
+            place, qkv_grad, wa, wb, latent_own, pert, gain, upd, loss_part,
         )
     with jax.named_scope("latent_gradient_over_member"):
         received = lax.all_to_all(send, MEMBER, 0, 0, tiled=True)
     with jax.named_scope("finish"):
         latent_grad, loss = call(
-            finish_kernel, [((HEAD, ROWS), f32), ((8, LANES), f32)], [], 10_000_000, received
+            finish_kernel, [((HEAD, ROWS), f32), ((8, LANES), f32)], [], 8, 10_000_000, received
         )
     loss = loss[0, 0] / (MEMBERS * node_total * VARS)
     return (loss, latent_grad.T, noise[None])

time: 235 us -> 180 us (0.77)
  waiting for transfers between devices: 66.4 us -> 25.9 us
  blocking collectives: 27.5 us -> 58.2 us
  starting transfers between devices: 70.2 us -> 53.4 us
  between operations: 16.2 us -> 2.66 us
  Pallas kernels: 36.2 us -> 27.5 us
  local copies, waits for them, and re-layouts: 15.5 us -> 10.4 us
    all_to_all x0 -> x3, blocking collectives: none -> 31.8 us  [the longest x1 12 us: shards(): lax.all_to_all(jnp.broadcast_to(mine[None], (4,) + mine.shape), ('xl', 'x...]
    ppermute x3 -> x2, waiting for transfers between devices: 26.6 us -> 9.57 us  [both_ways(): high = lax.ppermute(block, NODE, [(i + 1, i) for i in range(count - 1)])]
    all_gather x1 -> x0, waiting for transfers between devices: 10.1 us -> none  [shards(): latent_turned = lax.all_gather(extended[:HEAD], MEMBER, axis=0, tiled=True)]
    all_to_all x3 -> x2, waiting for transfers between devices: 9.76 us -> 0.01 us  [the longest x1 0.01 us: shards(): lax.all_to_all(latent_copies, MEMBER, 0, 0, tiled=True).reshape(WIDTH, ROWS)]
    pallas_call x7 -> x9, Pallas kernels: 36.2 us -> 27.5 us  [call(): pl.pallas_call(body, out_shape=tuple((jax.ShapeDtypeStruct(shape, kind) f...]
    ppermute x3 -> x2, waiting for transfers between devices: 16.9 us -> 9.98 us  [both_ways(): low = lax.ppermute(block, NODE, [(i, i + 1) for i in range(count - 1)])]
    ppermute x2 -> x1, starting transfers between devices: 9.8 us -> 3.83 us  [shards(): loss_part = lax.ppermute(loss_part, EVERY, loss_route())]
    ppermute x3 -> x2, starting transfers between devices: 17.5 us -> 12.1 us  [both_ways(): low = lax.ppermute(block, NODE, [(i, i + 1) for i in range(count - 1)])]
  transfers between devices with their start and end apart: 14 -> 9, of which waited for: 7 -> 4; matrix products, arithmetic and copies ran while one was open for 2% -> 0% of each run, Pallas kernels for 3% -> 7%
where the time goes in v2:
time: 180 us; the launch traced here: 179 us
  blocking collectives  58.2 us (32%)
  starting transfers between devices  53.4 us (30%)
  Pallas kernels  27.5 us (15%)
  waiting for transfers between devices  25.9 us (14%)
  local copies, waits for them, and re-layouts  10.4 us (6%)
  between operations  2.66 us (1%)
    pallas_call x9, Pallas kernels, call(): pl.pallas_call(body, out_shape=tuple((jax.ShapeDtypeStruct(shape, kind) f...  27.5 us
    all_to_all x1, blocking collectives, shards(): received = lax.all_to_all(send, MEMBER, 0, 0, tiled=True)  26.4 us
    ppermute x2, starting transfers between devices, both_ways(): low = lax.ppermute(block, NODE, [(i, i + 1) for i in range(count - 1)])  12.1 us
    ppermute x1, starting transfers between devices, shards(): mine = lax.ppermute(packed, EVERY, weight_route())  12.1 us
    all_to_all x1, blocking collectives, shards(): lax.all_to_all(jnp.broadcast_to(mine[None], (4,) + mine.shape), ('xl', 'x...  12 us
    all_to_all x1, blocking collectives, shards(): lax.all_to_all(forecast.reshape(MEMBERS, SLOT, LANES), MEMBER, 0, 0, tile...  10.9 us
    all_to_all x1, starting transfers between devices, shards(): lax.all_to_all(latent_copies, MEMBER, 0, 0, tiled=True).reshape(WIDTH, ROWS)  10.2 us
    all_to_all x1, starting transfers between devices, shards(): lax.all_to_all(jnp.broadcast_to(row[None], (4,) + row.shape), 'y', 0, 0,...  10.1 us
  transfers between devices with their start and end apart: 9, of which 4 were waited for; matrix products, arithmetic and copies ran while one was open for 0% of the time, Pallas kernels for 7%

profile of v2, /device:TPU:1, one launch (start us, length us, event | category | flops | bytes accessed | tf_op | source)
XLA Modules:
  0.0 178.8 jit_solution(5326410747953752803)
XLA Ops:
  0.6 0.0 copy-start
  0.6 0.0 copy-start.10
  0.7 0.0 copy-start.9
  0.7 0.0 copy-start.1
  0.7 0.8 broadcast_in_dim.36.gain_ref
  1.4 0.8 multiply_subtract_fusion
  2.2 0.0 copy-done
  2.2 0.1 constant_dynamic-slice_fusion
  2.3 0.1 copy.13
  2.4 1.0 pad.8.decoder_ref
  3.3 0.1 pad_add_fusion.place_ref
  3.4 0.1 broadcast_in_dim.17.area_ref
  3.5 1.6 broadcast_in_dim.37
  5.1 10.2 %all-to-all-start = ((bf16[16,64,256]{2,1,0:T(8,128)(2,1)}), bf16[16,64,256]{2,1,0:T(8,128)(2,1)S(1)}, u32[]{:S(2)}, u32[]{:S(2)}) async-start(bf16[16,64,256]{2,1,0:T(8,128)(2,1)} %broadcast_in_dim.37), calls=%async_computation | async-start | bytes 1048576 | tf_op jit(solution)/shard_map/latent_over_member/all_to_all | solution.py:525
  15.3 0.0 copy-done.10
  15.3 0.0 copy-done.9
  15.4 12.1 %collective-permute-start = (bf16[32,2048]{1,0:T(8,128)(2,1)S(1)}, bf16[32,2048]{1,0:T(8,128)(2,1)S(1)}, u32[]{:S(2)}, u32[]{:S(2)}) collective-permute-start(bf16[32,2048]{1,0:T(8,128)(2,1)S(1)} %maximum_maximum_fusion), channel_id=1, source_target_pairs={{0,0},{1,1},{64,2},{65,3},{128,4},{129,5},{192,6},{193,7},{256,8},... | collective-permute-start | bytes 393224 | tf_op jit(solution)/shard_map/weights_over_node/ppermute | solution.py:512
  27.5 0.0 all-to-all-done
  27.5 0.0 copy-done.1
  27.5 0.6 layer_norm.1
  28.1 0.0 copy-start.3
  28.1 2.6 %collective-permute-done = bf16[32,2048]{1,0:T(8,128)(2,1)S(1)} collective-permute-done((bf16[32,2048]{1,0:T(8,128)(2,1)S(1)}, bf16[32,2048]{1,0:T(8,128)(2,1)S(1)}, u32[]{:S(2)}, u32[]{:S(2)}) %collective-permute-start) | collective-permute-done | bytes 131104 | tf_op jit(solution)/shard_map/weights_over_node/ppermute | solution.py:512
  30.8 12.0 %all_to_all.30 = bf16[4,32,2048]{2,1,0:T(8,128)(2,1)S(1)} all-to-all(bf16[4,32,2048]{2,1,0:T(8,128)(2,1)S(1)} %broadcast_in_dim.38), channel_id=1, replica_groups=mesh['y'=4,'xl'=2,'c'=2,'z'=16,'xh'=2] {'xl','xh'}, dimensions={0} | all-to-all | bytes 1048576 | tf_op jit(solution)/shard_map/weights_over_x/all_to_all | solution.py:539
  42.7 1.6 broadcast_in_dim.40
  44.3 0.0 copy-done.3
  44.3 0.0 copy-start.2
  44.3 10.1 %all-to-all-start.2 = ((bf16[4,128,2048]{2,1,0:T(8,128)(2,1)}), bf16[4,128,2048]{2,1,0:T(8,128)(2,1)S(1)}, u32[]{:S(2)}, u32[]{:S(2)}) async-start(bf16[4,128,2048]{2,1,0:T(8,128)(2,1)} %broadcast_in_dim.40), calls=%async_computation.2 | async-start | bytes 4194304 | tf_op jit(solution)/shard_map/weights_over_y/all_to_all | solution.py:542
  54.4 1.3 collective-permute-start.2
  55.7 5.5 %collective-permute-start.1 = (bf16[256,1024]{1,0:T(8,128)(2,1)}, bf16[256,1024]{1,0:T(8,128)(2,1)S(1)}, u32[]{:S(2)}, u32[]{:S(2)}) collective-permute-start(bf16[256,1024]{1,0:T(8,128)(2,1)} %copy-done.3), channel_id=1, source_target_pairs={{0,1},{1,2},{2,3},{3,4},{4,5},{5,6},{6,7},{7,8},{8,9},{9,10},{10,1... | collective-permute-start | bytes 1572872 | tf_op jit(solution)/shard_map/normed_halo/ppermute | solution.py:451
  61.2 9.6 %collective-permute-done.2.high_ref = bf16[256,1024]{1,0:T(8,128)(2,1)S(1)} collective-permute-done((bf16[256,1024]{1,0:T(8,128)(2,1)}, bf16[256,1024]{1,0:T(8,128)(2,1)S(1)}, u32[]{:S(2)}, u32[]{:S(2)}) %collective-permute-start.2) | collective-permute-done | bytes 524320 | tf_op jit(solution)/shard_map/normed_halo/ppermute | solution.py:452
  70.8 0.0 copy-start.5
  70.8 0.8 copy-done.5
  71.6 10.0 %collective-permute-done.1.low_ref = bf16[256,1024]{1,0:T(8,128)(2,1)S(1)} collective-permute-done((bf16[256,1024]{1,0:T(8,128)(2,1)}, bf16[256,1024]{1,0:T(8,128)(2,1)S(1)}, u32[]{:S(2)}, u32[]{:S(2)}) %collective-permute-start.1) | collective-permute-done | bytes 524320 | tf_op jit(solution)/shard_map/normed_halo/ppermute | solution.py:451
  81.6 0.0 copy-start.7
  81.6 0.8 copy-done.7
  82.4 0.0 all-to-all-done.2
  82.4 2.4 %collective-permute-start.3 = (bf16[16,32,2048]{2,1,0:T(8,128)(2,1)S(1)}, bf16[16,32,2048]{2,1,0:T(8,128)(2,1)S(1)}, u32[]{:S(2)}, u32[]{:S(2)}) collective-permute-start(bf16[16,32,2048]{2,1,0:T(8,128)(2,1)S(1)} %bitcast.15), channel_id=1, source_target_pairs={{0,32},{32,0},{1,33},{33,1},{2,34},{34,2},{3,35},{35,3},{4,36},{36... | collective-permute-start | bytes 6291464 | tf_op jit(solution)/shard_map/weights_over_core/ppermute | solution.py:546
  84.8 3.8 %collective-permute-done.3.wb_ref = bf16[16,32,2048]{2,1,0:T(8,128)(2,1)S(1)} collective-permute-done((bf16[16,32,2048]{2,1,0:T(8,128)(2,1)S(1)}, bf16[16,32,2048]{2,1,0:T(8,128)(2,1)S(1)}, u32[]{:S(2)}, u32[]{:S(2)}) %collective-permute-start.3) | collective-permute-done | bytes 2097184 | tf_op jit(solution)/shard_map/weights_over_core/ppermute | solution.py:546
  88.5 0.0 copy-done.2
  88.6 0.0 copy-start.4
  88.6 1.0 copy-done.4
  89.6 0.0 copy-start.6
  89.6 1.0 copy-done.6
  90.6 0.0 copy-start.8
  90.6 1.0 copy-done.8
  91.7 8.4 %forward.1 = (bf16[768,512]{1,0:T(8,128)(2,1)S(1)}, bf16[768,512]{1,0:T(8,128)(2,1)S(1)}, bf16[768,512]{1,0:T(8,128)(2,1)S(1)}, f32[256,1024]{1,0:T(8,128)S(1)},...) custom-call(s32[4]{0:T(128)S(1)} %pad_add_fusion.place_ref, ...), custom_call_target="tpu_custom_call" | custom-call | flops 4000000000 | bytes 4000000 | tf_op jit(solution)/shard_map/forward/pallas_call | solution.py:437
  100.1 10.9 %all_to_all.31.forecast_ref = f32[16,16,128]{2,1,0:T(8,128)S(1)} all-to-all(f32[16,16,128]{2,1,0:T(8,128)S(1)} %bitcast.25), channel_id=1, replica_groups=mesh['y'=4,'xl'=2,'c'=2,'z'=16,'xh'=2] {'y','xl','c'}, dimensions={0} | all-to-all | bytes 262144 | tf_op jit(solution)/shard_map/forecasts_over_member/all_to_all | solution.py:560
  111.0 0.7 score.1
  111.6 8.9 %all_to_all.32 = bf16[16,16,128]{2,1,0:T(8,128)(2,1)S(1)} all-to-all(bf16[16,16,128]{2,1,0:T(8,128)(2,1)S(1)} %score.1), channel_id=1, replica_groups=mesh['y'=4,'xl'=2,'c'=2,'z'=16,'xh'=2] {'y','xl','c'}, dimensions={0} | all-to-all | bytes 131072 | tf_op jit(solution)/shard_map/gradients_over_member/all_to_all | solution.py:568
  120.6 2.1 %upstream.1 = (f32[256,1024]{1,0:T(8,128)S(1)}, bf16[256,512]{1,0:T(8,128)(2,1)S(1)}, bf16[256,512]{1,0:T(8,128)(2,1)S(1)}, bf16[256,512]{1,0:T(8,128)(2,1)S(1)}...) custom-call(s32[4]{0:T(128)S(1)} %pad_add_fusion.place_ref, bf16[256,128]{1,0:T(8,128)(2,1)S(1)} %bitcast.24, ...), custom_call_target="tpu_custom_call" | custom-call | flops 500000000 | bytes 4000000 | tf_op jit(solution)/shard_map/upstream/pallas_call | solution.py:437
  122.7 1.3 collective-permute-start.5
  124.0 6.6 %collective-permute-start.4 = (bf16[256,128]{1,0:T(8,128)(2,1)S(1)}, bf16[256,128]{1,0:T(8,128)(2,1)S(1)}, u32[]{:S(2)}, u32[]{:S(2)}) collective-permute-start(bf16[256,128]{1,0:T(8,128)(2,1)S(1)} %get-tuple-element.52), channel_id=1, source_target_pairs={{0,1},{1,2},{2,3},{3,4},{4,5},{5,6},{6,7},{7,8},{8,9},{9,10},{10,1... | collective-permute-start | bytes 196616 | tf_op jit(solution)/shard_map/gradient_halo/ppermute | solution.py:451
  130.6 4.5 %query_gradients.1.qgrad_ref = f32[256,512]{1,0:T(8,128)S(1)} custom-call(s32[4]{0:T(128)S(1)} %pad_add_fusion.place_ref, bf16[768,512]{1,0:T(8,128)(2,1)S(1)} %get-tuple-element.53.q_ref, bf16[768,512]{1,0:T(8,128)(2,1)S(1)} %get-tuple-element.54.k_ref, bf16[768,512]{1,0:T(8,128)(2,1)S(1)} %get-tuple-element.55.v_ref, ...), custom_call_target="tpu_custom_call" | custom-call | flops 4000000000 | bytes 4000000 | tf_op jit(solution)/shard_map/query_gradients/pallas_call | solution.py:437
  135.1 0.0 collective-permute-done.5.high_ref
  135.1 0.0 collective-permute-done.4.low_ref
  135.1 0.6 loss_over_node.1
  135.8 3.8 %collective-permute-start.6 = (f32[8,128]{1,0:T(8,128)S(1)}, f32[8,128]{1,0:T(8,128)S(1)}, u32[]{:S(2)}, u32[]{:S(2)}) collective-permute-start(f32[8,128]{1,0:T(8,128)S(1)} %loss_over_node.1), channel_id=1, source_target_pairs={{0,0},{1,1},{2,2},{3,3},{4,4},{5,5},{6,6},{7,7},{8,8},{9,9},{10,10... | collective-permute-start | bytes 12296 | tf_op jit(solution)/shard_map/loss_over_node/ppermute | solution.py:593
  139.6 6.8 %backward.1.qkv_grad_ref = bf16[256,1536]{1,0:T(8,128)(2,1)S(1)} custom-call(s32[4]{0:T(128)S(1)} %pad_add_fusion.place_ref, bf16[256,128]{1,0:T(8,128)(2,1)S(1)} %collective-permute-done.4.low_ref, bf16[256,128]{1,0:T(8,128)(2,1)S(1)} %collective-permute-done.5.high_ref, bf16[128,1024]{1,0:T(8,128)(2,1)S(1)} %pad.8.decoder_ref, ...), custom_call_target="tpu_custom_call" | custom-call | flops 4000000000 | bytes 4000000 | tf_op jit(solution)/shard_map/backward/pallas_call | solution.py:437
  146.3 0.0 collective-permute-done.6.loss_ref
  146.4 3.1 %hidden_gradient.1 = (f32[256,1024]{1,0:T(8,128)}, bf16[16,80,256]{2,1,0:T(8,128)(2,1)S(1)}) custom-call(s32[4]{0:T(128)S(1)} %pad_add_fusion.place_ref, bf16[256,1536]{1,0:T(8,128)(2,1)S(1)} %backward.1.qkv_grad_ref, bf16[16,32,2048]{2,1,0:T(8,128)(2,1)S(1)} %bitcast.19, bf16[16,32,2048]{2,1,0:T(8,128)(2,1)S(1)} %collective-permute-done.3.wb_ref, ...), custom_call_target="tpu_custom_call" | custom-call | flops 1000000000 | bytes 4000000 | tf_op jit(solution)/shard_map/hidden_gradient/pallas_call | solution.py:437
  149.5 26.4 %all_to_all.33.received_ref = bf16[16,80,256]{2,1,0:T(8,128)(2,1)S(1)} all-to-all(bf16[16,80,256]{2,1,0:T(8,128)(2,1)S(1)} %get-tuple-element.63), channel_id=1, replica_groups=mesh['y'=4,'xl'=2,'c'=2,'z'=16,'xh'=2] {'y','xl','c'}, dimensions={0} | all-to-all | bytes 1310720 | tf_op jit(solution)/shard_map/latent_gradient_over_member/all_to_all | solution.py:616
  175.9 0.7 finish.1
  176.6 0.5 slice.11
  (4 shorter events, 0.1 us)
Async XLA Ops:
  0.6 1.6 copy-start
  0.6 14.7 %copy-start.10 = (bf16[16,1024]{1,0:T(8,128)(2,1)S(1)}, bf16[16,1024]{1,0:T(8,128)(2,1)}, u32[]{:S(2)}) copy-start(bf16[16,1024]{1,0:T(8,128)(2,1)} %param.13) | copy-start | bytes 98308
  0.7 14.7 %copy-start.9 = (bf16[32,1536]{1,0:T(8,128)(2,1)S(1)}, bf16[32,1536]{1,0:T(8,128)(2,1)}, u32[]{:S(2)}) copy-start(bf16[32,1536]{1,0:T(8,128)(2,1)} %param.12) | copy-start | bytes 294916
  0.7 26.8 %copy-start.1 = (bf16[1,256,1024]{2,1,0:T(8,128)(2,1)S(1)}, bf16[1,256,1024]{2,1,0:T(8,128)(2,1)}, u32[]{:S(2)}) copy-start(bf16[1,256,1024]{2,1,0:T(8,128)(2,1)} %param.10) | copy-start | bytes 1572868
  5.1 22.4 %all-to-all-start = ((bf16[16,64,256]{2,1,0:T(8,128)(2,1)}), bf16[16,64,256]{2,1,0:T(8,128)(2,1)S(1)}, u32[]{:S(2)}, u32[]{:S(2)}) async-start(bf16[16,64,256]{2,1,0:T(8,128)(2,1)} %broadcast_in_dim.37), calls=%async_computation | async-start | bytes 1048576 | tf_op jit(solution)/shard_map/latent_over_member/all_to_all | solution.py:525
  15.4 15.3 %collective-permute-start = (bf16[32,2048]{1,0:T(8,128)(2,1)S(1)}, bf16[32,2048]{1,0:T(8,128)(2,1)S(1)}, u32[]{:S(2)}, u32[]{:S(2)}) collective-permute-start(bf16[32,2048]{1,0:T(8,128)(2,1)S(1)} %maximum_maximum_fusion), channel_id=1, source_target_pairs={{0,0},{1,1},{64,2},{65,3},{128,4},{129,5},{192,6},{193,7},{256,8},... | collective-permute-start | bytes 393224 | tf_op jit(solution)/shard_map/weights_over_node/ppermute | solution.py:512
  28.1 16.2 %copy-start.3 = (bf16[256,1024]{1,0:T(8,128)(2,1)}, bf16[256,1024]{1,0:T(8,128)(2,1)S(1)}, u32[]{:S(2)}) copy-start(bf16[256,1024]{1,0:T(8,128)(2,1)S(1)} %get-tuple-element.40.own_ref) | copy-start | bytes 1572868
  44.3 44.2 %copy-start.2 = (s32[256]{0:T(256)S(1)}, s32[256]{0:T(256)}, u32[]{:S(2)}) copy-start(s32[256]{0:T(256)} %param.17) | copy-start | bytes 3076
  44.3 38.1 %all-to-all-start.2 = ((bf16[4,128,2048]{2,1,0:T(8,128)(2,1)}), bf16[4,128,2048]{2,1,0:T(8,128)(2,1)S(1)}, u32[]{:S(2)}, u32[]{:S(2)}) async-start(bf16[4,128,2048]{2,1,0:T(8,128)(2,1)} %broadcast_in_dim.40), calls=%async_computation.2 | async-start | bytes 4194304 | tf_op jit(solution)/shard_map/weights_over_y/all_to_all | solution.py:542
  54.4 16.4 %collective-permute-start.2 = (bf16[256,1024]{1,0:T(8,128)(2,1)}, bf16[256,1024]{1,0:T(8,128)(2,1)S(1)}, u32[]{:S(2)}, u32[]{:S(2)}) collective-permute-start(bf16[256,1024]{1,0:T(8,128)(2,1)} %copy-done.3), channel_id=1, source_target_pairs={{1,0},{2,1},{3,2},{4,3},{5,4},{6,5},{7,6},{8,7},{9,8},{10,9},{11,1... | collective-permute-start | bytes 1572872 | tf_op jit(solution)/shard_map/normed_halo/ppermute | solution.py:452
  55.7 25.9 %collective-permute-start.1 = (bf16[256,1024]{1,0:T(8,128)(2,1)}, bf16[256,1024]{1,0:T(8,128)(2,1)S(1)}, u32[]{:S(2)}, u32[]{:S(2)}) collective-permute-start(bf16[256,1024]{1,0:T(8,128)(2,1)} %copy-done.3), channel_id=1, source_target_pairs={{0,1},{1,2},{2,3},{3,4},{4,5},{5,6},{6,7},{7,8},{8,9},{9,10},{10,1... | collective-permute-start | bytes 1572872 | tf_op jit(solution)/shard_map/normed_halo/ppermute | solution.py:451
  70.8 0.8 copy-start.5
  81.6 0.8 copy-start.7
  82.4 6.2 %collective-permute-start.3 = (bf16[16,32,2048]{2,1,0:T(8,128)(2,1)S(1)}, bf16[16,32,2048]{2,1,0:T(8,128)(2,1)S(1)}, u32[]{:S(2)}, u32[]{:S(2)}) collective-permute-start(bf16[16,32,2048]{2,1,0:T(8,128)(2,1)S(1)} %bitcast.15), channel_id=1, source_target_pairs={{0,32},{32,0},{1,33},{33,1},{2,34},{34,2},{3,35},{35,3},{4,36},{36... | collective-permute-start | bytes 6291464 | tf_op jit(solution)/shard_map/weights_over_core/ppermute | solution.py:546
  88.6 1.0 copy-start.4
  89.6 1.0 copy-start.6
  90.6 1.0 copy-start.8
  122.7 12.5 %collective-permute-start.5 = (bf16[256,128]{1,0:T(8,128)(2,1)S(1)}, bf16[256,128]{1,0:T(8,128)(2,1)S(1)}, u32[]{:S(2)}, u32[]{:S(2)}) collective-permute-start(bf16[256,128]{1,0:T(8,128)(2,1)S(1)} %get-tuple-element.52), channel_id=1, source_target_pairs={{1,0},{2,1},{3,2},{4,3},{5,4},{6,5},{7,6},{8,7},{9,8},{10,9},{11,1... | collective-permute-start | bytes 196616 | tf_op jit(solution)/shard_map/gradient_halo/ppermute | solution.py:452
  124.0 11.2 %collective-permute-start.4 = (bf16[256,128]{1,0:T(8,128)(2,1)S(1)}, bf16[256,128]{1,0:T(8,128)(2,1)S(1)}, u32[]{:S(2)}, u32[]{:S(2)}) collective-permute-start(bf16[256,128]{1,0:T(8,128)(2,1)S(1)} %get-tuple-element.52), channel_id=1, source_target_pairs={{0,1},{1,2},{2,3},{3,4},{4,5},{5,6},{6,7},{7,8},{8,9},{9,10},{10,1... | collective-permute-start | bytes 196616 | tf_op jit(solution)/shard_map/gradient_halo/ppermute | solution.py:451
  135.8 10.6 %collective-permute-start.6 = (f32[8,128]{1,0:T(8,128)S(1)}, f32[8,128]{1,0:T(8,128)S(1)}, u32[]{:S(2)}, u32[]{:S(2)}) collective-permute-start(f32[8,128]{1,0:T(8,128)S(1)} %loss_over_node.1), channel_id=1, source_target_pairs={{0,0},{1,1},{2,2},{3,3},{4,4},{5,5},{6,6},{7,7},{8,8},{9,9},{10,10... | collective-permute-start | bytes 12296 | tf_op jit(solution)/shard_map/loss_over_node/ppermute | solution.py:593

commit v3 on v2

--- a/solution.py
+++ b/solution.py
@@ -19,7 +19,7 @@
 LANES = 128
 MEMBERS = 16
 SLOT = ROWS // MEMBERS
-TILE = 128
+TILE = 256
 WINDOW = TILE + 2 * HALF
 LOSS_LANE = 122
 REACH_LANE = 125
@@ -68,13 +68,20 @@
     return jnp.concatenate(parts, axis=1)
 
 
+def head_means(value, segments):
+    rounded = value.astype(bf16)
+    return jnp.concatenate(
+        [mm(rounded[:, start : start + BLOCK], segments) for start in range(0, INNER, BLOCK)], axis=1
+    )
+
+
 def lane_index(rows, lanes):
     return lax.broadcasted_iota(jnp.int32, (rows, lanes), 1)
 
 
 def norm_kernel(lat_ref, pert_ref, gain_ref, normed_ref, latent_ref):
     gain = gain_ref[...].astype(f32)
-    for part in range(2):
+    for part in range(ROWS // TILE):
         rows = slice(part * TILE, (part + 1) * TILE)
         lat = lat_ref[:, rows].astype(f32).T
         latent_ref[rows, :] = lat.astype(bf16)
@@ -107,20 +114,23 @@
 
 
 def forward_kernel(
-    place_ref, low_ref, own_ref, high_ref, wa_ref, wb_ref, latent_ref, pert_ref, reach_ref, decoder_ref,
+    place_ref, normed_ref, wa_ref, wb_ref, latent_ref, pert_ref, reach_ref, decoder_ref,
     q_ref, k_ref, v_ref, unit_ref, factor_ref, mixed_ref, total_ref, forecast_ref,
     bias_ref, mixed_low_ref,
 ):
     row_start = place_ref[0]
     segments = segment_matrix(1.0 / HEAD)
     near, far = core_halves(place_ref, INNER)
-    for block, normed_ref in enumerate((low_ref, own_ref, high_ref)):
+    for block in range(3):
         rows = slice(block * ROWS, (block + 1) * ROWS)
-        left, right = normed_ref[:, near], normed_ref[:, far]
+        left, right = normed_ref[rows, near], normed_ref[rows, far]
+        together = mm(left, wa_ref[:, :, : 3 * INNER].reshape(INNER, 3 * INNER)) + mm(
+            right, wb_ref[:, :, : 3 * INNER].reshape(INNER, 3 * INNER)
+        )
         for part, out_ref in enumerate((q_ref, k_ref, v_ref)):
-            projected = mm(left, qkv_weights(wa_ref, part)) + mm(right, qkv_weights(wb_ref, part))
+            projected = together[:, part * INNER : (part + 1) * INNER]
             if part < 2:
-                factor = lax.rsqrt(head_sums(projected * projected, segments) + head_epsilon)
+                factor = lax.rsqrt(head_means(projected * projected, segments) + head_epsilon)
                 unit = projected * factor
                 if block == 1:
                     unit_ref[:, part * INNER : (part + 1) * INNER] = unit
@@ -129,7 +139,7 @@
             out_ref[rows, :] = projected.astype(bf16)
 
     column = column_of(reach_ref)
-    for tile in range(2):
+    for tile in range(ROWS // TILE):
         offset = (
             lane_index(TILE, WINDOW)
             - HALF
@@ -144,7 +154,7 @@
 
     for pair in range(HEADS // 2):
         lanes = slice(pair * LANES, (pair + 1) * LANES)
-        for tile in range(2):
+        for tile in range(ROWS // TILE):
             rows = slice(tile * TILE, (tile + 1) * TILE)
             window = slice(tile * TILE, tile * TILE + WINDOW)
             queries = q_ref[ROWS + tile * TILE : ROWS + (tile + 1) * TILE, lanes]
@@ -283,7 +293,7 @@
 ):
     row_start = place_ref[0]
     column = column_of(reach_ref)
-    for tile in range(2):
+    for tile in range(ROWS // TILE):
         offset = (
             lane_index(TILE, WINDOW)
             - HALF
@@ -297,7 +307,7 @@
 
     for pair in range(HEADS // 2):
         lanes = slice(pair * LANES, (pair + 1) * LANES)
-        for tile in range(2):
+        for tile in range(ROWS // TILE):
             rows = slice(tile * TILE, (tile + 1) * TILE)
             window = slice(tile * TILE, tile * TILE + WINDOW)
             queries = q_ref[ROWS + tile * TILE : ROWS + (tile + 1) * TILE, lanes]
@@ -341,7 +351,7 @@
         all_scaled[rows, :] = scaled
         gradient_operands(scaled, mm(message, expand_dot), all_g0, all_g1, rows)
 
-    for tile in range(2):
+    for tile in range(ROWS // TILE):
         offset = (
             HALF
             + lax.broadcasted_iota(jnp.int32, (TILE, WINDOW), 0)
@@ -354,7 +364,7 @@
     for pair in range(HEADS // 2):
         lanes = slice(pair * LANES, (pair + 1) * LANES)
         value_lanes = slice(INNER + pair * LANES, INNER + (pair + 1) * LANES)
-        for tile in range(2):
+        for tile in range(ROWS // TILE):
             rows = slice(tile * TILE, (tile + 1) * TILE)
             window = slice(tile * TILE, tile * TILE + WINDOW)
             keys = k_ref[ROWS + tile * TILE : ROWS + (tile + 1) * TILE, lanes]
@@ -377,7 +387,7 @@
     for part, grad in ((0, qgrad_ref[...]), (1, kv_ref[:, :INNER])):
         columns = slice(part * INNER, (part + 1) * INNER)
         unit = unit_ref[:, columns]
-        along = head_sums(grad * unit, segments)
+        along = head_means(grad * unit, segments)
         qkv_grad_ref[:, columns] = (factor_ref[:, columns] * (grad - unit * along)).astype(bf16)
     qkv_grad_ref[:, 2 * INNER :] = kv_ref[:, INNER:].astype(bf16)
 
@@ -394,7 +404,7 @@
             + mm_t(parts[2], qkv_weights(w_ref, 2))
         )
     gain = gain_ref[...].astype(f32)
-    for part in range(2):
+    for part in range(ROWS // TILE):
         rows = slice(part * TILE, (part + 1) * TILE)
         hidden = latent_ref[rows, :].astype(f32) + pert_ref[rows, :].astype(f32)
         centred = hidden - jnp.mean(hidden, axis=1, keepdims=True)
@@ -542,6 +552,8 @@
         wa = lax.all_to_all(jnp.broadcast_to(row[None], (4,) + row.shape), "y", 0, 0, tiled=True)
         wa = wa.reshape(16, 32, PACKED)
     wa, normed_low, normed_high = lax.optimization_barrier((wa, normed_low, normed_high))
+    with jax.named_scope("normed_rows"):
+        normed_all = jnp.concatenate([normed_low, normed, normed_high], axis=0)
     with jax.named_scope("weights_over_core"):
         wb = lax.ppermute(wa, "c", [(0, 1), (1, 0)])
     with jax.named_scope("forward"):
@@ -554,7 +566,7 @@
             [((2, TILE, WINDOW), f32), ((ROWS, INNER), bf16)],
             40,
             4_000_000_000,
-            place, normed_low, normed, normed_high, wa, wb, latent_own, pert, reach_row, decoder,
+            place, normed_all, wa, wb, latent_own, pert, reach_row, decoder,
         )
     with jax.named_scope("forecasts_over_member"):
         forecasts = lax.all_to_all(

time: 180 us -> 174 us (0.967)
  Pallas kernels: 27.5 us -> 24.1 us
  local copies, waits for them, and re-layouts: 10.4 us -> 7.28 us
  waiting for transfers between devices: 25.9 us -> 23 us
  starting transfers between devices: 53.4 us -> 55.2 us
    pallas_call x9, Pallas kernels: 27.5 us -> 24.1 us  [call(): pl.pallas_call(body, out_shape=tuple((jax.ShapeDtypeStruct(shape, kind) f...]
    unnamed x23 -> x15, local copies, waits for them, and re-layouts: 4.81 us -> 1.66 us
  transfers between devices with their start and end apart: 9 -> 9, of which waited for: 4 -> 4; matrix products, arithmetic and copies ran while one was open for 0% -> 1% of each run, Pallas kernels for 7% -> 6%
where the time goes in v3:
time: 174 us; the launch traced here: 173 us
  blocking collectives  58.8 us (34%)
  starting transfers between devices  55.2 us (32%)
  Pallas kernels  24.1 us (14%)
  waiting for transfers between devices  23 us (13%)
  local copies, waits for them, and re-layouts  7.28 us (4%)
  between operations  2.65 us (2%)
  other arithmetic  2.32 us (1%)
    all_to_all x1, blocking collectives, shards(): received = lax.all_to_all(send, MEMBER, 0, 0, tiled=True)  27.1 us
    pallas_call x9, Pallas kernels, call(): pl.pallas_call(body, out_shape=tuple((jax.ShapeDtypeStruct(shape, kind) f...  24.1 us
    ppermute x2, starting transfers between devices, both_ways(): low = lax.ppermute(block, NODE, [(i, i + 1) for i in range(count - 1)])  13 us
    ppermute x1, starting transfers between devices, shards(): mine = lax.ppermute(packed, EVERY, weight_route())  12.1 us
    all_to_all x1, blocking collectives, shards(): lax.all_to_all(jnp.broadcast_to(mine[None], (4,) + mine.shape), ('xl', 'x...  12 us
    all_to_all x1, blocking collectives, shards(): lax.all_to_all(forecast.reshape(MEMBERS, SLOT, LANES), MEMBER, 0, 0, tile...  10.8 us
    all_to_all x1, starting transfers between devices, shards(): lax.all_to_all(latent_copies, MEMBER, 0, 0, tiled=True).reshape(WIDTH, ROWS)  10.2 us
    ppermute x2, waiting for transfers between devices, both_ways(): low = lax.ppermute(block, NODE, [(i, i + 1) for i in range(count - 1)])  9.99 us
  transfers between devices with their start and end apart: 9, of which 4 were waited for; matrix products, arithmetic and copies ran while one was open for 1% of the time, Pallas kernels for 6%

profile of v3, /device:TPU:1, one launch (start us, length us, event | category | flops | bytes accessed | tf_op | source)
XLA Modules:
  0.0 173.3 jit_solution(5004191518297975358)
XLA Ops:
  0.6 0.0 copy-start
  0.6 0.0 copy-start.6
  0.7 0.0 copy-start.5
  0.7 0.0 copy-start.1
  0.7 0.8 broadcast_in_dim.36.gain_ref
  1.4 0.8 multiply_subtract_fusion
  2.2 0.0 copy-done
  2.2 0.1 constant_dynamic-slice_fusion
  2.3 0.1 copy.13
  2.4 1.0 pad.8.decoder_ref
  3.3 0.1 pad_add_fusion.place_ref
  3.4 0.1 broadcast_in_dim.17.area_ref
  3.5 1.6 broadcast_in_dim.37
  5.1 10.2 %all-to-all-start = ((bf16[16,64,256]{2,1,0:T(8,128)(2,1)}), bf16[16,64,256]{2,1,0:T(8,128)(2,1)S(1)}, u32[]{:S(2)}, u32[]{:S(2)}) async-start(bf16[16,64,256]{2,1,0:T(8,128)(2,1)} %broadcast_in_dim.37), calls=%async_computation | async-start | bytes 1048576 | tf_op jit(solution)/shard_map/latent_over_member/all_to_all | solution.py:535
  15.3 0.0 copy-done.6
  15.3 0.0 copy-done.5
  15.4 12.1 %collective-permute-start = (bf16[32,2048]{1,0:T(8,128)(2,1)S(1)}, bf16[32,2048]{1,0:T(8,128)(2,1)S(1)}, u32[]{:S(2)}, u32[]{:S(2)}) collective-permute-start(bf16[32,2048]{1,0:T(8,128)(2,1)S(1)} %maximum_maximum_fusion), channel_id=1, source_target_pairs={{0,0},{1,1},{64,2},{65,3},{128,4},{129,5},{192,6},{193,7},{256,8},... | collective-permute-start | bytes 393224 | tf_op jit(solution)/shard_map/weights_over_node/ppermute | solution.py:522
  27.5 0.0 all-to-all-done
  27.5 0.0 copy-done.1
  27.5 0.5 layer_norm.1
  28.0 0.0 copy-start.2
  28.0 0.8 copy-done.2
  28.8 1.9 %collective-permute-done = bf16[32,2048]{1,0:T(8,128)(2,1)S(1)} collective-permute-done((bf16[32,2048]{1,0:T(8,128)(2,1)S(1)}, bf16[32,2048]{1,0:T(8,128)(2,1)S(1)}, u32[]{:S(2)}, u32[]{:S(2)}) %collective-permute-start) | collective-permute-done | bytes 131104 | tf_op jit(solution)/shard_map/weights_over_node/ppermute | solution.py:522
  30.8 12.0 %all_to_all.30 = bf16[4,32,2048]{2,1,0:T(8,128)(2,1)S(1)} all-to-all(bf16[4,32,2048]{2,1,0:T(8,128)(2,1)S(1)} %broadcast_in_dim.38), channel_id=1, replica_groups=mesh['y'=4,'xl'=2,'c'=2,'z'=16,'xh'=2] {'xl','xh'}, dimensions={0} | all-to-all | bytes 1048576 | tf_op jit(solution)/shard_map/weights_over_x/all_to_all | solution.py:549
  42.7 1.6 broadcast_in_dim.40
  44.3 10.0 %all-to-all-start.2 = ((bf16[4,128,2048]{2,1,0:T(8,128)(2,1)}), bf16[4,128,2048]{2,1,0:T(8,128)(2,1)S(1)}, u32[]{:S(2)}, u32[]{:S(2)}) async-start(bf16[4,128,2048]{2,1,0:T(8,128)(2,1)} %broadcast_in_dim.40), calls=%async_computation.2 | async-start | bytes 4194304 | tf_op jit(solution)/shard_map/weights_over_y/all_to_all | solution.py:552
  54.3 0.0 copy-start.3
  54.3 1.4 collective-permute-start.2
  55.7 6.3 %collective-permute-start.1 = (bf16[256,1024]{1,0:T(8,128)(2,1)}, bf16[256,1024]{1,0:T(8,128)(2,1)}, u32[]{:S(2)}, u32[]{:S(2)}) collective-permute-start(bf16[256,1024]{1,0:T(8,128)(2,1)} %copy-done.2), channel_id=1, source_target_pairs={{0,1},{1,2},{2,3},{3,4},{4,5},{5,6},{6,7},{7,8},{8,9},{9,10},{10,1... | collective-permute-start | bytes 1572872 | tf_op jit(solution)/shard_map/normed_halo/ppermute | solution.py:461
  62.0 8.8 %collective-permute-done.2 = bf16[256,1024]{1,0:T(8,128)(2,1)S(1)} collective-permute-done((bf16[256,1024]{1,0:T(8,128)(2,1)}, bf16[256,1024]{1,0:T(8,128)(2,1)S(1)}, u32[]{:S(2)}, u32[]{:S(2)}) %collective-permute-start.2) | collective-permute-done | bytes 524320 | tf_op jit(solution)/shard_map/normed_halo/ppermute | solution.py:462
  70.8 0.0 copy-start.4
  70.8 0.8 copy-done.4
  71.6 10.0 %collective-permute-done.1 = bf16[256,1024]{1,0:T(8,128)(2,1)} collective-permute-done((bf16[256,1024]{1,0:T(8,128)(2,1)}, bf16[256,1024]{1,0:T(8,128)(2,1)}, u32[]{:S(2)}, u32[]{:S(2)}) %collective-permute-start.1) | collective-permute-done | bytes 524320 | tf_op jit(solution)/shard_map/normed_halo/ppermute | solution.py:461
  81.6 0.0 all-to-all-done.2
  81.6 2.4 %collective-permute-start.3 = (bf16[16,32,2048]{2,1,0:T(8,128)(2,1)S(1)}, bf16[16,32,2048]{2,1,0:T(8,128)(2,1)S(1)}, u32[]{:S(2)}, u32[]{:S(2)}) collective-permute-start(bf16[16,32,2048]{2,1,0:T(8,128)(2,1)S(1)} %bitcast.15), channel_id=1, source_target_pairs={{0,32},{32,0},{1,33},{33,1},{2,34},{34,2},{3,35},{35,3},{4,36},{36... | collective-permute-start | bytes 6291464 | tf_op jit(solution)/shard_map/weights_over_core/ppermute | solution.py:558
  84.0 1.5 pad_maximum_fusion.normed_ref
  85.5 2.3 %collective-permute-done.3.wb_ref = bf16[16,32,2048]{2,1,0:T(8,128)(2,1)S(1)} collective-permute-done((bf16[16,32,2048]{2,1,0:T(8,128)(2,1)S(1)}, bf16[16,32,2048]{2,1,0:T(8,128)(2,1)S(1)}, u32[]{:S(2)}, u32[]{:S(2)}) %collective-permute-start.3) | collective-permute-done | bytes 2097184 | tf_op jit(solution)/shard_map/weights_over_core/ppermute | solution.py:558
  87.7 0.0 copy-done.3
  87.7 6.7 %forward.1 = (bf16[768,512]{1,0:T(8,128)(2,1)S(1)}, bf16[768,512]{1,0:T(8,128)(2,1)S(1)}, bf16[768,512]{1,0:T(8,128)(2,1)S(1)}, f32[256,1024]{1,0:T(8,128)S(1)},...) custom-call(s32[4]{0:T(128)S(1)} %pad_add_fusion.place_ref, ...), custom_call_target="tpu_custom_call" | custom-call | flops 4000000000 | bytes 4000000 | tf_op jit(solution)/shard_map/forward/pallas_call | solution.py:447
  94.5 10.8 %all_to_all.31.forecast_ref = f32[16,16,128]{2,1,0:T(8,128)S(1)} all-to-all(f32[16,16,128]{2,1,0:T(8,128)S(1)} %bitcast.25), channel_id=1, replica_groups=mesh['y'=4,'xl'=2,'c'=2,'z'=16,'xh'=2] {'y','xl','c'}, dimensions={0} | all-to-all | bytes 262144 | tf_op jit(solution)/shard_map/forecasts_over_member/all_to_all | solution.py:572
  105.3 0.7 score.1
  106.0 8.9 %all_to_all.32 = bf16[16,16,128]{2,1,0:T(8,128)(2,1)S(1)} all-to-all(bf16[16,16,128]{2,1,0:T(8,128)(2,1)S(1)} %score.1), channel_id=1, replica_groups=mesh['y'=4,'xl'=2,'c'=2,'z'=16,'xh'=2] {'y','xl','c'}, dimensions={0} | all-to-all | bytes 131072 | tf_op jit(solution)/shard_map/gradients_over_member/all_to_all | solution.py:580
  114.9 2.1 %upstream.1 = (f32[256,1024]{1,0:T(8,128)S(1)}, bf16[256,512]{1,0:T(8,128)(2,1)S(1)}, bf16[256,512]{1,0:T(8,128)(2,1)S(1)}, bf16[256,512]{1,0:T(8,128)(2,1)S(1)}...) custom-call(s32[4]{0:T(128)S(1)} %pad_add_fusion.place_ref, bf16[256,128]{1,0:T(8,128)(2,1)S(1)} %bitcast.24, ...), custom_call_target="tpu_custom_call" | custom-call | flops 500000000 | bytes 4000000 | tf_op jit(solution)/shard_map/upstream/pallas_call | solution.py:447
  117.0 1.3 collective-permute-start.5
  118.3 6.7 %collective-permute-start.4 = (bf16[256,128]{1,0:T(8,128)(2,1)S(1)}, bf16[256,128]{1,0:T(8,128)(2,1)S(1)}, u32[]{:S(2)}, u32[]{:S(2)}) collective-permute-start(bf16[256,128]{1,0:T(8,128)(2,1)S(1)} %get-tuple-element.52), channel_id=1, source_target_pairs={{0,1},{1,2},{2,3},{3,4},{4,5},{5,6},{6,7},{7,8},{8,9},{9,10},{10,1... | collective-permute-start | bytes 196616 | tf_op jit(solution)/shard_map/gradient_halo/ppermute | solution.py:461
  125.0 3.5 %query_gradients.1.qgrad_ref = f32[256,512]{1,0:T(8,128)S(1)} custom-call(s32[4]{0:T(128)S(1)} %pad_add_fusion.place_ref, bf16[768,512]{1,0:T(8,128)(2,1)S(1)} %get-tuple-element.53.q_ref, bf16[768,512]{1,0:T(8,128)(2,1)S(1)} %get-tuple-element.54.k_ref, bf16[768,512]{1,0:T(8,128)(2,1)S(1)} %get-tuple-element.55.v_ref, ...), custom_call_target="tpu_custom_call" | custom-call | flops 4000000000 | bytes 4000000 | tf_op jit(solution)/shard_map/query_gradients/pallas_call | solution.py:447
  128.6 0.0 collective-permute-done.5.high_ref
  128.6 0.0 collective-permute-done.4.low_ref
  128.6 0.6 loss_over_node.1
  129.2 4.8 %collective-permute-start.6 = (f32[8,128]{1,0:T(8,128)S(1)}, f32[8,128]{1,0:T(8,128)S(1)}, u32[]{:S(2)}, u32[]{:S(2)}) collective-permute-start(f32[8,128]{1,0:T(8,128)S(1)} %loss_over_node.1), channel_id=1, source_target_pairs={{0,0},{1,1},{2,2},{3,3},{4,4},{5,5},{6,6},{7,7},{8,8},{9,9},{10,10... | collective-permute-start | bytes 12296 | tf_op jit(solution)/shard_map/loss_over_node/ppermute | solution.py:605
  134.0 6.2 %backward.1.qkv_grad_ref = bf16[256,1536]{1,0:T(8,128)(2,1)S(1)} custom-call(s32[4]{0:T(128)S(1)} %pad_add_fusion.place_ref, bf16[256,128]{1,0:T(8,128)(2,1)S(1)} %collective-permute-done.4.low_ref, bf16[256,128]{1,0:T(8,128)(2,1)S(1)} %collective-permute-done.5.high_ref, bf16[128,1024]{1,0:T(8,128)(2,1)S(1)} %pad.8.decoder_ref, ...), custom_call_target="tpu_custom_call" | custom-call | flops 4000000000 | bytes 4000000 | tf_op jit(solution)/shard_map/backward/pallas_call | solution.py:447
  140.2 0.0 collective-permute-done.6.loss_ref
  140.2 3.1 %hidden_gradient.1 = (f32[256,1024]{1,0:T(8,128)}, bf16[16,80,256]{2,1,0:T(8,128)(2,1)S(1)}) custom-call(s32[4]{0:T(128)S(1)} %pad_add_fusion.place_ref, bf16[256,1536]{1,0:T(8,128)(2,1)S(1)} %backward.1.qkv_grad_ref, bf16[16,32,2048]{2,1,0:T(8,128)(2,1)S(1)} %bitcast.19, bf16[16,32,2048]{2,1,0:T(8,128)(2,1)S(1)} %collective-permute-done.3.wb_ref, ...), custom_call_target="tpu_custom_call" | custom-call | flops 1000000000 | bytes 4000000 | tf_op jit(solution)/shard_map/hidden_gradient/pallas_call | solution.py:447
  143.3 27.1 %all_to_all.33.received_ref = bf16[16,80,256]{2,1,0:T(8,128)(2,1)S(1)} all-to-all(bf16[16,80,256]{2,1,0:T(8,128)(2,1)S(1)} %get-tuple-element.63), channel_id=1, replica_groups=mesh['y'=4,'xl'=2,'c'=2,'z'=16,'xh'=2] {'y','xl','c'}, dimensions={0} | all-to-all | bytes 1310720 | tf_op jit(solution)/shard_map/latent_gradient_over_member/all_to_all | solution.py:628
  170.3 0.7 finish.1
  171.1 0.5 slice.11
  (4 shorter events, 0.1 us)
Async XLA Ops:
  0.6 1.6 copy-start
  0.6 14.7 %copy-start.6 = (bf16[16,1024]{1,0:T(8,128)(2,1)S(1)}, bf16[16,1024]{1,0:T(8,128)(2,1)}, u32[]{:S(2)}) copy-start(bf16[16,1024]{1,0:T(8,128)(2,1)} %param.13) | copy-start | bytes 98308
  0.7 14.7 %copy-start.5 = (bf16[32,1536]{1,0:T(8,128)(2,1)S(1)}, bf16[32,1536]{1,0:T(8,128)(2,1)}, u32[]{:S(2)}) copy-start(bf16[32,1536]{1,0:T(8,128)(2,1)} %param.12) | copy-start | bytes 294916
  0.7 26.8 %copy-start.1 = (bf16[1,256,1024]{2,1,0:T(8,128)(2,1)S(1)}, bf16[1,256,1024]{2,1,0:T(8,128)(2,1)}, u32[]{:S(2)}) copy-start(bf16[1,256,1024]{2,1,0:T(8,128)(2,1)} %param.10) | copy-start | bytes 1572868
  5.1 22.4 %all-to-all-start = ((bf16[16,64,256]{2,1,0:T(8,128)(2,1)}), bf16[16,64,256]{2,1,0:T(8,128)(2,1)S(1)}, u32[]{:S(2)}, u32[]{:S(2)}) async-start(bf16[16,64,256]{2,1,0:T(8,128)(2,1)} %broadcast_in_dim.37), calls=%async_computation | async-start | bytes 1048576 | tf_op jit(solution)/shard_map/latent_over_member/all_to_all | solution.py:535
  15.4 15.3 %collective-permute-start = (bf16[32,2048]{1,0:T(8,128)(2,1)S(1)}, bf16[32,2048]{1,0:T(8,128)(2,1)S(1)}, u32[]{:S(2)}, u32[]{:S(2)}) collective-permute-start(bf16[32,2048]{1,0:T(8,128)(2,1)S(1)} %maximum_maximum_fusion), channel_id=1, source_target_pairs={{0,0},{1,1},{64,2},{65,3},{128,4},{129,5},{192,6},{193,7},{256,8},... | collective-permute-start | bytes 393224 | tf_op jit(solution)/shard_map/weights_over_node/ppermute | solution.py:522
  28.0 0.8 copy-start.2
  44.3 37.3 %all-to-all-start.2 = ((bf16[4,128,2048]{2,1,0:T(8,128)(2,1)}), bf16[4,128,2048]{2,1,0:T(8,128)(2,1)S(1)}, u32[]{:S(2)}, u32[]{:S(2)}) async-start(bf16[4,128,2048]{2,1,0:T(8,128)(2,1)} %broadcast_in_dim.40), calls=%async_computation.2 | async-start | bytes 4194304 | tf_op jit(solution)/shard_map/weights_over_y/all_to_all | solution.py:552
  54.3 33.5 %copy-start.3 = (s32[256]{0:T(256)S(1)}, s32[256]{0:T(256)}, u32[]{:S(2)}) copy-start(s32[256]{0:T(256)} %param.17) | copy-start | bytes 3076
  54.3 16.5 %collective-permute-start.2 = (bf16[256,1024]{1,0:T(8,128)(2,1)}, bf16[256,1024]{1,0:T(8,128)(2,1)S(1)}, u32[]{:S(2)}, u32[]{:S(2)}) collective-permute-start(bf16[256,1024]{1,0:T(8,128)(2,1)} %copy-done.2), channel_id=1, source_target_pairs={{1,0},{2,1},{3,2},{4,3},{5,4},{6,5},{7,6},{8,7},{9,8},{10,9},{11,1... | collective-permute-start | bytes 1572872 | tf_op jit(solution)/shard_map/normed_halo/ppermute | solution.py:462
  55.7 25.9 %collective-permute-start.1 = (bf16[256,1024]{1,0:T(8,128)(2,1)}, bf16[256,1024]{1,0:T(8,128)(2,1)}, u32[]{:S(2)}, u32[]{:S(2)}) collective-permute-start(bf16[256,1024]{1,0:T(8,128)(2,1)} %copy-done.2), channel_id=1, source_target_pairs={{0,1},{1,2},{2,3},{3,4},{4,5},{5,6},{6,7},{7,8},{8,9},{9,10},{10,1... | collective-permute-start | bytes 1572872 | tf_op jit(solution)/shard_map/normed_halo/ppermute | solution.py:461
  70.8 0.8 copy-start.4
  81.6 6.2 %collective-permute-start.3 = (bf16[16,32,2048]{2,1,0:T(8,128)(2,1)S(1)}, bf16[16,32,2048]{2,1,0:T(8,128)(2,1)S(1)}, u32[]{:S(2)}, u32[]{:S(2)}) collective-permute-start(bf16[16,32,2048]{2,1,0:T(8,128)(2,1)S(1)} %bitcast.15), channel_id=1, source_target_pairs={{0,32},{32,0},{1,33},{33,1},{2,34},{34,2},{3,35},{35,3},{4,36},{36... | collective-permute-start | bytes 6291464 | tf_op jit(solution)/shard_map/weights_over_core/ppermute | solution.py:558
  117.0 11.6 %collective-permute-start.5 = (bf16[256,128]{1,0:T(8,128)(2,1)S(1)}, bf16[256,128]{1,0:T(8,128)(2,1)S(1)}, u32[]{:S(2)}, u32[]{:S(2)}) collective-permute-start(bf16[256,128]{1,0:T(8,128)(2,1)S(1)} %get-tuple-element.52), channel_id=1, source_target_pairs={{1,0},{2,1},{3,2},{4,3},{5,4},{6,5},{7,6},{8,7},{9,8},{10,9},{11,1... | collective-permute-start | bytes 196616 | tf_op jit(solution)/shard_map/gradient_halo/ppermute | solution.py:462
  118.3 10.3 %collective-permute-start.4 = (bf16[256,128]{1,0:T(8,128)(2,1)S(1)}, bf16[256,128]{1,0:T(8,128)(2,1)S(1)}, u32[]{:S(2)}, u32[]{:S(2)}) collective-permute-start(bf16[256,128]{1,0:T(8,128)(2,1)S(1)} %get-tuple-element.52), channel_id=1, source_target_pairs={{0,1},{1,2},{2,3},{3,4},{4,5},{5,6},{6,7},{7,8},{8,9},{9,10},{10,1... | collective-permute-start | bytes 196616 | tf_op jit(solution)/shard_map/gradient_halo/ppermute | solution.py:461
  129.2 11.0 %collective-permute-start.6 = (f32[8,128]{1,0:T(8,128)S(1)}, f32[8,128]{1,0:T(8,128)S(1)}, u32[]{:S(2)}, u32[]{:S(2)}) collective-permute-start(f32[8,128]{1,0:T(8,128)S(1)} %loss_over_node.1), channel_id=1, source_target_pairs={{0,0},{1,1},{2,2},{3,3},{4,4},{5,5},{6,6},{7,7},{8,8},{9,9},{10,10... | collective-permute-start | bytes 12296 | tf_op jit(solution)/shard_map/loss_over_node/ppermute | solution.py:605

commit v4 on v3

--- a/solution.py
+++ b/solution.py
@@ -520,17 +520,7 @@
     )
     with jax.named_scope("weights_over_node"):
         mine = lax.ppermute(packed, EVERY, weight_route())
-    decoder = jnp.pad(decoder_weight_matrix, ((0, LANES - VARS), (0, 0)))
-    truth = lax.dynamic_slice_in_dim(observed_truth, member * SLOT, SLOT, 1)
-    truth = jnp.pad(truth.T, ((0, 0), (0, LANES - VARS)))
-    mask = lax.dynamic_slice_in_dim(region_mask, member * SLOT, SLOT, 0)
-    area = (1.0 - (1.0 - region_share) * mask.astype(f32))[:, None]
-    area = jnp.broadcast_to(area, (SLOT, LANES))
     latent_copies = jnp.broadcast_to(latent.T[None], (MEMBERS, HEAD, ROWS))
-    place, reach_row, decoder, truth, area, gain, latent_copies = lax.optimization_barrier(
-        (place, node_window_halfspan[None], decoder, truth, area,
-         layer_norm_gain[None], latent_copies)
-    )
     with jax.named_scope("latent_over_member"):
         latent_turned = lax.all_to_all(latent_copies, MEMBER, 0, 0, tiled=True).reshape(WIDTH, ROWS)
     with jax.named_scope("layer_norm"):
@@ -540,9 +530,20 @@
             [],
             8,
             1_000_000_000,
-            latent_turned, pert, gain,
-        )
-    mine, normed = lax.optimization_barrier((mine, normed))
+            latent_turned, pert, layer_norm_gain[None],
+        )
+    (mine, normed, decoder_weight_matrix, observed_truth, region_mask, gain, reach_row, place) = (
+        lax.optimization_barrier(
+            (mine, normed, decoder_weight_matrix, observed_truth, region_mask, layer_norm_gain[None],
+             node_window_halfspan[None], place)
+        )
+    )
+    decoder = jnp.pad(decoder_weight_matrix, ((0, LANES - VARS), (0, 0)))
+    truth = lax.dynamic_slice_in_dim(observed_truth, member * SLOT, SLOT, 1)
+    truth = jnp.pad(truth.T, ((0, 0), (0, LANES - VARS)))
+    mask = lax.dynamic_slice_in_dim(region_mask, member * SLOT, SLOT, 0)
+    area = (1.0 - (1.0 - region_share) * mask.astype(f32))[:, None]
+    area = jnp.broadcast_to(area, (SLOT, LANES))
     with jax.named_scope("normed_halo"):
         normed_low, normed_high = both_ways(normed)
     with jax.named_scope("weights_over_x"):
@@ -551,7 +552,9 @@
     with jax.named_scope("weights_over_y"):
         wa = lax.all_to_all(jnp.broadcast_to(row[None], (4,) + row.shape), "y", 0, 0, tiled=True)
         wa = wa.reshape(16, 32, PACKED)
-    wa, normed_low, normed_high = lax.optimization_barrier((wa, normed_low, normed_high))
+    wa, normed_low, normed_high, decoder, truth, area, gain, reach_row, place = lax.optimization_barrier(
+        (wa, normed_low, normed_high, decoder, truth, area, gain, reach_row, place)
+    )
     with jax.named_scope("normed_rows"):
         normed_all = jnp.concatenate([normed_low, normed, normed_high], axis=0)
     with jax.named_scope("weights_over_core"):

time: 174 us -> 171 us (0.983)
  waiting for transfers between devices: 23 us -> 20.8 us
  blocking collectives: 58.8 us -> 57 us
    all_to_all x1, blocking collectives: 27.1 us -> 25.3 us  [shards(): received = lax.all_to_all(send, MEMBER, 0, 0, tiled=True)]
    ppermute x1, waiting for transfers between devices: 1.89 us -> 0.09 us  [shards(): mine = lax.ppermute(packed, EVERY, weight_route())]
  transfers between devices with their start and end apart: 9 -> 9, of which waited for: 4 -> 4; matrix products, arithmetic and copies ran while one was open for 1% -> 3% of each run, Pallas kernels for 6% -> 6%
where the time goes in v4:
time: 171 us
  blocking collectives  57 us (33%)
  starting transfers between devices  55.4 us (32%)
  Pallas kernels  24.1 us (14%)
  waiting for transfers between devices  20.8 us (12%)
  local copies, waits for them, and re-layouts  8.15 us (5%)
  between operations  2.6 us (2%)
  other arithmetic  2.54 us (1%)
    all_to_all x1, blocking collectives, shards(): received = lax.all_to_all(send, MEMBER, 0, 0, tiled=True)  25.3 us
    pallas_call x9, Pallas kernels, call(): pl.pallas_call(body, out_shape=tuple((jax.ShapeDtypeStruct(shape, kind) f...  24.1 us
    ppermute x2, starting transfers between devices, both_ways(): low = lax.ppermute(block, NODE, [(i, i + 1) for i in range(count - 1)])  13 us
    ppermute x1, starting transfers between devices, shards(): mine = lax.ppermute(packed, EVERY, weight_route())  12.1 us
    all_to_all x1, blocking collectives, shards(): lax.all_to_all(jnp.broadcast_to(mine[None], (4,) + mine.shape), ('xl', 'x...  12 us
    all_to_all x1, blocking collectives, shards(): lax.all_to_all(forecast.reshape(MEMBERS, SLOT, LANES), MEMBER, 0, 0, tile...  10.9 us
    ppermute x2, waiting for transfers between devices, both_ways(): low = lax.ppermute(block, NODE, [(i, i + 1) for i in range(count - 1)])  10.7 us
    all_to_all x1, starting transfers between devices, shards(): lax.all_to_all(latent_copies, MEMBER, 0, 0, tiled=True).reshape(WIDTH, ROWS)  10.2 us
  transfers between devices with their start and end apart: 9, of which 4 were waited for; matrix products, arithmetic and copies ran while one was open for 3% of the time, Pallas kernels for 6%

profile of v4, /device:TPU:1, one launch (start us, length us, event | category | flops | bytes accessed | tf_op | source)
XLA Modules:
  0.0 170.6 jit_solution(8065414710213366986)
XLA Ops:
  0.6 1.6 broadcast_in_dim.16
  2.2 10.2 %all-to-all-start = ((bf16[16,64,256]{2,1,0:T(8,128)(2,1)}), bf16[16,64,256]{2,1,0:T(8,128)(2,1)S(1)}, u32[]{:S(2)}, u32[]{:S(2)}) async-start(bf16[16,64,256]{2,1,0:T(8,128)(2,1)} %broadcast_in_dim.16), calls=%async_computation | async-start | bytes 1048576 | tf_op jit(solution)/shard_map/latent_over_member/all_to_all | solution.py:525
  12.5 0.7 fusion
  13.2 0.9 maximum_maximum_fusion
  14.1 12.1 %collective-permute-start = (bf16[32,2048]{1,0:T(8,128)(2,1)S(1)}, bf16[32,2048]{1,0:T(8,128)(2,1)S(1)}, u32[]{:S(2)}, u32[]{:S(2)}) collective-permute-start(bf16[32,2048]{1,0:T(8,128)(2,1)S(1)} %maximum_maximum_fusion), channel_id=1, source_target_pairs={{0,0},{1,1},{64,2},{65,3},{128,4},{129,5},{192,6},{193,7},{256,8},... | collective-permute-start | bytes 393224 | tf_op jit(solution)/shard_map/weights_over_node/ppermute | solution.py:522
  26.2 0.1 pad_add_fusion.place_ref
  26.3 0.7 broadcast_in_dim.17.gain_ref
  27.0 0.0 all-to-all-done
  27.0 0.0 copy-start
  27.0 1.0 copy-done
  28.0 0.5 layer_norm.1
  28.6 0.0 copy-start.2
  28.6 0.8 copy-done.2
  29.3 0.1 collective-permute-done
  29.5 12.0 %all_to_all.30 = bf16[4,32,2048]{2,1,0:T(8,128)(2,1)S(1)} all-to-all(bf16[4,32,2048]{2,1,0:T(8,128)(2,1)S(1)} %broadcast_in_dim.38), channel_id=1, replica_groups=mesh['y'=4,'xl'=2,'c'=2,'z'=16,'xh'=2] {'xl','xh'}, dimensions={0} | all-to-all | bytes 1048576 | tf_op jit(solution)/shard_map/weights_over_x/all_to_all | solution.py:550
  41.5 1.6 broadcast_in_dim.40
  43.1 0.0 copy-start.4
  43.1 0.0 copy-start.5
  43.1 10.1 %all-to-all-start.2 = ((bf16[4,128,2048]{2,1,0:T(8,128)(2,1)}), bf16[4,128,2048]{2,1,0:T(8,128)(2,1)S(1)}, u32[]{:S(2)}, u32[]{:S(2)}) async-start(bf16[4,128,2048]{2,1,0:T(8,128)(2,1)} %broadcast_in_dim.40), calls=%async_computation.2 | async-start | bytes 4194304 | tf_op jit(solution)/shard_map/weights_over_y/all_to_all | solution.py:553
  53.2 0.0 copy-start.1
  53.2 0.0 copy-start.3
  53.2 1.4 collective-permute-start.2
  54.6 6.3 %collective-permute-start.1 = (bf16[256,1024]{1,0:T(8,128)(2,1)}, bf16[256,1024]{1,0:T(8,128)(2,1)}, u32[]{:S(2)}, u32[]{:S(2)}) collective-permute-start(bf16[256,1024]{1,0:T(8,128)(2,1)} %copy-done.2), channel_id=1, source_target_pairs={{0,1},{1,2},{2,3},{3,4},{4,5},{5,6},{6,7},{7,8},{8,9},{9,10},{10,1... | collective-permute-start | bytes 1572872 | tf_op jit(solution)/shard_map/normed_halo/ppermute | solution.py:461
  60.9 0.0 copy-done.4
  60.9 0.1 copy.12
  61.0 1.0 pad.8.decoder_ref
  62.0 0.0 copy-done.5
  62.0 0.1 multiply_subtract_fusion
  62.1 7.7 %collective-permute-done.2 = bf16[256,1024]{1,0:T(8,128)(2,1)} collective-permute-done((bf16[256,1024]{1,0:T(8,128)(2,1)}, bf16[256,1024]{1,0:T(8,128)(2,1)}, u32[]{:S(2)}, u32[]{:S(2)}) %collective-permute-start.2) | collective-permute-done | bytes 524320 | tf_op jit(solution)/shard_map/normed_halo/ppermute | solution.py:462
  69.8 10.7 %collective-permute-done.1 = bf16[256,1024]{1,0:T(8,128)(2,1)} collective-permute-done((bf16[256,1024]{1,0:T(8,128)(2,1)}, bf16[256,1024]{1,0:T(8,128)(2,1)}, u32[]{:S(2)}, u32[]{:S(2)}) %collective-permute-start.1) | collective-permute-done | bytes 524320 | tf_op jit(solution)/shard_map/normed_halo/ppermute | solution.py:461
  80.5 0.0 all-to-all-done.2
  80.5 0.1 broadcast_in_dim.41.area_ref
  80.5 2.4 %collective-permute-start.3 = (bf16[16,32,2048]{2,1,0:T(8,128)(2,1)S(1)}, bf16[16,32,2048]{2,1,0:T(8,128)(2,1)S(1)}, u32[]{:S(2)}, u32[]{:S(2)}) collective-permute-start(bf16[16,32,2048]{2,1,0:T(8,128)(2,1)S(1)} %bitcast.16), channel_id=1, source_target_pairs={{0,32},{32,0},{1,33},{33,1},{2,34},{34,2},{3,35},{35,3},{4,36},{36... | collective-permute-start | bytes 6291464 | tf_op jit(solution)/shard_map/weights_over_core/ppermute | solution.py:561
  82.9 1.5 pad_maximum_fusion.normed_ref
  84.4 2.3 %collective-permute-done.3.wb_ref = bf16[16,32,2048]{2,1,0:T(8,128)(2,1)S(1)} collective-permute-done((bf16[16,32,2048]{2,1,0:T(8,128)(2,1)S(1)}, bf16[16,32,2048]{2,1,0:T(8,128)(2,1)S(1)}, u32[]{:S(2)}, u32[]{:S(2)}) %collective-permute-start.3) | collective-permute-done | bytes 2097184 | tf_op jit(solution)/shard_map/weights_over_core/ppermute | solution.py:561
  86.7 0.0 copy-done.1
  86.7 0.0 copy-done.3
  86.7 6.7 %forward.1 = (bf16[768,512]{1,0:T(8,128)(2,1)S(1)}, bf16[768,512]{1,0:T(8,128)(2,1)S(1)}, bf16[768,512]{1,0:T(8,128)(2,1)S(1)}, f32[256,1024]{1,0:T(8,128)S(1)},...) custom-call(s32[4]{0:T(128)S(1)} %pad_add_fusion.place_ref, ...), custom_call_target="tpu_custom_call" | custom-call | flops 4000000000 | bytes 4000000 | tf_op jit(solution)/shard_map/forward/pallas_call | solution.py:447
  93.4 10.9 %all_to_all.31.forecast_ref = f32[16,16,128]{2,1,0:T(8,128)S(1)} all-to-all(f32[16,16,128]{2,1,0:T(8,128)S(1)} %bitcast.26), channel_id=1, replica_groups=mesh['y'=4,'xl'=2,'c'=2,'z'=16,'xh'=2] {'y','xl','c'}, dimensions={0} | all-to-all | bytes 262144 | tf_op jit(solution)/shard_map/forecasts_over_member/all_to_all | solution.py:575
  104.3 0.7 score.1
  104.9 8.9 %all_to_all.32 = bf16[16,16,128]{2,1,0:T(8,128)(2,1)S(1)} all-to-all(bf16[16,16,128]{2,1,0:T(8,128)(2,1)S(1)} %score.1), channel_id=1, replica_groups=mesh['y'=4,'xl'=2,'c'=2,'z'=16,'xh'=2] {'y','xl','c'}, dimensions={0} | all-to-all | bytes 131072 | tf_op jit(solution)/shard_map/gradients_over_member/all_to_all | solution.py:583
  113.9 2.1 %upstream.1 = (f32[256,1024]{1,0:T(8,128)S(1)}, bf16[256,512]{1,0:T(8,128)(2,1)S(1)}, bf16[256,512]{1,0:T(8,128)(2,1)S(1)}, bf16[256,512]{1,0:T(8,128)(2,1)S(1)}...) custom-call(s32[4]{0:T(128)S(1)} %pad_add_fusion.place_ref, bf16[256,128]{1,0:T(8,128)(2,1)S(1)} %bitcast.25, ...), custom_call_target="tpu_custom_call" | custom-call | flops 500000000 | bytes 4000000 | tf_op jit(solution)/shard_map/upstream/pallas_call | solution.py:447
  115.9 1.3 collective-permute-start.5
  117.2 6.7 %collective-permute-start.4 = (bf16[256,128]{1,0:T(8,128)(2,1)S(1)}, bf16[256,128]{1,0:T(8,128)(2,1)S(1)}, u32[]{:S(2)}, u32[]{:S(2)}) collective-permute-start(bf16[256,128]{1,0:T(8,128)(2,1)S(1)} %get-tuple-element.61), channel_id=1, source_target_pairs={{0,1},{1,2},{2,3},{3,4},{4,5},{5,6},{6,7},{7,8},{8,9},{9,10},{10,1... | collective-permute-start | bytes 196616 | tf_op jit(solution)/shard_map/gradient_halo/ppermute | solution.py:461
  124.0 3.6 %query_gradients.1.qgrad_ref = f32[256,512]{1,0:T(8,128)S(1)} custom-call(s32[4]{0:T(128)S(1)} %pad_add_fusion.place_ref, bf16[768,512]{1,0:T(8,128)(2,1)S(1)} %get-tuple-element.62.q_ref, bf16[768,512]{1,0:T(8,128)(2,1)S(1)} %get-tuple-element.63.k_ref, bf16[768,512]{1,0:T(8,128)(2,1)S(1)} %get-tuple-element.64.v_ref, ...), custom_call_target="tpu_custom_call" | custom-call | flops 4000000000 | bytes 4000000 | tf_op jit(solution)/shard_map/query_gradients/pallas_call | solution.py:447
  127.5 0.0 collective-permute-done.5.high_ref
  127.5 0.0 collective-permute-done.4.low_ref
  127.5 0.6 loss_over_node.1
  128.2 4.8 %collective-permute-start.6 = (f32[8,128]{1,0:T(8,128)S(1)}, f32[8,128]{1,0:T(8,128)S(1)}, u32[]{:S(2)}, u32[]{:S(2)}) collective-permute-start(f32[8,128]{1,0:T(8,128)S(1)} %loss_over_node.1), channel_id=1, source_target_pairs={{0,0},{1,1},{2,2},{3,3},{4,4},{5,5},{6,6},{7,7},{8,8},{9,9},{10,10... | collective-permute-start | bytes 12296 | tf_op jit(solution)/shard_map/loss_over_node/ppermute | solution.py:608
  133.0 6.2 %backward.1.qkv_grad_ref = bf16[256,1536]{1,0:T(8,128)(2,1)S(1)} custom-call(s32[4]{0:T(128)S(1)} %pad_add_fusion.place_ref, bf16[256,128]{1,0:T(8,128)(2,1)S(1)} %collective-permute-done.4.low_ref, bf16[256,128]{1,0:T(8,128)(2,1)S(1)} %collective-permute-done.5.high_ref, bf16[128,1024]{1,0:T(8,128)(2,1)S(1)} %pad.8.decoder_ref, ...), custom_call_target="tpu_custom_call" | custom-call | flops 4000000000 | bytes 4000000 | tf_op jit(solution)/shard_map/backward/pallas_call | solution.py:447
  139.2 0.0 collective-permute-done.6.loss_ref
  139.2 3.1 %hidden_gradient.1 = (f32[256,1024]{1,0:T(8,128)}, bf16[16,80,256]{2,1,0:T(8,128)(2,1)S(1)}) custom-call(s32[4]{0:T(128)S(1)} %pad_add_fusion.place_ref, bf16[256,1536]{1,0:T(8,128)(2,1)S(1)} %backward.1.qkv_grad_ref, bf16[16,32,2048]{2,1,0:T(8,128)(2,1)S(1)} %bitcast.20, bf16[16,32,2048]{2,1,0:T(8,128)(2,1)S(1)} %collective-permute-done.3.wb_ref, ...), custom_call_target="tpu_custom_call" | custom-call | flops 1000000000 | bytes 4000000 | tf_op jit(solution)/shard_map/hidden_gradient/pallas_call | solution.py:447
  142.3 25.3 %all_to_all.33.received_ref = bf16[16,80,256]{2,1,0:T(8,128)(2,1)S(1)} all-to-all(bf16[16,80,256]{2,1,0:T(8,128)(2,1)S(1)} %get-tuple-element.73), channel_id=1, replica_groups=mesh['y'=4,'xl'=2,'c'=2,'z'=16,'xh'=2] {'y','xl','c'}, dimensions={0} | all-to-all | bytes 1310720 | tf_op jit(solution)/shard_map/latent_gradient_over_member/all_to_all | solution.py:631
  167.6 0.7 finish.1
  168.3 0.5 slice.11
  (3 shorter events, 0.1 us)
Async XLA Ops:
  2.2 24.8 %all-to-all-start = ((bf16[16,64,256]{2,1,0:T(8,128)(2,1)}), bf16[16,64,256]{2,1,0:T(8,128)(2,1)S(1)}, u32[]{:S(2)}, u32[]{:S(2)}) async-start(bf16[16,64,256]{2,1,0:T(8,128)(2,1)} %broadcast_in_dim.16), calls=%async_computation | async-start | bytes 1048576 | tf_op jit(solution)/shard_map/latent_over_member/all_to_all | solution.py:525
  14.1 15.3 %collective-permute-start = (bf16[32,2048]{1,0:T(8,128)(2,1)S(1)}, bf16[32,2048]{1,0:T(8,128)(2,1)S(1)}, u32[]{:S(2)}, u32[]{:S(2)}) collective-permute-start(bf16[32,2048]{1,0:T(8,128)(2,1)S(1)} %maximum_maximum_fusion), channel_id=1, source_target_pairs={{0,0},{1,1},{64,2},{65,3},{128,4},{129,5},{192,6},{193,7},{256,8},... | collective-permute-start | bytes 393224 | tf_op jit(solution)/shard_map/weights_over_node/ppermute | solution.py:522
  27.0 1.0 copy-start
  28.6 0.8 copy-start.2
  43.1 17.8 %copy-start.4 = (f32[98,256]{1,0:T(8,128)S(1)}, f32[98,256]{1,0:T(8,128)}, u32[]{:S(2)}) copy-start(f32[98,256]{1,0:T(8,128)} %param.15) | copy-start | bytes 301060
  43.1 18.9 %copy-start.5 = (s32[256]{0:T(256)S(1)}, s32[256]{0:T(256)}, u32[]{:S(2)}) copy-start(s32[256]{0:T(256)} %param.16) | copy-start | bytes 3076
  43.1 37.4 %all-to-all-start.2 = ((bf16[4,128,2048]{2,1,0:T(8,128)(2,1)}), bf16[4,128,2048]{2,1,0:T(8,128)(2,1)S(1)}, u32[]{:S(2)}, u32[]{:S(2)}) async-start(bf16[4,128,2048]{2,1,0:T(8,128)(2,1)} %broadcast_in_dim.40), calls=%async_computation.2 | async-start | bytes 4194304 | tf_op jit(solution)/shard_map/weights_over_y/all_to_all | solution.py:553
  53.2 33.5 %copy-start.1 = (bf16[1,256,1024]{2,1,0:T(8,128)(2,1)S(1)}, bf16[1,256,1024]{2,1,0:T(8,128)(2,1)}, u32[]{:S(2)}) copy-start(bf16[1,256,1024]{2,1,0:T(8,128)(2,1)} %param.10) | copy-start | bytes 1572868
  53.2 33.5 %copy-start.3 = (s32[256]{0:T(256)S(1)}, s32[256]{0:T(256)}, u32[]{:S(2)}) copy-start(s32[256]{0:T(256)} %param.17) | copy-start | bytes 3076
  53.2 16.6 %collective-permute-start.2 = (bf16[256,1024]{1,0:T(8,128)(2,1)}, bf16[256,1024]{1,0:T(8,128)(2,1)}, u32[]{:S(2)}, u32[]{:S(2)}) collective-permute-start(bf16[256,1024]{1,0:T(8,128)(2,1)} %copy-done.2), channel_id=1, source_target_pairs={{1,0},{2,1},{3,2},{4,3},{5,4},{6,5},{7,6},{8,7},{9,8},{10,9},{11,1... | collective-permute-start | bytes 1572872 | tf_op jit(solution)/shard_map/normed_halo/ppermute | solution.py:462
  54.6 25.9 %collective-permute-start.1 = (bf16[256,1024]{1,0:T(8,128)(2,1)}, bf16[256,1024]{1,0:T(8,128)(2,1)}, u32[]{:S(2)}, u32[]{:S(2)}) collective-permute-start(bf16[256,1024]{1,0:T(8,128)(2,1)} %copy-done.2), channel_id=1, source_target_pairs={{0,1},{1,2},{2,3},{3,4},{4,5},{5,6},{6,7},{7,8},{8,9},{9,10},{10,1... | collective-permute-start | bytes 1572872 | tf_op jit(solution)/shard_map/normed_halo/ppermute | solution.py:461
  80.5 6.2 %collective-permute-start.3 = (bf16[16,32,2048]{2,1,0:T(8,128)(2,1)S(1)}, bf16[16,32,2048]{2,1,0:T(8,128)(2,1)S(1)}, u32[]{:S(2)}, u32[]{:S(2)}) collective-permute-start(bf16[16,32,2048]{2,1,0:T(8,128)(2,1)S(1)} %bitcast.16), channel_id=1, source_target_pairs={{0,32},{32,0},{1,33},{33,1},{2,34},{34,2},{3,35},{35,3},{4,36},{36... | collective-permute-start | bytes 6291464 | tf_op jit(solution)/shard_map/weights_over_core/ppermute | solution.py:561
  115.9 11.6 %collective-permute-start.5 = (bf16[256,128]{1,0:T(8,128)(2,1)S(1)}, bf16[256,128]{1,0:T(8,128)(2,1)S(1)}, u32[]{:S(2)}, u32[]{:S(2)}) collective-permute-start(bf16[256,128]{1,0:T(8,128)(2,1)S(1)} %get-tuple-element.61), channel_id=1, source_target_pairs={{1,0},{2,1},{3,2},{4,3},{5,4},{6,5},{7,6},{8,7},{9,8},{10,9},{11,1... | collective-permute-start | bytes 196616 | tf_op jit(solution)/shard_map/gradient_halo/ppermute | solution.py:462
  117.2 10.3 %collective-permute-start.4 = (bf16[256,128]{1,0:T(8,128)(2,1)S(1)}, bf16[256,128]{1,0:T(8,128)(2,1)S(1)}, u32[]{:S(2)}, u32[]{:S(2)}) collective-permute-start(bf16[256,128]{1,0:T(8,128)(2,1)S(1)} %get-tuple-element.61), channel_id=1, source_target_pairs={{0,1},{1,2},{2,3},{3,4},{4,5},{5,6},{6,7},{7,8},{8,9},{9,10},{10,1... | collective-permute-start | bytes 196616 | tf_op jit(solution)/shard_map/gradient_halo/ppermute | solution.py:461
  128.2 11.0 %collective-permute-start.6 = (f32[8,128]{1,0:T(8,128)S(1)}, f32[8,128]{1,0:T(8,128)S(1)}, u32[]{:S(2)}, u32[]{:S(2)}) collective-permute-start(f32[8,128]{1,0:T(8,128)S(1)} %loss_over_node.1), channel_id=1, source_target_pairs={{0,0},{1,1},{2,2},{3,3},{4,4},{5,5},{6,6},{7,7},{8,8},{9,9},{10,10... | collective-permute-start | bytes 12296 | tf_op jit(solution)/shard_map/loss_over_node/ppermute | solution.py:608

commit v5 on v4

--- a/solution.py
+++ b/solution.py
@@ -429,12 +429,12 @@
         send_ref[member, HEAD:, :] = tail.astype(bf16)
 
 
-def finish_kernel(received_ref, latent_grad_ref, loss_ref):
+def finish_kernel(scale, received_ref, latent_grad_ref, loss_ref):
     total = received_ref[0].astype(f32)
     for member in range(1, MEMBERS):
         total = total + received_ref[member].astype(f32)
     latent_grad_ref[...] = total[:HEAD]
-    loss_ref[...] = jnp.broadcast_to(jnp.sum(total[HEAD : HEAD + 1, :], axis=1, keepdims=True), (8, LANES))
+    loss_ref[...] = jnp.sum(total[HEAD : HEAD + 1, :], axis=1, keepdims=True) * scale
 
 
 def call(body, outs, scratch, megabytes, cost, *operands, far=()):
@@ -631,10 +631,10 @@
         received = lax.all_to_all(send, MEMBER, 0, 0, tiled=True)
     with jax.named_scope("finish"):
         latent_grad, loss = call(
-            finish_kernel, [((HEAD, ROWS), f32), ((8, LANES), f32)], [], 8, 10_000_000, received
-        )
-    loss = loss[0, 0] / (MEMBERS * node_total * VARS)
-    return (loss, latent_grad.T, noise[None])
+            functools.partial(finish_kernel, 1.0 / (MEMBERS * node_total * VARS)),
+            [((HEAD, ROWS), f32), ((1, 1), f32)], [], 8, 10_000_000, received,
+        )
+    return (loss.reshape(()), latent_grad.T, noise[None])
 
 
 def solution(mesh):

time: 171 us -> 169 us (0.988)
  between operations: 2.6 us -> 0.82 us
where the time goes in v5:
time: 169 us; the launch traced here: 168 us
  blocking collectives  57 us (34%)
  starting transfers between devices  55.4 us (33%)
  Pallas kernels  24.1 us (14%)
  waiting for transfers between devices  21.6 us (13%)
  local copies, waits for them, and re-layouts  6.85 us (4%)
  other arithmetic  2.54 us (2%)
    all_to_all x1, blocking collectives, shards(): received = lax.all_to_all(send, MEMBER, 0, 0, tiled=True)  25.2 us
    pallas_call x9, Pallas kernels, call(): pl.pallas_call(body, out_shape=tuple((jax.ShapeDtypeStruct(shape, kind) f...  24.1 us
    ppermute x2, starting transfers between devices, both_ways(): low = lax.ppermute(block, NODE, [(i, i + 1) for i in range(count - 1)])  13 us
    ppermute x1, starting transfers between devices, shards(): mine = lax.ppermute(packed, EVERY, weight_route())  12.1 us
    all_to_all x1, blocking collectives, shards(): lax.all_to_all(jnp.broadcast_to(mine[None], (4,) + mine.shape), ('xl', 'x...  12 us
    all_to_all x1, blocking collectives, shards(): lax.all_to_all(forecast.reshape(MEMBERS, SLOT, LANES), MEMBER, 0, 0, tile...  10.9 us
    ppermute x2, waiting for transfers between devices, both_ways(): low = lax.ppermute(block, NODE, [(i, i + 1) for i in range(count - 1)])  10.7 us
    all_to_all x1, starting transfers between devices, shards(): lax.all_to_all(latent_copies, MEMBER, 0, 0, tiled=True).reshape(WIDTH, ROWS)  10.2 us
  transfers between devices with their start and end apart: 9, of which 4 were waited for; matrix products, arithmetic and copies ran while one was open for 3% of the time, Pallas kernels for 6%

profile of v5, /device:TPU:1, one launch (start us, length us, event | category | flops | bytes accessed | tf_op | source)
XLA Modules:
  0.0 168.3 jit_solution(14525349275379604851)
XLA Ops:
  0.6 1.6 broadcast_in_dim.16
  2.2 10.2 %all-to-all-start = ((bf16[16,64,256]{2,1,0:T(8,128)(2,1)}), bf16[16,64,256]{2,1,0:T(8,128)(2,1)S(1)}, u32[]{:S(2)}, u32[]{:S(2)}) async-start(bf16[16,64,256]{2,1,0:T(8,128)(2,1)} %broadcast_in_dim.16), calls=%async_computation | async-start | bytes 1048576 | tf_op jit(solution)/shard_map/latent_over_member/all_to_all | solution.py:525
  12.5 0.7 fusion
  13.2 0.9 maximum_maximum_fusion
  14.1 12.1 %collective-permute-start = (bf16[32,2048]{1,0:T(8,128)(2,1)S(1)}, bf16[32,2048]{1,0:T(8,128)(2,1)S(1)}, u32[]{:S(2)}, u32[]{:S(2)}) collective-permute-start(bf16[32,2048]{1,0:T(8,128)(2,1)S(1)} %maximum_maximum_fusion), channel_id=1, source_target_pairs={{0,0},{1,1},{64,2},{65,3},{128,4},{129,5},{192,6},{193,7},{256,8},... | collective-permute-start | bytes 393224 | tf_op jit(solution)/shard_map/weights_over_node/ppermute | solution.py:522
  26.2 0.1 pad_add_fusion.place_ref
  26.3 0.7 broadcast_in_dim.17.gain_ref
  27.0 0.0 all-to-all-done
  27.0 0.0 copy-start
  27.0 1.0 copy-done
  28.0 0.5 layer_norm.1
  28.6 0.0 copy-start.2
  28.6 0.9 collective-permute-done
  29.5 12.0 %all_to_all.30 = bf16[4,32,2048]{2,1,0:T(8,128)(2,1)S(1)} all-to-all(bf16[4,32,2048]{2,1,0:T(8,128)(2,1)S(1)} %broadcast_in_dim.38), channel_id=1, replica_groups=mesh['y'=4,'xl'=2,'c'=2,'z'=16,'xh'=2] {'xl','xh'}, dimensions={0} | all-to-all | bytes 1048576 | tf_op jit(solution)/shard_map/weights_over_x/all_to_all | solution.py:550
  41.5 1.6 broadcast_in_dim.40
  43.1 0.0 copy-done.2
  43.1 0.0 copy-start.4
  43.1 0.0 copy-start.5
  43.1 10.1 %all-to-all-start.2 = ((bf16[4,128,2048]{2,1,0:T(8,128)(2,1)}), bf16[4,128,2048]{2,1,0:T(8,128)(2,1)S(1)}, u32[]{:S(2)}, u32[]{:S(2)}) async-start(bf16[4,128,2048]{2,1,0:T(8,128)(2,1)} %broadcast_in_dim.40), calls=%async_computation.2 | async-start | bytes 4194304 | tf_op jit(solution)/shard_map/weights_over_y/all_to_all | solution.py:553
  53.2 0.0 copy-start.1
  53.2 0.0 copy-start.3
  53.2 1.4 collective-permute-start.2
  54.6 6.3 %collective-permute-start.1 = (bf16[256,1024]{1,0:T(8,128)(2,1)}, bf16[256,1024]{1,0:T(8,128)(2,1)}, u32[]{:S(2)}, u32[]{:S(2)}) collective-permute-start(bf16[256,1024]{1,0:T(8,128)(2,1)} %copy-done.2), channel_id=1, source_target_pairs={{0,1},{1,2},{2,3},{3,4},{4,5},{5,6},{6,7},{7,8},{8,9},{9,10},{10,1... | collective-permute-start | bytes 1572872 | tf_op jit(solution)/shard_map/normed_halo/ppermute | solution.py:461
  60.9 0.0 copy-done.4
  60.9 0.1 copy.12
  61.0 1.0 pad.8.decoder_ref
  62.0 0.0 copy-done.5
  62.0 0.1 multiply_subtract_fusion
  62.1 7.7 %collective-permute-done.2 = bf16[256,1024]{1,0:T(8,128)(2,1)} collective-permute-done((bf16[256,1024]{1,0:T(8,128)(2,1)}, bf16[256,1024]{1,0:T(8,128)(2,1)}, u32[]{:S(2)}, u32[]{:S(2)}) %collective-permute-start.2) | collective-permute-done | bytes 524320 | tf_op jit(solution)/shard_map/normed_halo/ppermute | solution.py:462
  69.8 10.7 %collective-permute-done.1 = bf16[256,1024]{1,0:T(8,128)(2,1)} collective-permute-done((bf16[256,1024]{1,0:T(8,128)(2,1)}, bf16[256,1024]{1,0:T(8,128)(2,1)}, u32[]{:S(2)}, u32[]{:S(2)}) %collective-permute-start.1) | collective-permute-done | bytes 524320 | tf_op jit(solution)/shard_map/normed_halo/ppermute | solution.py:461
  80.5 0.0 all-to-all-done.2
  80.5 0.1 broadcast_in_dim.41.area_ref
  80.5 2.4 %collective-permute-start.3 = (bf16[16,32,2048]{2,1,0:T(8,128)(2,1)S(1)}, bf16[16,32,2048]{2,1,0:T(8,128)(2,1)S(1)}, u32[]{:S(2)}, u32[]{:S(2)}) collective-permute-start(bf16[16,32,2048]{2,1,0:T(8,128)(2,1)S(1)} %bitcast.16), channel_id=1, source_target_pairs={{0,32},{32,0},{1,33},{33,1},{2,34},{34,2},{3,35},{35,3},{4,36},{36... | collective-permute-start | bytes 6291464 | tf_op jit(solution)/shard_map/weights_over_core/ppermute | solution.py:561
  82.9 1.5 pad_maximum_fusion.normed_ref
  84.4 2.3 %collective-permute-done.3.wb_ref = bf16[16,32,2048]{2,1,0:T(8,128)(2,1)S(1)} collective-permute-done((bf16[16,32,2048]{2,1,0:T(8,128)(2,1)S(1)}, bf16[16,32,2048]{2,1,0:T(8,128)(2,1)S(1)}, u32[]{:S(2)}, u32[]{:S(2)}) %collective-permute-start.3) | collective-permute-done | bytes 2097184 | tf_op jit(solution)/shard_map/weights_over_core/ppermute | solution.py:561
  86.7 0.0 copy-done.1
  86.7 0.0 copy-done.3
  86.7 6.7 %forward.1 = (bf16[768,512]{1,0:T(8,128)(2,1)S(1)}, bf16[768,512]{1,0:T(8,128)(2,1)S(1)}, bf16[768,512]{1,0:T(8,128)(2,1)S(1)}, f32[256,1024]{1,0:T(8,128)S(1)},...) custom-call(s32[4]{0:T(128)S(1)} %pad_add_fusion.place_ref, ...), custom_call_target="tpu_custom_call" | custom-call | flops 4000000000 | bytes 4000000 | tf_op jit(solution)/shard_map/forward/pallas_call | solution.py:447
  93.4 10.9 %all_to_all.31.forecast_ref = f32[16,16,128]{2,1,0:T(8,128)S(1)} all-to-all(f32[16,16,128]{2,1,0:T(8,128)S(1)} %bitcast.26), channel_id=1, replica_groups=mesh['y'=4,'xl'=2,'c'=2,'z'=16,'xh'=2] {'y','xl','c'}, dimensions={0} | all-to-all | bytes 262144 | tf_op jit(solution)/shard_map/forecasts_over_member/all_to_all | solution.py:575
  104.3 0.7 score.1
  104.9 8.9 %all_to_all.32 = bf16[16,16,128]{2,1,0:T(8,128)(2,1)S(1)} all-to-all(bf16[16,16,128]{2,1,0:T(8,128)(2,1)S(1)} %score.1), channel_id=1, replica_groups=mesh['y'=4,'xl'=2,'c'=2,'z'=16,'xh'=2] {'y','xl','c'}, dimensions={0} | all-to-all | bytes 131072 | tf_op jit(solution)/shard_map/gradients_over_member/all_to_all | solution.py:583
  113.9 2.1 %upstream.1 = (f32[256,1024]{1,0:T(8,128)S(1)}, bf16[256,512]{1,0:T(8,128)(2,1)S(1)}, bf16[256,512]{1,0:T(8,128)(2,1)S(1)}, bf16[256,512]{1,0:T(8,128)(2,1)S(1)}...) custom-call(s32[4]{0:T(128)S(1)} %pad_add_fusion.place_ref, bf16[256,128]{1,0:T(8,128)(2,1)S(1)} %bitcast.25, ...), custom_call_target="tpu_custom_call" | custom-call | flops 500000000 | bytes 4000000 | tf_op jit(solution)/shard_map/upstream/pallas_call | solution.py:447
  115.9 1.3 collective-permute-start.5
  117.2 6.7 %collective-permute-start.4 = (bf16[256,128]{1,0:T(8,128)(2,1)S(1)}, bf16[256,128]{1,0:T(8,128)(2,1)S(1)}, u32[]{:S(2)}, u32[]{:S(2)}) collective-permute-start(bf16[256,128]{1,0:T(8,128)(2,1)S(1)} %get-tuple-element.61), channel_id=1, source_target_pairs={{0,1},{1,2},{2,3},{3,4},{4,5},{5,6},{6,7},{7,8},{8,9},{9,10},{10,1... | collective-permute-start | bytes 196616 | tf_op jit(solution)/shard_map/gradient_halo/ppermute | solution.py:461
  124.0 3.6 %query_gradients.1.qgrad_ref = f32[256,512]{1,0:T(8,128)S(1)} custom-call(s32[4]{0:T(128)S(1)} %pad_add_fusion.place_ref, bf16[768,512]{1,0:T(8,128)(2,1)S(1)} %get-tuple-element.62.q_ref, bf16[768,512]{1,0:T(8,128)(2,1)S(1)} %get-tuple-element.63.k_ref, bf16[768,512]{1,0:T(8,128)(2,1)S(1)} %get-tuple-element.64.v_ref, ...), custom_call_target="tpu_custom_call" | custom-call | flops 4000000000 | bytes 4000000 | tf_op jit(solution)/shard_map/query_gradients/pallas_call | solution.py:447
  127.5 0.0 collective-permute-done.5.high_ref
  127.5 0.0 collective-permute-done.4.low_ref
  127.5 0.6 loss_over_node.1
  128.2 4.8 %collective-permute-start.6 = (f32[8,128]{1,0:T(8,128)S(1)}, f32[8,128]{1,0:T(8,128)S(1)}, u32[]{:S(2)}, u32[]{:S(2)}) collective-permute-start(f32[8,128]{1,0:T(8,128)S(1)} %loss_over_node.1), channel_id=1, source_target_pairs={{0,0},{1,1},{2,2},{3,3},{4,4},{5,5},{6,6},{7,7},{8,8},{9,9},{10,10... | collective-permute-start | bytes 12296 | tf_op jit(solution)/shard_map/loss_over_node/ppermute | solution.py:608
  133.0 6.2 %backward.1.qkv_grad_ref = bf16[256,1536]{1,0:T(8,128)(2,1)S(1)} custom-call(s32[4]{0:T(128)S(1)} %pad_add_fusion.place_ref, bf16[256,128]{1,0:T(8,128)(2,1)S(1)} %collective-permute-done.4.low_ref, bf16[256,128]{1,0:T(8,128)(2,1)S(1)} %collective-permute-done.5.high_ref, bf16[128,1024]{1,0:T(8,128)(2,1)S(1)} %pad.8.decoder_ref, ...), custom_call_target="tpu_custom_call" | custom-call | flops 4000000000 | bytes 4000000 | tf_op jit(solution)/shard_map/backward/pallas_call | solution.py:447
  139.2 0.0 collective-permute-done.6.loss_ref
  139.2 3.1 %hidden_gradient.1 = (f32[256,1024]{1,0:T(8,128)}, bf16[16,80,256]{2,1,0:T(8,128)(2,1)S(1)}) custom-call(s32[4]{0:T(128)S(1)} %pad_add_fusion.place_ref, bf16[256,1536]{1,0:T(8,128)(2,1)S(1)} %backward.1.qkv_grad_ref, bf16[16,32,2048]{2,1,0:T(8,128)(2,1)S(1)} %bitcast.20, bf16[16,32,2048]{2,1,0:T(8,128)(2,1)S(1)} %collective-permute-done.3.wb_ref, ...), custom_call_target="tpu_custom_call" | custom-call | flops 1000000000 | bytes 4000000 | tf_op jit(solution)/shard_map/hidden_gradient/pallas_call | solution.py:447
  142.3 25.2 %all_to_all.33.received_ref = bf16[16,80,256]{2,1,0:T(8,128)(2,1)S(1)} all-to-all(bf16[16,80,256]{2,1,0:T(8,128)(2,1)S(1)} %get-tuple-element.73), channel_id=1, replica_groups=mesh['y'=4,'xl'=2,'c'=2,'z'=16,'xh'=2] {'y','xl','c'}, dimensions={0} | all-to-all | bytes 1310720 | tf_op jit(solution)/shard_map/latent_gradient_over_member/all_to_all | solution.py:631
  167.6 0.7 finish.1
  (3 shorter events, 0.1 us)
Async XLA Ops:
  2.2 24.8 %all-to-all-start = ((bf16[16,64,256]{2,1,0:T(8,128)(2,1)}), bf16[16,64,256]{2,1,0:T(8,128)(2,1)S(1)}, u32[]{:S(2)}, u32[]{:S(2)}) async-start(bf16[16,64,256]{2,1,0:T(8,128)(2,1)} %broadcast_in_dim.16), calls=%async_computation | async-start | bytes 1048576 | tf_op jit(solution)/shard_map/latent_over_member/all_to_all | solution.py:525
  14.1 15.3 %collective-permute-start = (bf16[32,2048]{1,0:T(8,128)(2,1)S(1)}, bf16[32,2048]{1,0:T(8,128)(2,1)S(1)}, u32[]{:S(2)}, u32[]{:S(2)}) collective-permute-start(bf16[32,2048]{1,0:T(8,128)(2,1)S(1)} %maximum_maximum_fusion), channel_id=1, source_target_pairs={{0,0},{1,1},{64,2},{65,3},{128,4},{129,5},{192,6},{193,7},{256,8},... | collective-permute-start | bytes 393224 | tf_op jit(solution)/shard_map/weights_over_node/ppermute | solution.py:522
  27.0 1.0 copy-start
  28.6 14.5 %copy-start.2 = (bf16[256,1024]{1,0:T(8,128)(2,1)}, bf16[256,1024]{1,0:T(8,128)(2,1)S(1)}, u32[]{:S(2)}) copy-start(bf16[256,1024]{1,0:T(8,128)(2,1)S(1)} %get-tuple-element.42) | copy-start | bytes 1572868
  43.1 17.8 %copy-start.4 = (f32[98,256]{1,0:T(8,128)S(1)}, f32[98,256]{1,0:T(8,128)}, u32[]{:S(2)}) copy-start(f32[98,256]{1,0:T(8,128)} %param.15) | copy-start | bytes 301060
  43.1 18.9 %copy-start.5 = (s32[256]{0:T(256)S(1)}, s32[256]{0:T(256)}, u32[]{:S(2)}) copy-start(s32[256]{0:T(256)} %param.16) | copy-start | bytes 3076
  43.1 37.4 %all-to-all-start.2 = ((bf16[4,128,2048]{2,1,0:T(8,128)(2,1)}), bf16[4,128,2048]{2,1,0:T(8,128)(2,1)S(1)}, u32[]{:S(2)}, u32[]{:S(2)}) async-start(bf16[4,128,2048]{2,1,0:T(8,128)(2,1)} %broadcast_in_dim.40), calls=%async_computation.2 | async-start | bytes 4194304 | tf_op jit(solution)/shard_map/weights_over_y/all_to_all | solution.py:553
  53.2 33.5 %copy-start.1 = (bf16[1,256,1024]{2,1,0:T(8,128)(2,1)S(1)}, bf16[1,256,1024]{2,1,0:T(8,128)(2,1)}, u32[]{:S(2)}) copy-start(bf16[1,256,1024]{2,1,0:T(8,128)(2,1)} %param.10) | copy-start | bytes 1572868
  53.2 33.5 %copy-start.3 = (s32[256]{0:T(256)S(1)}, s32[256]{0:T(256)}, u32[]{:S(2)}) copy-start(s32[256]{0:T(256)} %param.17) | copy-start | bytes 3076
  53.2 16.6 %collective-permute-start.2 = (bf16[256,1024]{1,0:T(8,128)(2,1)}, bf16[256,1024]{1,0:T(8,128)(2,1)}, u32[]{:S(2)}, u32[]{:S(2)}) collective-permute-start(bf16[256,1024]{1,0:T(8,128)(2,1)} %copy-done.2), channel_id=1, source_target_pairs={{1,0},{2,1},{3,2},{4,3},{5,4},{6,5},{7,6},{8,7},{9,8},{10,9},{11,1... | collective-permute-start | bytes 1572872 | tf_op jit(solution)/shard_map/normed_halo/ppermute | solution.py:462
  54.6 25.9 %collective-permute-start.1 = (bf16[256,1024]{1,0:T(8,128)(2,1)}, bf16[256,1024]{1,0:T(8,128)(2,1)}, u32[]{:S(2)}, u32[]{:S(2)}) collective-permute-start(bf16[256,1024]{1,0:T(8,128)(2,1)} %copy-done.2), channel_id=1, source_target_pairs={{0,1},{1,2},{2,3},{3,4},{4,5},{5,6},{6,7},{7,8},{8,9},{9,10},{10,1... | collective-permute-start | bytes 1572872 | tf_op jit(solution)/shard_map/normed_halo/ppermute | solution.py:461
  80.5 6.2 %collective-permute-start.3 = (bf16[16,32,2048]{2,1,0:T(8,128)(2,1)S(1)}, bf16[16,32,2048]{2,1,0:T(8,128)(2,1)S(1)}, u32[]{:S(2)}, u32[]{:S(2)}) collective-permute-start(bf16[16,32,2048]{2,1,0:T(8,128)(2,1)S(1)} %bitcast.16), channel_id=1, source_target_pairs={{0,32},{32,0},{1,33},{33,1},{2,34},{34,2},{3,35},{35,3},{4,36},{36... | collective-permute-start | bytes 6291464 | tf_op jit(solution)/shard_map/weights_over_core/ppermute | solution.py:561
  115.9 11.6 %collective-permute-start.5 = (bf16[256,128]{1,0:T(8,128)(2,1)S(1)}, bf16[256,128]{1,0:T(8,128)(2,1)S(1)}, u32[]{:S(2)}, u32[]{:S(2)}) collective-permute-start(bf16[256,128]{1,0:T(8,128)(2,1)S(1)} %get-tuple-element.61), channel_id=1, source_target_pairs={{1,0},{2,1},{3,2},{4,3},{5,4},{6,5},{7,6},{8,7},{9,8},{10,9},{11,1... | collective-permute-start | bytes 196616 | tf_op jit(solution)/shard_map/gradient_halo/ppermute | solution.py:462
  117.2 10.3 %collective-permute-start.4 = (bf16[256,128]{1,0:T(8,128)(2,1)S(1)}, bf16[256,128]{1,0:T(8,128)(2,1)S(1)}, u32[]{:S(2)}, u32[]{:S(2)}) collective-permute-start(bf16[256,128]{1,0:T(8,128)(2,1)S(1)} %get-tuple-element.61), channel_id=1, source_target_pairs={{0,1},{1,2},{2,3},{3,4},{4,5},{5,6},{6,7},{7,8},{8,9},{9,10},{10,1... | collective-permute-start | bytes 196616 | tf_op jit(solution)/shard_map/gradient_halo/ppermute | solution.py:461
  128.2 11.0 %collective-permute-start.6 = (f32[8,128]{1,0:T(8,128)S(1)}, f32[8,128]{1,0:T(8,128)S(1)}, u32[]{:S(2)}, u32[]{:S(2)}) collective-permute-start(f32[8,128]{1,0:T(8,128)S(1)} %loss_over_node.1), channel_id=1, source_target_pairs={{0,0},{1,1},{2,2},{3,3},{4,4},{5,5},{6,6},{7,7},{8,8},{9,9},{10,10... | collective-permute-start | bytes 12296 | tf_op jit(solution)/shard_map/loss_over_node/ppermute | solution.py:608

commit v6 on v5

--- a/solution.py
+++ b/solution.py
@@ -77,6 +77,22 @@
 
 def lane_index(rows, lanes):
     return lax.broadcasted_iota(jnp.int32, (rows, lanes), 1)
+
+
+def copies_kernel(block_ref, out_ref):
+    out_ref[0] = block_ref[...]
+
+
+def copies(block, count):
+    return pl.pallas_call(
+        copies_kernel,
+        grid=(count,),
+        out_shape=jax.ShapeDtypeStruct((count,) + block.shape, block.dtype),
+        in_specs=[pl.BlockSpec(block.shape, lambda i: (0, 0))],
+        out_specs=pl.BlockSpec((1,) + block.shape, lambda i: (i, 0, 0)),
+        compiler_params=pltpu.CompilerParams(vmem_limit_bytes=8 * 1024 * 1024),
+        cost_estimate=pl.CostEstimate(flops=0, bytes_accessed=2 * count * block.size, transcendentals=0),
+    )(block)
 
 
 def norm_kernel(lat_ref, pert_ref, gain_ref, normed_ref, latent_ref):
@@ -550,7 +566,7 @@
         row = lax.all_to_all(jnp.broadcast_to(mine[None], (4,) + mine.shape), ("xl", "xh"), 0, 0, tiled=True)
         row = row.reshape(128, PACKED)
     with jax.named_scope("weights_over_y"):
-        wa = lax.all_to_all(jnp.broadcast_to(row[None], (4,) + row.shape), "y", 0, 0, tiled=True)
+        wa = lax.all_to_all(copies(row, 4), "y", 0, 0, tiled=True)
         wa = wa.reshape(16, 32, PACKED)
     wa, normed_low, normed_high, decoder, truth, area, gain, reach_row, place = lax.optimization_barrier(
         (wa, normed_low, normed_high, decoder, truth, area, gain, reach_row, place)

time: 169 us -> 169 us (level)
  no operation moved by 1% of the time
where the time goes in v6:
time: 169 us; the launch traced here: 168 us
  blocking collectives  57 us (34%)
  starting transfers between devices  55.4 us (33%)
  Pallas kernels  24.3 us (14%)
  waiting for transfers between devices  21.6 us (13%)
  local copies, waits for them, and re-layouts  6.59 us (4%)
  other arithmetic  2.54 us (2%)
    all_to_all x1, blocking collectives, shards(): received = lax.all_to_all(send, MEMBER, 0, 0, tiled=True)  25.3 us
    pallas_call x9, Pallas kernels, call(): pl.pallas_call(body, out_shape=tuple((jax.ShapeDtypeStruct(shape, kind) f...  24.1 us
    ppermute x2, starting transfers between devices, both_ways(): low = lax.ppermute(block, NODE, [(i, i + 1) for i in range(count - 1)])  13 us
    ppermute x1, starting transfers between devices, shards(): mine = lax.ppermute(packed, EVERY, weight_route())  12.1 us
    all_to_all x1, blocking collectives, shards(): lax.all_to_all(jnp.broadcast_to(mine[None], (4,) + mine.shape), ('xl', 'x...  12 us
    all_to_all x1, blocking collectives, shards(): lax.all_to_all(forecast.reshape(MEMBERS, SLOT, LANES), MEMBER, 0, 0, tile...  10.9 us
    ppermute x2, waiting for transfers between devices, both_ways(): low = lax.ppermute(block, NODE, [(i, i + 1) for i in range(count - 1)])  10.7 us
    all_to_all x1, starting transfers between devices, shards(): lax.all_to_all(latent_copies, MEMBER, 0, 0, tiled=True).reshape(WIDTH, ROWS)  10.2 us
  transfers between devices with their start and end apart: 9, of which 4 were waited for; matrix products, arithmetic and copies ran while one was open for 3% of the time, Pallas kernels for 6%

profile of v6, /device:TPU:1, one launch (start us, length us, event | category | flops | bytes accessed | tf_op | source)
XLA Modules:
  0.0 168.2 jit_solution(457600783211465390)
XLA Ops:
  0.6 1.6 broadcast_in_dim.12
  2.2 10.2 %all-to-all-start = ((bf16[16,64,256]{2,1,0:T(8,128)(2,1)}), bf16[16,64,256]{2,1,0:T(8,128)(2,1)S(1)}, u32[]{:S(2)}, u32[]{:S(2)}) async-start(bf16[16,64,256]{2,1,0:T(8,128)(2,1)} %broadcast_in_dim.12), calls=%async_computation | async-start | bytes 1048576 | tf_op jit(solution)/shard_map/latent_over_member/all_to_all | solution.py:541
  12.5 0.7 fusion
  13.2 0.9 maximum_maximum_fusion
  14.1 12.1 %collective-permute-start = (bf16[32,2048]{1,0:T(8,128)(2,1)S(1)}, bf16[32,2048]{1,0:T(8,128)(2,1)S(1)}, u32[]{:S(2)}, u32[]{:S(2)}) collective-permute-start(bf16[32,2048]{1,0:T(8,128)(2,1)S(1)} %maximum_maximum_fusion), channel_id=1, source_target_pairs={{0,0},{1,1},{64,2},{65,3},{128,4},{129,5},{192,6},{193,7},{256,8},... | collective-permute-start | bytes 393224 | tf_op jit(solution)/shard_map/weights_over_node/ppermute | solution.py:538
  26.2 0.1 pad_add_fusion.place_ref
  26.3 0.7 broadcast_in_dim.13.gain_ref
  27.0 0.0 all-to-all-done
  27.0 0.0 copy-start.1
  27.0 1.0 copy-done.1
  28.0 0.5 layer_norm.1
  28.6 0.0 copy-start.3
  28.6 0.9 collective-permute-done
  29.5 12.0 %all_to_all.30 = bf16[4,32,2048]{2,1,0:T(8,128)(2,1)S(1)} all-to-all(bf16[4,32,2048]{2,1,0:T(8,128)(2,1)S(1)} %broadcast_in_dim.15), channel_id=1, replica_groups=mesh['y'=4,'xl'=2,'c'=2,'z'=16,'xh'=2] {'xl','xh'}, dimensions={0} | all-to-all | bytes 1048576 | tf_op jit(solution)/shard_map/weights_over_x/all_to_all | solution.py:566
  41.5 0.2 weights_over_y.1
  41.7 0.0 copy-done.3
  41.7 0.0 copy-start
  41.7 1.3 copy-done
  43.0 0.0 copy-start.5
  43.0 0.0 copy-start.6
  43.0 10.1 %all-to-all-start.2 = ((bf16[4,128,2048]{2,1,0:T(8,128)(2,1)}), bf16[4,128,2048]{2,1,0:T(8,128)(2,1)S(1)}, u32[]{:S(2)}, u32[]{:S(2)}) async-start(bf16[4,128,2048]{2,1,0:T(8,128)(2,1)} %copy-done), calls=%async_computation.2 | async-start | bytes 4194304 | tf_op jit(solution)/shard_map/weights_over_y/all_to_all | solution.py:569
  53.1 0.0 copy-start.2
  53.1 0.0 copy-start.4
  53.1 1.4 collective-permute-start.2
  54.5 6.3 %collective-permute-start.1 = (bf16[256,1024]{1,0:T(8,128)(2,1)}, bf16[256,1024]{1,0:T(8,128)(2,1)}, u32[]{:S(2)}, u32[]{:S(2)}) collective-permute-start(bf16[256,1024]{1,0:T(8,128)(2,1)} %copy-done.3), channel_id=1, source_target_pairs={{0,1},{1,2},{2,3},{3,4},{4,5},{5,6},{6,7},{7,8},{8,9},{9,10},{10,1... | collective-permute-start | bytes 1572872 | tf_op jit(solution)/shard_map/normed_halo/ppermute | solution.py:477
  60.8 0.0 copy-done.5
  60.8 0.1 copy.12
  61.0 1.0 pad.8.decoder_ref
  61.9 0.0 copy-done.6
  61.9 0.1 multiply_subtract_fusion
  62.0 7.7 %collective-permute-done.2 = bf16[256,1024]{1,0:T(8,128)(2,1)} collective-permute-done((bf16[256,1024]{1,0:T(8,128)(2,1)}, bf16[256,1024]{1,0:T(8,128)(2,1)}, u32[]{:S(2)}, u32[]{:S(2)}) %collective-permute-start.2) | collective-permute-done | bytes 524320 | tf_op jit(solution)/shard_map/normed_halo/ppermute | solution.py:478
  69.7 10.7 %collective-permute-done.1 = bf16[256,1024]{1,0:T(8,128)(2,1)} collective-permute-done((bf16[256,1024]{1,0:T(8,128)(2,1)}, bf16[256,1024]{1,0:T(8,128)(2,1)}, u32[]{:S(2)}, u32[]{:S(2)}) %collective-permute-start.1) | collective-permute-done | bytes 524320 | tf_op jit(solution)/shard_map/normed_halo/ppermute | solution.py:477
  80.4 0.0 all-to-all-done.2
  80.4 0.1 broadcast_in_dim.32.area_ref
  80.5 2.4 %collective-permute-start.3 = (bf16[16,32,2048]{2,1,0:T(8,128)(2,1)S(1)}, bf16[16,32,2048]{2,1,0:T(8,128)(2,1)S(1)}, u32[]{:S(2)}, u32[]{:S(2)}) collective-permute-start(bf16[16,32,2048]{2,1,0:T(8,128)(2,1)S(1)} %bitcast.16), channel_id=1, source_target_pairs={{0,32},{32,0},{1,33},{33,1},{2,34},{34,2},{3,35},{35,3},{4,36},{36... | collective-permute-start | bytes 6291464 | tf_op jit(solution)/shard_map/weights_over_core/ppermute | solution.py:577
  82.9 1.5 pad_maximum_fusion.normed_ref
  84.4 2.3 %collective-permute-done.3.wb_ref = bf16[16,32,2048]{2,1,0:T(8,128)(2,1)S(1)} collective-permute-done((bf16[16,32,2048]{2,1,0:T(8,128)(2,1)S(1)}, bf16[16,32,2048]{2,1,0:T(8,128)(2,1)S(1)}, u32[]{:S(2)}, u32[]{:S(2)}) %collective-permute-start.3) | collective-permute-done | bytes 2097184 | tf_op jit(solution)/shard_map/weights_over_core/ppermute | solution.py:577
  86.6 0.0 copy-done.2
  86.6 0.0 copy-done.4
  86.6 6.7 %forward.1 = (bf16[768,512]{1,0:T(8,128)(2,1)S(1)}, bf16[768,512]{1,0:T(8,128)(2,1)S(1)}, bf16[768,512]{1,0:T(8,128)(2,1)S(1)}, f32[256,1024]{1,0:T(8,128)S(1)},...) custom-call(s32[4]{0:T(128)S(1)} %pad_add_fusion.place_ref, ...), custom_call_target="tpu_custom_call" | custom-call | flops 4000000000 | bytes 4000000 | tf_op jit(solution)/shard_map/forward/pallas_call | solution.py:463
  93.4 10.9 %all_to_all.31.forecast_ref = f32[16,16,128]{2,1,0:T(8,128)S(1)} all-to-all(f32[16,16,128]{2,1,0:T(8,128)S(1)} %bitcast.27), channel_id=1, replica_groups=mesh['y'=4,'xl'=2,'c'=2,'z'=16,'xh'=2] {'y','xl','c'}, dimensions={0} | all-to-all | bytes 262144 | tf_op jit(solution)/shard_map/forecasts_over_member/all_to_all | solution.py:591
  104.2 0.7 score.1
  104.9 8.9 %all_to_all.32 = bf16[16,16,128]{2,1,0:T(8,128)(2,1)S(1)} all-to-all(bf16[16,16,128]{2,1,0:T(8,128)(2,1)S(1)} %score.1), channel_id=1, replica_groups=mesh['y'=4,'xl'=2,'c'=2,'z'=16,'xh'=2] {'y','xl','c'}, dimensions={0} | all-to-all | bytes 131072 | tf_op jit(solution)/shard_map/gradients_over_member/all_to_all | solution.py:599
  113.8 2.1 %upstream.1 = (f32[256,1024]{1,0:T(8,128)S(1)}, bf16[256,512]{1,0:T(8,128)(2,1)S(1)}, bf16[256,512]{1,0:T(8,128)(2,1)S(1)}, bf16[256,512]{1,0:T(8,128)(2,1)S(1)}...) custom-call(s32[4]{0:T(128)S(1)} %pad_add_fusion.place_ref, bf16[256,128]{1,0:T(8,128)(2,1)S(1)} %bitcast.26, ...), custom_call_target="tpu_custom_call" | custom-call | flops 500000000 | bytes 4000000 | tf_op jit(solution)/shard_map/upstream/pallas_call | solution.py:463
  115.9 1.3 collective-permute-start.5
  117.2 6.7 %collective-permute-start.4 = (bf16[256,128]{1,0:T(8,128)(2,1)S(1)}, bf16[256,128]{1,0:T(8,128)(2,1)S(1)}, u32[]{:S(2)}, u32[]{:S(2)}) collective-permute-start(bf16[256,128]{1,0:T(8,128)(2,1)S(1)} %get-tuple-element.61), channel_id=1, source_target_pairs={{0,1},{1,2},{2,3},{3,4},{4,5},{5,6},{6,7},{7,8},{8,9},{9,10},{10,1... | collective-permute-start | bytes 196616 | tf_op jit(solution)/shard_map/gradient_halo/ppermute | solution.py:477
  123.9 3.5 %query_gradients.1.qgrad_ref = f32[256,512]{1,0:T(8,128)S(1)} custom-call(s32[4]{0:T(128)S(1)} %pad_add_fusion.place_ref, bf16[768,512]{1,0:T(8,128)(2,1)S(1)} %get-tuple-element.62.q_ref, bf16[768,512]{1,0:T(8,128)(2,1)S(1)} %get-tuple-element.63.k_ref, bf16[768,512]{1,0:T(8,128)(2,1)S(1)} %get-tuple-element.64.v_ref, ...), custom_call_target="tpu_custom_call" | custom-call | flops 4000000000 | bytes 4000000 | tf_op jit(solution)/shard_map/query_gradients/pallas_call | solution.py:463
  127.5 0.0 collective-permute-done.5.high_ref
  127.5 0.0 collective-permute-done.4.low_ref
  127.5 0.6 loss_over_node.1
  128.1 4.8 %collective-permute-start.6 = (f32[8,128]{1,0:T(8,128)S(1)}, f32[8,128]{1,0:T(8,128)S(1)}, u32[]{:S(2)}, u32[]{:S(2)}) collective-permute-start(f32[8,128]{1,0:T(8,128)S(1)} %loss_over_node.1), channel_id=1, source_target_pairs={{0,0},{1,1},{2,2},{3,3},{4,4},{5,5},{6,6},{7,7},{8,8},{9,9},{10,10... | collective-permute-start | bytes 12296 | tf_op jit(solution)/shard_map/loss_over_node/ppermute | solution.py:624
  132.9 6.2 %backward.1.qkv_grad_ref = bf16[256,1536]{1,0:T(8,128)(2,1)S(1)} custom-call(s32[4]{0:T(128)S(1)} %pad_add_fusion.place_ref, bf16[256,128]{1,0:T(8,128)(2,1)S(1)} %collective-permute-done.4.low_ref, bf16[256,128]{1,0:T(8,128)(2,1)S(1)} %collective-permute-done.5.high_ref, bf16[128,1024]{1,0:T(8,128)(2,1)S(1)} %pad.8.decoder_ref, ...), custom_call_target="tpu_custom_call" | custom-call | flops 4000000000 | bytes 4000000 | tf_op jit(solution)/shard_map/backward/pallas_call | solution.py:463
  139.2 0.0 collective-permute-done.6.loss_ref
  139.2 3.1 %hidden_gradient.1 = (f32[256,1024]{1,0:T(8,128)}, bf16[16,80,256]{2,1,0:T(8,128)(2,1)S(1)}) custom-call(s32[4]{0:T(128)S(1)} %pad_add_fusion.place_ref, bf16[256,1536]{1,0:T(8,128)(2,1)S(1)} %backward.1.qkv_grad_ref, bf16[16,32,2048]{2,1,0:T(8,128)(2,1)S(1)} %bitcast.20, bf16[16,32,2048]{2,1,0:T(8,128)(2,1)S(1)} %collective-permute-done.3.wb_ref, ...), custom_call_target="tpu_custom_call" | custom-call | flops 1000000000 | bytes 4000000 | tf_op jit(solution)/shard_map/hidden_gradient/pallas_call | solution.py:463
  142.3 25.3 %all_to_all.33.received_ref = bf16[16,80,256]{2,1,0:T(8,128)(2,1)S(1)} all-to-all(bf16[16,80,256]{2,1,0:T(8,128)(2,1)S(1)} %get-tuple-element.73), channel_id=1, replica_groups=mesh['y'=4,'xl'=2,'c'=2,'z'=16,'xh'=2] {'y','xl','c'}, dimensions={0} | all-to-all | bytes 1310720 | tf_op jit(solution)/shard_map/latent_gradient_over_member/all_to_all | solution.py:647
  167.5 0.7 finish.1
  (3 shorter events, 0.1 us)
Async XLA Ops:
  2.2 24.8 %all-to-all-start = ((bf16[16,64,256]{2,1,0:T(8,128)(2,1)}), bf16[16,64,256]{2,1,0:T(8,128)(2,1)S(1)}, u32[]{:S(2)}, u32[]{:S(2)}) async-start(bf16[16,64,256]{2,1,0:T(8,128)(2,1)} %broadcast_in_dim.12), calls=%async_computation | async-start | bytes 1048576 | tf_op jit(solution)/shard_map/latent_over_member/all_to_all | solution.py:541
  14.1 15.3 %collective-permute-start = (bf16[32,2048]{1,0:T(8,128)(2,1)S(1)}, bf16[32,2048]{1,0:T(8,128)(2,1)S(1)}, u32[]{:S(2)}, u32[]{:S(2)}) collective-permute-start(bf16[32,2048]{1,0:T(8,128)(2,1)S(1)} %maximum_maximum_fusion), channel_id=1, source_target_pairs={{0,0},{1,1},{64,2},{65,3},{128,4},{129,5},{192,6},{193,7},{256,8},... | collective-permute-start | bytes 393224 | tf_op jit(solution)/shard_map/weights_over_node/ppermute | solution.py:538
  27.0 1.0 copy-start.1
  28.6 13.1 %copy-start.3 = (bf16[256,1024]{1,0:T(8,128)(2,1)}, bf16[256,1024]{1,0:T(8,128)(2,1)S(1)}, u32[]{:S(2)}) copy-start(bf16[256,1024]{1,0:T(8,128)(2,1)S(1)} %get-tuple-element.42) | copy-start | bytes 1572868
  41.7 1.3 copy-start
  43.0 17.8 %copy-start.5 = (f32[98,256]{1,0:T(8,128)S(1)}, f32[98,256]{1,0:T(8,128)}, u32[]{:S(2)}) copy-start(f32[98,256]{1,0:T(8,128)} %param.15) | copy-start | bytes 301060
  43.0 18.9 %copy-start.6 = (s32[256]{0:T(256)S(1)}, s32[256]{0:T(256)}, u32[]{:S(2)}) copy-start(s32[256]{0:T(256)} %param.16) | copy-start | bytes 3076
  43.0 37.4 %all-to-all-start.2 = ((bf16[4,128,2048]{2,1,0:T(8,128)(2,1)}), bf16[4,128,2048]{2,1,0:T(8,128)(2,1)S(1)}, u32[]{:S(2)}, u32[]{:S(2)}) async-start(bf16[4,128,2048]{2,1,0:T(8,128)(2,1)} %copy-done), calls=%async_computation.2 | async-start | bytes 4194304 | tf_op jit(solution)/shard_map/weights_over_y/all_to_all | solution.py:569
  53.1 33.5 %copy-start.2 = (bf16[1,256,1024]{2,1,0:T(8,128)(2,1)S(1)}, bf16[1,256,1024]{2,1,0:T(8,128)(2,1)}, u32[]{:S(2)}) copy-start(bf16[1,256,1024]{2,1,0:T(8,128)(2,1)} %param.10) | copy-start | bytes 1572868
  53.1 33.5 %copy-start.4 = (s32[256]{0:T(256)S(1)}, s32[256]{0:T(256)}, u32[]{:S(2)}) copy-start(s32[256]{0:T(256)} %param.17) | copy-start | bytes 3076
  53.1 16.6 %collective-permute-start.2 = (bf16[256,1024]{1,0:T(8,128)(2,1)}, bf16[256,1024]{1,0:T(8,128)(2,1)}, u32[]{:S(2)}, u32[]{:S(2)}) collective-permute-start(bf16[256,1024]{1,0:T(8,128)(2,1)} %copy-done.3), channel_id=1, source_target_pairs={{1,0},{2,1},{3,2},{4,3},{5,4},{6,5},{7,6},{8,7},{9,8},{10,9},{11,1... | collective-permute-start | bytes 1572872 | tf_op jit(solution)/shard_map/normed_halo/ppermute | solution.py:478
  54.5 25.9 %collective-permute-start.1 = (bf16[256,1024]{1,0:T(8,128)(2,1)}, bf16[256,1024]{1,0:T(8,128)(2,1)}, u32[]{:S(2)}, u32[]{:S(2)}) collective-permute-start(bf16[256,1024]{1,0:T(8,128)(2,1)} %copy-done.3), channel_id=1, source_target_pairs={{0,1},{1,2},{2,3},{3,4},{4,5},{5,6},{6,7},{7,8},{8,9},{9,10},{10,1... | collective-permute-start | bytes 1572872 | tf_op jit(solution)/shard_map/normed_halo/ppermute | solution.py:477
  80.5 6.2 %collective-permute-start.3 = (bf16[16,32,2048]{2,1,0:T(8,128)(2,1)S(1)}, bf16[16,32,2048]{2,1,0:T(8,128)(2,1)S(1)}, u32[]{:S(2)}, u32[]{:S(2)}) collective-permute-start(bf16[16,32,2048]{2,1,0:T(8,128)(2,1)S(1)} %bitcast.16), channel_id=1, source_target_pairs={{0,32},{32,0},{1,33},{33,1},{2,34},{34,2},{3,35},{35,3},{4,36},{36... | collective-permute-start | bytes 6291464 | tf_op jit(solution)/shard_map/weights_over_core/ppermute | solution.py:577
  115.9 11.6 %collective-permute-start.5 = (bf16[256,128]{1,0:T(8,128)(2,1)S(1)}, bf16[256,128]{1,0:T(8,128)(2,1)S(1)}, u32[]{:S(2)}, u32[]{:S(2)}) collective-permute-start(bf16[256,128]{1,0:T(8,128)(2,1)S(1)} %get-tuple-element.61), channel_id=1, source_target_pairs={{1,0},{2,1},{3,2},{4,3},{5,4},{6,5},{7,6},{8,7},{9,8},{10,9},{11,1... | collective-permute-start | bytes 196616 | tf_op jit(solution)/shard_map/gradient_halo/ppermute | solution.py:478
  117.2 10.3 %collective-permute-start.4 = (bf16[256,128]{1,0:T(8,128)(2,1)S(1)}, bf16[256,128]{1,0:T(8,128)(2,1)S(1)}, u32[]{:S(2)}, u32[]{:S(2)}) collective-permute-start(bf16[256,128]{1,0:T(8,128)(2,1)S(1)} %get-tuple-element.61), channel_id=1, source_target_pairs={{0,1},{1,2},{2,3},{3,4},{4,5},{5,6},{6,7},{7,8},{8,9},{9,10},{10,1... | collective-permute-start | bytes 196616 | tf_op jit(solution)/shard_map/gradient_halo/ppermute | solution.py:477
  128.1 11.0 %collective-permute-start.6 = (f32[8,128]{1,0:T(8,128)S(1)}, f32[8,128]{1,0:T(8,128)S(1)}, u32[]{:S(2)}, u32[]{:S(2)}) collective-permute-start(f32[8,128]{1,0:T(8,128)S(1)} %loss_over_node.1), channel_id=1, source_target_pairs={{0,0},{1,1},{2,2},{3,3},{4,4},{5,5},{6,6},{7,7},{8,8},{9,9},{10,10... | collective-permute-start | bytes 12296 | tf_op jit(solution)/shard_map/loss_over_node/ppermute | solution.py:624
